TPU v7x, 512 devices: a whole 4x8x8 slice. The times are simulated.
512 devices in a mesh: slide: 16 (over z, y_lo), strip: 32 (over y_hi, x, core).
Axes of the slice: x: 4, y: 8 (y_hi: 4, y_lo: 2; y = y_hi * 2 + y_lo), z: 8, core: 2. Of those that a mesh axis runs over, the one named last changes fastest.
Arguments:
- image: bfloat16 [16, 192, 64, 256], P('slide', 'strip'), may hold values from -6 to 6
- cotangent: bfloat16 [16, 192, 64, 256], P('slide', 'strip'), may hold values from -6 to 6
- kernel_tall: bfloat16 [51, 5, 256], replicated, may hold values from -0.375 to 0.375
- kernel_wide: bfloat16 [5, 51, 256], replicated, may hold values from -0.375 to 0.375
- layer_norm_gain: float32 [256], replicated, may hold values from 0.5 to 1.5
- layer_norm_bias: float32 [256], replicated, may hold values from -3 to 3
- w_in: bfloat16 [256, 1024], replicated, may hold values from -0.375 to 0.375
- b_in: float32 [1024], replicated, may hold values from -3 to 3
- w_out: bfloat16 [1024, 256], replicated, may hold values from -0.1875 to 0.1875
- b_out: float32 [256], replicated, may hold values from -3 to 3
Outputs:
- output: bfloat16 [16, 192, 64, 256], P('slide', 'strip')
- grad_image: bfloat16 [16, 192, 64, 256], P('slide', 'strip')
- grad_tall: float32 [51, 5, 256], replicated
- grad_wide: float32 [5, 51, 256], replicated
- grad_gain: float32 [256], replicated
- grad_shift: float32 [256], replicated
- grad_w_in: float32 [256, 1024], replicated
- grad_b_in: float32 [1024], replicated
- grad_w_out: float32 [1024, 256], replicated
- grad_b_out: float32 [256], replicated
All inputs are finite; a program needn't handle non-finite values.
Results may differ from a plain program's by a relative error of at most 0.0085.
Values may be sent and summed in bfloat16 or wider, within the bound.
No kernel may reach another device: no remote copies, remote signals or barrier semaphores. Data moves between devices by JAX's collectives and lax.ppermute only.
A program may use at most 64 MiB of HBM per device.

v0:
```python
import functools

import jax
import jax.numpy as jnp
from jax import lax
from jax.experimental import pallas as pl
from jax.experimental.pallas import tpu as pltpu
from jax.sharding import PartitionSpec as P

F32 = jnp.float32
BF16 = jnp.bfloat16
STRIPS = 32
ROWS = 6
COLS = 64
H = STRIPS * ROWS
C = 256
FF = 1024
LONG = 51
SHORT = 5
PAIRS = 4
BAND = 64
REACH = 32
MSG = ROWS * PAIRS
CELLS = ROWS * COLS
epsilon = 1e-06

PARAMS = pltpu.CompilerParams(vmem_limit_bytes=48 * 1024 * 1024)


def call(kernel, out_shape, scratch=()):
    return pl.pallas_call(
        kernel,
        out_shape=out_shape,
        scratch_shapes=list(scratch),
        compiler_params=PARAMS,
    )


def put_rows(block, k, scr):
    tall = jnp.concatenate([block[:, :128], block[:, 128:]], axis=0).T
    for cp in range(PAIRS):
        scr[pl.ds(k * PAIRS + cp, STRIPS, stride=MSG), :] = tall[cp * STRIPS : (cp + 1) * STRIPS]


def get_rows(scr, k):
    tall = jnp.concatenate(
        [scr[pl.ds(k * PAIRS + cp, STRIPS, stride=MSG), :] for cp in range(PAIRS)], axis=0
    ).T
    return jnp.concatenate([tall[:COLS], tall[COLS:]], axis=1)


def half_masks(shape):
    lane = lax.broadcasted_iota(jnp.int32, shape, len(shape) - 1)
    return lane, lane < COLS


def shifted(x, by):
    if by == 0:
        return x
    column = lax.broadcasted_iota(jnp.int32, x.shape, 1) % COLS + by
    return jnp.where((column >= 0) & (column < COLS), pltpu.roll(x, (-by) % 128, 1), 0.0)


def sloped(row, first_shift, count):
    eight = pltpu.roll(jnp.broadcast_to(row, (8, 128)), 0, 1, stride=1, stride_axis=0)
    return jnp.concatenate(
        [pltpu.roll(eight, (first_shift + i) % 128, 1) for i in range(0, count, 8)], axis=0
    )


def tall_matrix(taps_ref, q, c):
    return sloped(taps_ref[q * 8 + c : q * 8 + c + 1, :], REACH - (LONG - 1) // 2, BAND)


def wide_matrix(taps_ref, p, cp, in_block):
    first = -((LONG - 1) // 2)
    turned = jnp.concatenate(
        [
            sloped(taps_ref[n : n + 1, :], first + COLS * c2, COLS)
            for c2, n in enumerate((p * 8 + cp, p * 8 + 4 + cp))
        ],
        axis=0,
    )
    return jnp.where(in_block, turned, 0.0)


def block_mask():
    row = lax.broadcasted_iota(jnp.int32, (128, 128), 0)
    lane = lax.broadcasted_iota(jnp.int32, (128, 128), 1)
    return (row < COLS) == (lane < COLS)


def tall_conv(padded, taps_ref, cp, sign):
    matrix = jnp.concatenate(
        [
            jnp.concatenate([tall_matrix(taps_ref, q, c2 * 4 + cp) for c2 in range(2)], axis=1)
            for q in range(SHORT)
        ],
        axis=0,
    ).astype(BF16)
    _, first = half_masks((128, 128))
    zero = jnp.zeros((128, 128), BF16)
    sides = []
    for b in range(H // BAND):
        window = padded[b * BAND : b * BAND + 128]
        sides.append(
            jnp.concatenate([jnp.where(first, window, zero), jnp.where(first, zero, window)], axis=0)
        )
    product = jnp.dot(matrix, jnp.concatenate(sides, axis=1), preferred_element_type=F32)
    bands = []
    for b in range(H // BAND):
        total = None
        for q in range(SHORT):
            part = product[q * BAND : (q + 1) * BAND, b * 128 : (b + 1) * 128]
            part = shifted(part, sign * (q - 2))
            total = part if total is None else total + part
        bands.append(total)
    return jnp.concatenate(bands, axis=0)


def wide_conv(scr, taps_ref, cp, sign, in_block):
    source = jnp.concatenate(
        [scr[8 + sign * (p - 2) : 8 + sign * (p - 2) + H, :].astype(BF16) for p in range(SHORT)],
        axis=1,
    )
    matrix = jnp.concatenate(
        [wide_matrix(taps_ref, p, cp, in_block) for p in range(SHORT)], axis=0
    ).astype(BF16)
    return jnp.dot(source, matrix, preferred_element_type=F32)


def pad_rows(x):
    zero = jnp.zeros((REACH, 128), x.dtype)
    return jnp.concatenate([zero, x, zero], axis=0)


def pack_kernel(image_ref, out_ref, scr):
    for k in range(ROWS):
        put_rows(image_ref[k].astype(F32), k, scr)
    out_ref[...] = scr[...].astype(BF16)


def forward_kernel(image_ref, tall_ref, wide_ref, conv_ref, mixed_ref, scr, pad, out):
    scr[...] = image_ref[...].astype(F32)
    in_block = block_mask()
    pad[0:8, :] = jnp.zeros((8, 128), F32)
    pad[H + 8 : H + 16, :] = jnp.zeros((8, 128), F32)
    for cp in range(PAIRS):
        source = scr[pl.ds(cp, H, stride=PAIRS), :].astype(BF16)
        mixed = tall_conv(pad_rows(source), tall_ref, cp, 1).astype(BF16)
        mixed_ref[cp] = mixed
        pad[8 : H + 8, :] = mixed.astype(F32)
        out[pl.ds(cp, H, stride=PAIRS), :] = wide_conv(pad, wide_ref, cp, 1, in_block)
    conv_ref[...] = out[...].astype(BF16)


def diagonal(x, offset):
    total = None
    for i in range(0, x.shape[0], 8):
        part = pltpu.roll(x[i : i + 8], (offset - i) % 128, 1)
        total = part if total is None else total + part
    row = lax.broadcasted_iota(jnp.int32, (8, 128), 0)
    for bit in (1, 2, 4):
        total = jnp.where(row & bit != 0, pltpu.roll(total, 128 - bit, 1), total)
    return jnp.sum(total, axis=0, keepdims=True)


def backward_kernel(
    scale,
    d_conv_ref,
    image_ref,
    mixed_ref,
    tall_ref,
    wide_ref,
    small_ref,
    d_image_ref,
    grads_ref,
    d_scr,
    i_scr,
    d_pad,
    m_pad,
    out,
    g_scr,
):
    d_scr[...] = d_conv_ref[...].astype(F32)
    i_scr[...] = image_ref[...].astype(F32)
    in_block = block_mask()
    for ref in (d_pad, m_pad):
        ref[0:8, :] = jnp.zeros((8, 128), F32)
        ref[H + 8 : H + 16, :] = jnp.zeros((8, 128), F32)
    g_scr[40:48, :] = jnp.zeros((8, 128), F32)
    g_scr[48:64, :] = small_ref[...]
    lane, first = half_masks((1, 128))
    lane_b, first_b = half_masks((BAND, 128))
    for cp in range(PAIRS):
        d_conv = d_scr[pl.ds(cp, H, stride=PAIRS), :]
        d_pad[8 : H + 8, :] = d_conv
        m_pad[8 : H + 8, :] = mixed_ref[cp].astype(F32)
        source = pad_rows(i_scr[pl.ds(cp, H, stride=PAIRS), :].astype(BF16))
        d_mixed = wide_conv(d_pad, wide_ref, cp, -1, in_block).astype(BF16)
        moved = jnp.concatenate(
            [m_pad[6 + p : 6 + p + H, :].astype(BF16) for p in range(SHORT)], axis=1
        )
        corr = lax.dot_general(
            d_conv.astype(BF16), moved, (((0,), (0,)), ((), ())), preferred_element_type=F32
        )
        for p in range(SHORT):
            part = jnp.where(in_block, corr[:, p * 128 : (p + 1) * 128], 0.0)
            low = diagonal(part[:COLS], 32)
            high = diagonal(part[COLS:], 32)
            row = 20 + p * PAIRS + cp
            g_scr[row : row + 1, :] = jnp.where(first, low, high) * scale
        parts = []
        d_mixed_f = d_mixed.astype(F32)
        for q in range(SHORT):
            parts.append(shifted(d_mixed_f, 2 - q))
        left = []
        for c2 in range(2):
            for q in range(SHORT):
                bands = []
                for b in range(H // BAND):
                    band = parts[q][b * BAND : (b + 1) * BAND]
                    bands.append(jnp.where(first_b == (c2 == 0), band, 0.0))
                left.append(jnp.concatenate(bands, axis=1))
        left = jnp.concatenate(left, axis=0).astype(BF16)
        right = jnp.concatenate(
            [source[b * BAND : b * BAND + 128] for b in range(H // BAND)], axis=1
        )
        corr = lax.dot_general(
            left, right, (((1,), (1,)), ((), ())), preferred_element_type=F32
        )
        for q in range(SHORT):
            low = diagonal(corr[q * BAND : (q + 1) * BAND], 0)
            high = diagonal(corr[(SHORT + q) * BAND : (SHORT + q + 1) * BAND], COLS)
            row = q * PAIRS + cp
            g_scr[row : row + 1, :] = jnp.where(first, low, high) * scale
        out[pl.ds(cp, H, stride=PAIRS), :] = tall_conv(pad_rows(d_mixed), tall_ref, cp, -1)
    d_image_ref[...] = out[...].astype(BF16)
    grads_ref[...] = g_scr[...].astype(BF16)


def mlp_kernel(
    scale,
    conv_ref,
    image_ref,
    cot_ref,
    gain_ref,
    bias_ref,
    w_in_ref,
    b_in_ref,
    w_out_ref,
    b_out_ref,
    output_ref,
    d_conv_ref,
    grads_ref,
    small_ref,
    scr,
    xhat_scr,
    inv_scr,
    normed_scr,
    hidden_scr,
    d_pre_scr,
    out,
):
    scr[...] = conv_ref[...].astype(F32)
    gain, bias = gain_ref[...], bias_ref[...]
    sums = [jnp.zeros((1, C), F32), jnp.zeros((1, C), F32), jnp.zeros((1, C), F32)]
    g_b_in = jnp.zeros((1, FF), F32)
    step = 2
    for k in range(0, ROWS, step):
        rows = slice(k * COLS, (k + step) * COLS)
        conv = jnp.concatenate([get_rows(scr, k + i) for i in range(step)], axis=0)
        centred = conv - jnp.mean(conv, axis=1, keepdims=True)
        inverse = lax.rsqrt(jnp.mean(centred * centred, axis=1, keepdims=True) + epsilon)
        xhat = centred * inverse
        normed = (xhat * gain + bias).astype(BF16)
        normed_scr[rows, :] = normed
        pre_act = jnp.dot(normed, w_in_ref[...], preferred_element_type=F32) + b_in_ref[...]
        cdf = 0.5 * (1.0 + lax.erf(pre_act * 0.7071067811865476))
        hidden = (pre_act * cdf).astype(BF16)
        hidden_scr[rows, :] = hidden
        branch = jnp.dot(hidden, w_out_ref[...], preferred_element_type=F32) + b_out_ref[...]
        cot = cot_ref[rows, :]
        output_ref[rows, :] = (image_ref[rows, :].astype(F32) + branch).astype(BF16)
        d_hidden = lax.dot_general(
            cot, w_out_ref[...], (((1,), (1,)), ((), ())), preferred_element_type=F32
        )
        slope = cdf + pre_act * jnp.exp(-0.5 * pre_act * pre_act) * 0.3989422804014327
        d_pre = (d_hidden * slope).astype(BF16)
        d_pre_scr[rows, :] = d_pre
        g_b_in = g_b_in + jnp.sum(d_pre.astype(F32), axis=0, keepdims=True)
        d_norm = lax.dot_general(
            d_pre, w_in_ref[...], (((1,), (1,)), ((), ())), preferred_element_type=F32
        )
        sums[0] = sums[0] + jnp.sum(d_norm * xhat, axis=0, keepdims=True)
        sums[1] = sums[1] + jnp.sum(d_norm, axis=0, keepdims=True)
        sums[2] = sums[2] + jnp.sum(cot.astype(F32), axis=0, keepdims=True)
        g = d_norm * gain
        d_conv = inverse * (
            g
            - jnp.mean(g, axis=1, keepdims=True)
            - xhat * jnp.mean(g * xhat, axis=1, keepdims=True)
        )
        for i in range(step):
            put_rows(d_conv[i * COLS : (i + 1) * COLS], k + i, out)
    d_conv_ref[...] = out[...].astype(BF16)
    contract = (((0,), (0,)), ((), ()))
    grads_ref[0:C, :] = (
        lax.dot_general(normed_scr[...], d_pre_scr[...], contract, preferred_element_type=F32)
        * scale
    ).astype(BF16)
    grads_ref[C : 2 * C, :] = (
        lax.dot_general(cot_ref[...], hidden_scr[...], contract, preferred_element_type=F32)
        * scale
    ).astype(BF16)
    small_ref[...] = jnp.zeros((16, 128), F32)
    for i in range(FF // 128):
        small_ref[i : i + 1, :] = g_b_in[:, i * 128 : (i + 1) * 128] * scale
    for n in range(3):
        for i in range(2):
            row = 8 + 2 * n + i
            small_ref[row : row + 1, :] = sums[n][:, i * 128 : (i + 1) * 128] * scale


def strip_sum_kernel(parts_ref, grads_ref, out_ref):
    total = parts_ref[0].astype(F32)
    for i in range(1, STRIPS):
        total = total + parts_ref[i].astype(F32)
    for i in range(FF // 128):
        out_ref[i * 16 : (i + 1) * 16, :] = total[:, i * 128 : (i + 1) * 128].astype(BF16)
    out_ref[128:192, :] = grads_ref[...]


def slide_sum_kernel(parts_ref, out_ref):
    total = parts_ref[0].astype(F32)
    for i in range(1, parts_ref.shape[0]):
        total = total + parts_ref[i].astype(F32)
    out_ref[...] = total.astype(BF16)


SHARE = 192


def finish_kernel(
    parts_ref, tall_ref, wide_ref, small_ref, w_in_ref, w_out_ref, scr, turn
):
    for d in range(STRIPS):
        part = parts_ref[d].astype(F32)
        scr[d * SHARE : (d + 1) * SHARE, :] = part
        for i in range(FF // 128):
            piece = part[i * 16 : (i + 1) * 16]
            if d < 16:
                w_in_ref[d * 16 : (d + 1) * 16, i * 128 : (i + 1) * 128] = piece
            else:
                turn[(d - 16) * 16 : (d - 15) * 16, i * 128 : (i + 1) * 128] = piece
    for half in range(2):
        for i in range(FF // 128):
            w_out_ref[i * 128 : (i + 1) * 128, half * 128 : (half + 1) * 128] = turn[
                half * 128 : (half + 1) * 128, i * 128 : (i + 1) * 128
            ].T
    for q in range(SHORT):
        for start, ref in ((0, tall_ref), (20, wide_ref)):
            rows = jnp.concatenate(
                [
                    scr[pl.ds(128 + start + q * PAIRS + cp, STRIPS, stride=SHARE), :]
                    for cp in range(PAIRS)
                ],
                axis=0,
            ).T
            ref[q] = jnp.concatenate([rows[:COLS], rows[COLS:]], axis=1)
    total = scr[176:192, :]
    for d in range(1, STRIPS):
        total = total + scr[d * SHARE + 176 : d * SHARE + 192, :]
    small_ref[...] = total


def residual_kernel(d_image_ref, cot_ref, out_ref, scr):
    scr[...] = d_image_ref[...].astype(F32)
    for k in range(ROWS):
        out_ref[k] = (cot_ref[k].astype(F32) + get_rows(scr, k)).astype(BF16)


def exchange(x, axis):
    return lax.all_to_all(x, axis, 0, 0, tiled=True)


def messages(x):
    return exchange(x.reshape(STRIPS, MSG, 128), "strip").reshape(STRIPS * MSG, 128)


def shape(dims, dtype):
    return jax.ShapeDtypeStruct(dims, dtype)


def local(
    image,
    cotangent,
    kernel_tall,
    kernel_wide,
    layer_norm_gain,
    layer_norm_bias,
    w_in,
    b_in,
    w_out,
    b_out,
):
    source = image[0]
    upstream = cotangent[0]
    slides = lax.axis_size("slide")
    scale = float(CELLS * slides * STRIPS) ** (-0.5)
    packed_f = pltpu.VMEM((STRIPS * MSG, 128), F32)
    packed_b = shape((STRIPS * MSG, 128), BF16)
    edge = pltpu.VMEM((H + 16, 128), F32)

    image_msg = call(pack_kernel, packed_b, [packed_f])(source)
    me = lax.axis_index("strip")
    own = jnp.arange(8)[:, None] * STRIPS + me == jnp.arange(C)[None, :]
    own = own.astype(BF16)

    def taps(kernel, spec):
        picked = jnp.einsum(spec, kernel, own, preferred_element_type=F32)
        picked = picked.reshape(SHORT * 8, LONG)
        pad = ((0, 0), (0, 128 - LONG))
        return jnp.pad(picked, pad), jnp.pad(picked[:, ::-1], pad)

    tall, tall_flipped = taps(kernel_tall, "pqc,kc->qkp")
    wide, wide_flipped = taps(kernel_wide, "pqc,kc->pkq")

    image_ch = messages(image_msg)
    conv_ch, mixed = call(
        forward_kernel,
        (packed_b, shape((PAIRS, H, 128), BF16)),
        [packed_f, edge, packed_f],
    )(image_ch, tall, wide_flipped)
    conv = messages(conv_ch)
    output, d_conv_msg, grads, small = call(
        functools.partial(mlp_kernel, scale),
        (
            shape((CELLS, C), BF16),
            packed_b,
            shape((2 * C, FF), BF16),
            shape((16, 128), F32),
        ),
        [
            packed_f,
            pltpu.VMEM((8, 128), F32),
            pltpu.VMEM((8, 128), F32),
            pltpu.VMEM((CELLS, C), BF16),
            pltpu.VMEM((CELLS, FF), BF16),
            pltpu.VMEM((CELLS, FF), BF16),
            packed_f,
        ],
    )(
        conv,
        source.reshape(CELLS, C),
        upstream.reshape(CELLS, C),
        layer_norm_gain[None],
        layer_norm_bias[None],
        w_in,
        b_in[None],
        w_out,
        b_out[None],
    )
    d_conv = messages(d_conv_msg)
    grad_parts = exchange(grads.reshape(STRIPS, 16, FF), "strip")
    d_image_msg, own_grads = call(
        functools.partial(backward_kernel, scale),
        (packed_b, shape((64, 128), BF16)),
        [packed_f, packed_f, edge, edge, packed_f, pltpu.VMEM((64, 128), F32)],
    )(d_conv, image_ch, mixed, tall_flipped, wide, small)
    d_image = messages(d_image_msg)
    share = call(strip_sum_kernel, shape((SHARE, 128), BF16))(grad_parts, own_grads)
    shares = exchange(jnp.broadcast_to(share[None], (slides, SHARE, 128)), "slide")
    total = call(slide_sum_kernel, shape((SHARE, 128), BF16))(shares)
    totals = exchange(jnp.broadcast_to(total[None], (STRIPS, SHARE, 128)), "strip")
    long_tall, long_wide, small_sum, g_w_in, g_w_out = call(
        finish_kernel,
        (
            shape((SHORT, COLS, C), F32),
            shape((SHORT, COLS, C), F32),
            shape((16, 128), F32),
            shape((C, FF), F32),
            shape((FF, C), F32),
        ),
        [pltpu.VMEM((STRIPS * SHARE, 128), F32), pltpu.VMEM((C, FF), F32)],
    )(totals)
    grad_image = call(residual_kernel, shape((ROWS, COLS, C), BF16), [packed_f])(d_image, upstream)
    g_tall = jnp.transpose(long_tall[:, 7 : 7 + LONG], (1, 0, 2))
    g_wide = long_wide[:, 7 : 7 + LONG]
    g_b_in = small_sum[:8].reshape(FF)
    g_gain, g_shift, g_b_out = (small_sum[8 + 2 * i : 10 + 2 * i].reshape(C) for i in range(3))
    return (
        output.reshape(image.shape),
        grad_image[None],
        g_tall,
        g_wide,
        g_gain,
        g_shift,
        g_w_in,
        g_b_in,
        g_w_out,
        g_b_out,
    )


def solution(mesh):
    cells = P("slide", "strip", None, None)
    return jax.shard_map(
        local,
        mesh=mesh,
        in_specs=(cells, cells) + (P(),) * 8,
        out_specs=(cells, cells) + (P(),) * 8,
        check_vma=False,
    )
```

profile of v0, /device:TPU:1, one launch (start us, length us, event | category | flops | bytes accessed | tf_op | source)
XLA Modules:
  0.0 194.2 jit_solution(16710047541893876730)
XLA Ops:
  0.6 0.0 copy-start
  0.7 0.0 copy-start.7
  0.7 1.0 copy-done.1
  1.7 0.8 shard_map.177
  2.5 11.2 %all-to-all-start = ((bf16[32,24,128]{2,1,0:T(8,128)(2,1)}), bf16[32,24,128]{2,1,0:T(8,128)(2,1)S(1)}, u32[]{:S(2)}, u32[]{:S(2)}) async-start(bf16[32,24,128]{2,1,0:T(8,128)(2,1)} %bitcast.1), calls=%async_computation | async-start | bytes 393216 | tf_op jit(solution)/shard_map/all_to_all | solution.py:384
  13.8 0.2 convolution_bitcast_fusion
  13.9 0.1 rev.6
  14.0 1.1 convolution_bitcast_fusion.1
  15.1 10.4 %all-to-all-done = bf16[32,24,128]{2,1,0:T(8,128)(2,1)S(1)} async-done(((bf16[32,24,128]{2,1,0:T(8,128)(2,1)}), bf16[32,24,128]{2,1,0:T(8,128)(2,1)S(1)}, u32[]{:S(2)}, u32[]{:S(2)}) %all-to-all-start) | async-done | bytes 196640 | tf_op jit(solution)/shard_map/all_to_all | solution.py:384
  25.5 2.0 %shard_map.178 = (bf16[768,128]{1,0:T(8,128)(2,1)S(1)}, bf16[4,192,128]{2,1,0:T(8,128)(2,1)S(1)}) custom-call(bf16[768,128]{1,0:T(8,128)(2,1)S(1)} %bitcast.43, f32[40,128]{1,0:T(8,128)S(1)} %pad.13.tall_ref, f32[40,128]{1,0:T(8,128)S(1)} %pad.14.wide_ref), custom_call_target="tpu_custom_call" | custom-call | tf_op jit(solution)/shard_map/pallas_call | solution.py:430
  27.6 16.0 %all_to_all.35 = bf16[32,24,128]{2,1,0:T(8,128)(2,1)S(1)} all-to-all(bf16[32,24,128]{2,1,0:T(8,128)(2,1)S(1)} %bitcast.53), channel_id=1, replica_groups=mesh['slide'=16,'strip'=32] {'strip'}, dimensions={0} | all-to-all | bytes 393216 | tf_op jit(solution)/shard_map/all_to_all | solution.py:384
  43.6 3.6 %shard_map.179 = (bf16[384,256]{1,0:T(8,128)(2,1)}, bf16[768,128]{1,0:T(8,128)(2,1)S(1)}, bf16[512,1024]{1,0:T(8,128)(2,1)}, f32[16,128]{1,0:T(8,128)S(1)}) custom-call(bf16[768,128]{1,0:T(8,128)(2,1)S(1)} %bitcast.49, bf16[384,256]{1,0:T(8,128)(2,1)S(1)} %bitcast.48, bf16[384,256]{1,0:T(8,128)(2,1)S(1)} %bitcast.50, f32[1,256]{1,0:T(1,128)S(1)} %bitcast.55, ...), custom_call_target="tpu_custom_call" | custom-call | tf_op jit(solution)/shard_map/pallas_call | solution.py:436
  47.2 15.5 %all_to_all.36 = bf16[32,24,128]{2,1,0:T(8,128)(2,1)S(1)} all-to-all(bf16[32,24,128]{2,1,0:T(8,128)(2,1)S(1)} %bitcast.52), channel_id=1, replica_groups=mesh['slide'=16,'strip'=32] {'strip'}, dimensions={0} | all-to-all | bytes 393216 | tf_op jit(solution)/shard_map/all_to_all | solution.py:384
  62.7 3.9 %all-to-all-start.4 = ((bf16[32,16,1024]{2,1,0:T(8,128)(2,1)}), bf16[32,16,1024]{2,1,0:T(8,128)(2,1)S(1)}, u32[]{:S(2)}, u32[]{:S(2)}) async-start(bf16[32,16,1024]{2,1,0:T(8,128)(2,1)} %bitcast.25), calls=%async_computation.4 | async-start | bytes 2097152 | tf_op jit(solution)/shard_map/all_to_all | solution.py:384
  66.6 0.1 rev.7
  66.7 5.9 %shard_map.180 = (bf16[768,128]{1,0:T(8,128)(2,1)}, bf16[64,128]{1,0:T(8,128)(2,1)S(1)}) custom-call(bf16[768,128]{1,0:T(8,128)(2,1)S(1)} %bitcast.45, bf16[768,128]{1,0:T(8,128)(2,1)S(1)} %bitcast.44, bf16[4,192,128]{2,1,0:T(8,128)(2,1)S(1)} %get-tuple-element.26.mixed_ref, f32[40,128]{1,0:T(8,128)S(1)} %pad.15.tall_ref, f32[40,128]{1,0:T(8,128)S(1)} %pad.16.wide_ref, ...), custom_call_target="tpu_custom_call" | custom-call | tf_op jit(solution)/shard_map/pallas_call | solution.py:466
  72.5 22.7 %all-to-all-done.4.parts_ref = bf16[32,16,1024]{2,1,0:T(8,128)(2,1)S(1)} async-done(((bf16[32,16,1024]{2,1,0:T(8,128)(2,1)}), bf16[32,16,1024]{2,1,0:T(8,128)(2,1)S(1)}, u32[]{:S(2)}, u32[]{:S(2)}) %all-to-all-start.4) | async-done | bytes 1048608 | tf_op jit(solution)/shard_map/all_to_all | solution.py:384
  95.2 0.2 shard_map.182
  95.4 0.1 broadcast_in_dim.34
  95.5 31.6 %all_to_all.37.parts_ref = bf16[16,192,128]{2,1,0:T(8,128)(2,1)S(1)} all-to-all(bf16[16,192,128]{2,1,0:T(8,128)(2,1)S(1)} %broadcast_in_dim.34), channel_id=1, replica_groups=mesh['slide'=16,'strip'=32] {'slide'}, dimensions={0} | all-to-all | bytes 1572864 | tf_op jit(solution)/shard_map/all_to_all | solution.py:384
  127.1 5.9 %all-to-all-start.3 = ((bf16[32,24,128]{2,1,0:T(8,128)(2,1)}), bf16[32,24,128]{2,1,0:T(8,128)(2,1)S(1)}, u32[]{:S(2)}, u32[]{:S(2)}) async-start(bf16[32,24,128]{2,1,0:T(8,128)(2,1)} %bitcast.21), calls=%async_computation.3 | async-start | bytes 393216 | tf_op jit(solution)/shard_map/all_to_all | solution.py:384
  133.0 0.1 shard_map.183
  133.2 12.5 %all-to-all-done.3 = bf16[32,24,128]{2,1,0:T(8,128)(2,1)S(1)} async-done(((bf16[32,24,128]{2,1,0:T(8,128)(2,1)}), bf16[32,24,128]{2,1,0:T(8,128)(2,1)S(1)}, u32[]{:S(2)}, u32[]{:S(2)}) %all-to-all-start.3) | async-done | bytes 196640 | tf_op jit(solution)/shard_map/all_to_all | solution.py:384
  145.6 1.5 broadcast_in_dim.35
  147.2 3.8 %all-to-all-start.6 = ((bf16[32,192,128]{2,1,0:T(8,128)(2,1)}), bf16[32,192,128]{2,1,0:T(8,128)(2,1)S(1)}, u32[]{:S(2)}, u32[]{:S(2)}) async-start(bf16[32,192,128]{2,1,0:T(8,128)(2,1)} %broadcast_in_dim.35), calls=%async_computation.6 | async-start | bytes 3145728 | tf_op jit(solution)/shard_map/all_to_all | solution.py:384
  150.9 0.9 shard_map.181
  151.8 38.1 %all-to-all-done.6.parts_ref = bf16[32,192,128]{2,1,0:T(8,128)(2,1)S(1)} async-done(((bf16[32,192,128]{2,1,0:T(8,128)(2,1)}), bf16[32,192,128]{2,1,0:T(8,128)(2,1)S(1)}, u32[]{:S(2)}, u32[]{:S(2)}) %all-to-all-start.6) | async-done | bytes 1572896 | tf_op jit(solution)/shard_map/all_to_all | solution.py:384
  189.8 1.7 shard_map.184
  191.5 0.6 slice_bitcast_fusion.2
  192.1 0.6 slice_bitcast_fusion.1
  192.7 0.7 slice_bitcast_fusion
  193.4 0.7 slice.19
  (22 shorter events, 0.1 us)
Async XLA Ops:
  0.6 13.1 %copy-start = (bf16[5,51,256]{2,1,0:T(8,128)(2,1)S(1)}, bf16[5,51,256]{2,1,0:T(8,128)(2,1)}, u32[]{:S(2)}) copy-start(bf16[5,51,256]{2,1,0:T(8,128)(2,1)} %param.13) | copy-start | bytes 391684
  0.7 42.9 %copy-start.7 = (f32[256]{0:T(256)S(1)}, f32[256]{0:T(256)}, u32[]{:S(2)}) copy-start(f32[256]{0:T(256)} %param.14) | copy-start | bytes 3076
  0.7 1.0 copy-start.1
  1.6 41.9 %copy-start.2 = (bf16[1,6,64,256]{3,2,1,0:T(8,128)(2,1)S(1)}, bf16[1,6,64,256]{3,2,1,0:T(8,128)(2,1)}, u32[]{:S(2)}) copy-start(bf16[1,6,64,256]{3,2,1,0:T(8,128)(2,1)} %param.10) | copy-start | bytes 589828
  1.6 41.9 %copy-start.3 = (bf16[1,6,64,256]{3,2,1,0:T(8,128)(2,1)S(1)}, bf16[1,6,64,256]{3,2,1,0:T(8,128)(2,1)}, u32[]{:S(2)}) copy-start(bf16[1,6,64,256]{3,2,1,0:T(8,128)(2,1)} %param.11) | copy-start | bytes 589828
  1.6 41.9 %copy-start.4 = (bf16[256,1024]{1,0:T(8,128)(2,1)S(1)}, bf16[256,1024]{1,0:T(8,128)(2,1)}, u32[]{:S(2)}) copy-start(bf16[256,1024]{1,0:T(8,128)(2,1)} %w_in_ref.1) | copy-start | bytes 1572868
  1.6 41.9 %copy-start.5 = (bf16[1024,256]{1,0:T(8,128)(2,1)S(1)}, bf16[1024,256]{1,0:T(8,128)(2,1)}, u32[]{:S(2)}) copy-start(bf16[1024,256]{1,0:T(8,128)(2,1)} %w_out_ref.1) | copy-start | bytes 1572868
  1.6 41.9 %copy-start.6 = (f32[1024]{0:T(1024)S(1)}, f32[1024]{0:T(1024)}, u32[]{:S(2)}) copy-start(f32[1024]{0:T(1024)} %param.17) | copy-start | bytes 12292
  1.7 41.9 %copy-start.8 = (f32[256]{0:T(256)S(1)}, f32[256]{0:T(256)}, u32[]{:S(2)}) copy-start(f32[256]{0:T(256)} %param.15) | copy-start | bytes 3076
  1.7 41.9 %copy-start.9 = (f32[256]{0:T(256)S(1)}, f32[256]{0:T(256)}, u32[]{:S(2)}) copy-start(f32[256]{0:T(256)} %param.19) | copy-start | bytes 3076
  2.5 23.0 %all-to-all-start = ((bf16[32,24,128]{2,1,0:T(8,128)(2,1)}), bf16[32,24,128]{2,1,0:T(8,128)(2,1)S(1)}, u32[]{:S(2)}, u32[]{:S(2)}) async-start(bf16[32,24,128]{2,1,0:T(8,128)(2,1)} %bitcast.1), calls=%async_computation | async-start | bytes 393216 | tf_op jit(solution)/shard_map/all_to_all | solution.py:384
  62.7 32.5 %all-to-all-start.4 = ((bf16[32,16,1024]{2,1,0:T(8,128)(2,1)}), bf16[32,16,1024]{2,1,0:T(8,128)(2,1)S(1)}, u32[]{:S(2)}, u32[]{:S(2)}) async-start(bf16[32,16,1024]{2,1,0:T(8,128)(2,1)} %bitcast.25), calls=%async_computation.4 | async-start | bytes 2097152 | tf_op jit(solution)/shard_map/all_to_all | solution.py:384
  127.1 18.5 %all-to-all-start.3 = ((bf16[32,24,128]{2,1,0:T(8,128)(2,1)}), bf16[32,24,128]{2,1,0:T(8,128)(2,1)S(1)}, u32[]{:S(2)}, u32[]{:S(2)}) async-start(bf16[32,24,128]{2,1,0:T(8,128)(2,1)} %bitcast.21), calls=%async_computation.3 | async-start | bytes 393216 | tf_op jit(solution)/shard_map/all_to_all | solution.py:384
  147.2 42.7 %all-to-all-start.6 = ((bf16[32,192,128]{2,1,0:T(8,128)(2,1)}), bf16[32,192,128]{2,1,0:T(8,128)(2,1)S(1)}, u32[]{:S(2)}, u32[]{:S(2)}) async-start(bf16[32,192,128]{2,1,0:T(8,128)(2,1)} %broadcast_in_dim.35), calls=%async_computation.6 | async-start | bytes 3145728 | tf_op jit(solution)/shard_map/all_to_all | solution.py:384
where the time goes:
time: 195 us; the launch traced here: 194 us
  waiting for transfers between devices  83.6 us (43%)
  blocking collectives  63.1 us (32%)
  starting transfers between devices  24.7 us (13%)
  Pallas kernels  15.1 us (8%)
  local copies, waits for them, and re-layouts  5.47 us (3%)
    all_to_all x4, waiting for transfers between devices, exchange(): return lax.all_to_all(x, axis, 0, 0, tiled=True)  83.6 us
    all_to_all x3, blocking collectives, exchange(): return lax.all_to_all(x, axis, 0, 0, tiled=True)  63.1 us
    all_to_all x4, starting transfers between devices, exchange(): return lax.all_to_all(x, axis, 0, 0, tiled=True)  24.7 us
    pallas_call x1, Pallas kernels, local(): call(functools.partial(backward_kernel, scale), (packed_b, shape((64, 128...  5.86 us
  transfers between devices with their start and end apart: 4, of which 4 were waited for; matrix products, arithmetic and copies ran while one was open for 1% of the time, Pallas kernels for 4%

commit v1 on v0

--- a/solution.py
+++ b/solution.py
@@ -9,7 +9,9 @@
 
 F32 = jnp.float32
 BF16 = jnp.bfloat16
-STRIPS = 32
+CORES = 2
+CHIPS = 16
+STRIPS = CORES * CHIPS
 ROWS = 6
 COLS = 64
 H = STRIPS * ROWS
@@ -22,31 +24,53 @@
 REACH = 32
 MSG = ROWS * PAIRS
 CELLS = ROWS * COLS
+DATA = CORES * MSG
+GRADS = C * FF // 128
+OWN = GRADS // CHIPS
+SHARE = OWN + 64
+LAST = DATA + SHARE
 epsilon = 1e-06
 
 PARAMS = pltpu.CompilerParams(vmem_limit_bytes=48 * 1024 * 1024)
 
 
-def call(kernel, out_shape, scratch=()):
+def call(kernel, out_shape, scratch=(), scalars=0):
+    extra = {}
+    if scalars:
+        vmem = pl.BlockSpec(memory_space=pltpu.VMEM)
+        smem = pl.BlockSpec(memory_space=pltpu.SMEM)
+        extra["in_specs"] = [smem] + [vmem] * scalars
     return pl.pallas_call(
         kernel,
         out_shape=out_shape,
+        **extra,
         scratch_shapes=list(scratch),
         compiler_params=PARAMS,
     )
 
 
-def put_rows(block, k, scr):
-    tall = jnp.concatenate([block[:, :128], block[:, 128:]], axis=0).T
+def turned_rows(block):
+    return jnp.concatenate([block[:, :128], block[:, 128:]], axis=0).T
+
+
+def put_by_strip(block, k, scr):
+    rows = turned_rows(block)
     for cp in range(PAIRS):
-        scr[pl.ds(k * PAIRS + cp, STRIPS, stride=MSG), :] = tall[cp * STRIPS : (cp + 1) * STRIPS]
-
-
-def get_rows(scr, k):
-    tall = jnp.concatenate(
-        [scr[pl.ds(k * PAIRS + cp, STRIPS, stride=MSG), :] for cp in range(PAIRS)], axis=0
-    ).T
-    return jnp.concatenate([tall[:COLS], tall[COLS:]], axis=1)
+        for core in range(CORES):
+            first = cp * STRIPS + core * CHIPS
+            at = pl.ds(core * MSG + k * PAIRS + cp, CHIPS, stride=CORES * MSG)
+            scr[at, :] = rows[first : first + CHIPS]
+
+
+def put_by_core(block, k, scr):
+    rows = turned_rows(block)
+    for cp in range(PAIRS):
+        scr[pl.ds(k * PAIRS + cp, STRIPS, stride=MSG), :] = rows[cp * STRIPS : (cp + 1) * STRIPS]
+
+
+def untwisted(parts):
+    rows = jnp.concatenate(parts, axis=0).T
+    return jnp.concatenate([rows[:COLS], rows[COLS:]], axis=1)
 
 
 def half_masks(shape):
@@ -136,7 +160,7 @@
 
 def pack_kernel(image_ref, out_ref, scr):
     for k in range(ROWS):
-        put_rows(image_ref[k].astype(F32), k, scr)
+        put_by_strip(image_ref[k].astype(F32), k, scr)
     out_ref[...] = scr[...].astype(BF16)
 
 
@@ -167,14 +191,14 @@
 
 def backward_kernel(
     scale,
-    d_conv_ref,
+    parts_ref,
     image_ref,
     mixed_ref,
     tall_ref,
     wide_ref,
     small_ref,
     d_image_ref,
-    grads_ref,
+    share_ref,
     d_scr,
     i_scr,
     d_pad,
@@ -182,7 +206,12 @@
     out,
     g_scr,
 ):
-    d_scr[...] = d_conv_ref[...].astype(F32)
+    total = None
+    for i in range(CHIPS):
+        part = parts_ref[i].astype(F32)
+        d_scr[i * DATA : (i + 1) * DATA, :] = part[:DATA]
+        total = part[DATA:] if total is None else total + part[DATA:]
+    share_ref[0:OWN, :] = total.astype(BF16)
     i_scr[...] = image_ref[...].astype(F32)
     in_block = block_mask()
     for ref in (d_pad, m_pad):
@@ -236,11 +265,12 @@
             g_scr[row : row + 1, :] = jnp.where(first, low, high) * scale
         out[pl.ds(cp, H, stride=PAIRS), :] = tall_conv(pad_rows(d_mixed), tall_ref, cp, -1)
     d_image_ref[...] = out[...].astype(BF16)
-    grads_ref[...] = g_scr[...].astype(BF16)
+    share_ref[OWN:SHARE, :] = g_scr[...].astype(BF16)
 
 
 def mlp_kernel(
     scale,
+    core_ref,
     conv_ref,
     image_ref,
     cot_ref,
@@ -251,17 +281,15 @@
     w_out_ref,
     b_out_ref,
     output_ref,
-    d_conv_ref,
-    grads_ref,
+    theirs_ref,
+    mine_ref,
+    left_ref,
+    right_ref,
     small_ref,
     scr,
-    xhat_scr,
-    inv_scr,
-    normed_scr,
-    hidden_scr,
-    d_pre_scr,
     out,
 ):
+    core = core_ref[0]
     scr[...] = conv_ref[...].astype(F32)
     gain, bias = gain_ref[...], bias_ref[...]
     sums = [jnp.zeros((1, C), F32), jnp.zeros((1, C), F32), jnp.zeros((1, C), F32)]
@@ -269,25 +297,38 @@
     step = 2
     for k in range(0, ROWS, step):
         rows = slice(k * COLS, (k + step) * COLS)
-        conv = jnp.concatenate([get_rows(scr, k + i) for i in range(step)], axis=0)
+        conv = jnp.concatenate(
+            [
+                untwisted(
+                    [
+                        scr[pl.ds(c * MSG + i * PAIRS + cp, CHIPS, stride=CORES * MSG), :]
+                        for cp in range(PAIRS)
+                        for c in range(CORES)
+                    ]
+                )
+                for i in range(k, k + step)
+            ],
+            axis=0,
+        )
         centred = conv - jnp.mean(conv, axis=1, keepdims=True)
         inverse = lax.rsqrt(jnp.mean(centred * centred, axis=1, keepdims=True) + epsilon)
         xhat = centred * inverse
         normed = (xhat * gain + bias).astype(BF16)
-        normed_scr[rows, :] = normed
+        left_ref[0, rows, :] = normed
         pre_act = jnp.dot(normed, w_in_ref[...], preferred_element_type=F32) + b_in_ref[...]
         cdf = 0.5 * (1.0 + lax.erf(pre_act * 0.7071067811865476))
         hidden = (pre_act * cdf).astype(BF16)
-        hidden_scr[rows, :] = hidden
+        right_ref[1, rows, :] = hidden
         branch = jnp.dot(hidden, w_out_ref[...], preferred_element_type=F32) + b_out_ref[...]
         cot = cot_ref[rows, :]
+        left_ref[1, rows, :] = cot
         output_ref[rows, :] = (image_ref[rows, :].astype(F32) + branch).astype(BF16)
         d_hidden = lax.dot_general(
             cot, w_out_ref[...], (((1,), (1,)), ((), ())), preferred_element_type=F32
         )
         slope = cdf + pre_act * jnp.exp(-0.5 * pre_act * pre_act) * 0.3989422804014327
         d_pre = (d_hidden * slope).astype(BF16)
-        d_pre_scr[rows, :] = d_pre
+        right_ref[0, rows, :] = d_pre
         g_b_in = g_b_in + jnp.sum(d_pre.astype(F32), axis=0, keepdims=True)
         d_norm = lax.dot_general(
             d_pre, w_in_ref[...], (((1,), (1,)), ((), ())), preferred_element_type=F32
@@ -302,17 +343,11 @@
             - xhat * jnp.mean(g * xhat, axis=1, keepdims=True)
         )
         for i in range(step):
-            put_rows(d_conv[i * COLS : (i + 1) * COLS], k + i, out)
-    d_conv_ref[...] = out[...].astype(BF16)
-    contract = (((0,), (0,)), ((), ()))
-    grads_ref[0:C, :] = (
-        lax.dot_general(normed_scr[...], d_pre_scr[...], contract, preferred_element_type=F32)
-        * scale
-    ).astype(BF16)
-    grads_ref[C : 2 * C, :] = (
-        lax.dot_general(cot_ref[...], hidden_scr[...], contract, preferred_element_type=F32)
-        * scale
-    ).astype(BF16)
+            put_by_core(d_conv[i * COLS : (i + 1) * COLS], k + i, out)
+    half = CHIPS * MSG
+    theirs_ref[GRADS : GRADS + half, :] = out[pl.ds((1 - core) * half, half), :].astype(BF16)
+    mine_ref[...] = out[pl.ds(core * half, half), :].astype(BF16)
+    weight_grads(scale, left_ref, right_ref, 1 - core, theirs_ref)
     small_ref[...] = jnp.zeros((16, 128), F32)
     for i in range(FF // 128):
         small_ref[i : i + 1, :] = g_b_in[:, i * 128 : (i + 1) * 128] * scale
@@ -322,70 +357,129 @@
             small_ref[row : row + 1, :] = sums[n][:, i * 128 : (i + 1) * 128] * scale
 
 
-def strip_sum_kernel(parts_ref, grads_ref, out_ref):
-    total = parts_ref[0].astype(F32)
-    for i in range(1, STRIPS):
-        total = total + parts_ref[i].astype(F32)
-    for i in range(FF // 128):
-        out_ref[i * 16 : (i + 1) * 16, :] = total[:, i * 128 : (i + 1) * 128].astype(BF16)
-    out_ref[128:192, :] = grads_ref[...]
-
-
-def slide_sum_kernel(parts_ref, out_ref):
+def weight_grads(scale, left_ref, right_ref, which, out_ref):
+    grads = lax.dot_general(
+        left_ref[which], right_ref[which], (((0,), (0,)), ((), ())), preferred_element_type=F32
+    )
+    grads = (grads * scale).astype(out_ref.dtype)
+    for i in range(CHIPS):
+        for j in range(FF // 128):
+            at = (i * (FF // 128) + j) * 16
+            out_ref[at : at + 16, :] = grads[i * 16 : (i + 1) * 16, j * 128 : (j + 1) * 128]
+
+
+def own_grads_kernel(scale, core_ref, left_ref, right_ref, out_ref):
+    weight_grads(scale, left_ref, right_ref, core_ref[0], out_ref)
+
+
+def merge_kernel(core_ref, mine_ref, grads_ref, got_ref, out_ref):
+    half = CHIPS * MSG
+    mine = mine_ref[...].astype(F32)
+    got = got_ref[GRADS : GRADS + half, :].astype(F32)
+    low = core_ref[0] == 0
+    one, two = jnp.where(low, mine, got), jnp.where(low, got, mine)
+    for i in range(CHIPS):
+        rows = slice(i * MSG, (i + 1) * MSG)
+        out_ref[i, 0:DATA, :] = jnp.concatenate([one[rows], two[rows]], axis=0).astype(BF16)
+        rows = slice(i * OWN, (i + 1) * OWN)
+        out_ref[i, DATA : DATA + OWN, :] = (grads_ref[rows, :] + got_ref[rows, :].astype(F32)).astype(BF16)
+
+
+def pair_sum_kernel(mine_ref, got_ref, out_ref):
+    total = (mine_ref[...].astype(F32) + got_ref[...].astype(F32)).astype(BF16)
+    for i in range(out_ref.shape[0]):
+        out_ref[i] = total
+
+
+def gather_kernel(parts_ref, d_image_ref, out_ref):
     total = parts_ref[0].astype(F32)
     for i in range(1, parts_ref.shape[0]):
         total = total + parts_ref[i].astype(F32)
-    out_ref[...] = total.astype(BF16)
-
-
-SHARE = 192
+    total = total.astype(BF16)
+    for i in range(CHIPS):
+        out_ref[i, 0:DATA, :] = d_image_ref[i * DATA : (i + 1) * DATA, :]
+        out_ref[i, DATA : DATA + SHARE, :] = total
 
 
 def finish_kernel(
-    parts_ref, tall_ref, wide_ref, small_ref, w_in_ref, w_out_ref, scr, turn
+    core_ref,
+    mine_ref,
+    got_ref,
+    cot_ref,
+    out_ref,
+    tall_ref,
+    wide_ref,
+    gain_ref,
+    shift_ref,
+    w_in_ref,
+    b_in_ref,
+    w_out_ref,
+    b_out_ref,
+    scr,
+    turn,
 ):
-    for d in range(STRIPS):
-        part = parts_ref[d].astype(F32)
-        scr[d * SHARE : (d + 1) * SHARE, :] = part
-        for i in range(FF // 128):
-            piece = part[i * 16 : (i + 1) * 16]
-            if d < 16:
-                w_in_ref[d * 16 : (d + 1) * 16, i * 128 : (i + 1) * 128] = piece
-            else:
-                turn[(d - 16) * 16 : (d - 15) * 16, i * 128 : (i + 1) * 128] = piece
+    core = core_ref[0]
+    for i in range(CHIPS):
+        rows = slice(i * LAST, (i + 1) * LAST)
+        scr[core, rows, :] = mine_ref[i].astype(F32)
+        scr[1 - core, rows, :] = got_ref[i].astype(F32)
+    for k in range(ROWS):
+        d_image = untwisted(
+            [
+                scr.at[c][pl.ds(core * MSG + k * PAIRS + cp, CHIPS, stride=LAST), :]
+                for cp in range(PAIRS)
+                for c in range(CORES)
+            ]
+        )
+        out_ref[k] = (cot_ref[k].astype(F32) + d_image).astype(BF16)
+    for i in range(CHIPS):
+        for j in range(FF // 128):
+            at = i * LAST + DATA + j * 16
+            w_in_ref[i * 16 : (i + 1) * 16, j * 128 : (j + 1) * 128] = scr[0, at : at + 16, :]
+            turn[i * 16 : (i + 1) * 16, j * 128 : (j + 1) * 128] = scr[1, at : at + 16, :]
     for half in range(2):
-        for i in range(FF // 128):
-            w_out_ref[i * 128 : (i + 1) * 128, half * 128 : (half + 1) * 128] = turn[
-                half * 128 : (half + 1) * 128, i * 128 : (i + 1) * 128
+        for j in range(FF // 128):
+            w_out_ref[j * 128 : (j + 1) * 128, half * 128 : (half + 1) * 128] = turn[
+                half * 128 : (half + 1) * 128, j * 128 : (j + 1) * 128
             ].T
     for q in range(SHORT):
-        for start, ref in ((0, tall_ref), (20, wide_ref)):
-            rows = jnp.concatenate(
+        for start, is_tall in ((0, True), (20, False)):
+            taps = untwisted(
                 [
-                    scr[pl.ds(128 + start + q * PAIRS + cp, STRIPS, stride=SHARE), :]
+                    scr.at[c][pl.ds(DATA + OWN + start + q * PAIRS + cp, CHIPS, stride=LAST), :]
                     for cp in range(PAIRS)
-                ],
-                axis=0,
-            ).T
-            ref[q] = jnp.concatenate([rows[:COLS], rows[COLS:]], axis=1)
-    total = scr[176:192, :]
-    for d in range(1, STRIPS):
-        total = total + scr[d * SHARE + 176 : d * SHARE + 192, :]
-    small_ref[...] = total
-
-
-def residual_kernel(d_image_ref, cot_ref, out_ref, scr):
-    scr[...] = d_image_ref[...].astype(F32)
-    for k in range(ROWS):
-        out_ref[k] = (cot_ref[k].astype(F32) + get_rows(scr, k)).astype(BF16)
-
-
-def exchange(x, axis):
-    return lax.all_to_all(x, axis, 0, 0, tiled=True)
+                    for c in range(CORES)
+                ]
+            )[7 : 7 + LONG]
+            if is_tall:
+                tall_ref[:, q, :] = taps
+            else:
+                wide_ref[q] = taps
+    total = None
+    for c in range(CORES):
+        for i in range(CHIPS):
+            at = i * LAST + LAST - 16
+            part = scr[c, at : at + 16, :]
+            total = part if total is None else total + part
+    for i in range(FF // 128):
+        b_in_ref[:, i * 128 : (i + 1) * 128] = total[i : i + 1]
+    for n, ref in enumerate((gain_ref, shift_ref, b_out_ref)):
+        for i in range(2):
+            ref[:, i * 128 : (i + 1) * 128] = total[8 + 2 * n + i : 9 + 2 * n + i]
 
 
 def messages(x):
-    return exchange(x.reshape(STRIPS, MSG, 128), "strip").reshape(STRIPS * MSG, 128)
+    x = lax.all_to_all(x.reshape(STRIPS, MSG, 128), "strip", 0, 0, tiled=True)
+    return x.reshape(STRIPS * MSG, 128)
+
+
+def between_chips(x):
+    groups = [[CORES * i + c for i in range(CHIPS)] for c in range(CORES)]
+    return lax.all_to_all(x, "strip", 0, 0, axis_index_groups=groups, tiled=True)
+
+
+def between_cores(x):
+    return lax.ppermute(x, "strip", [(i, i ^ 1) for i in range(STRIPS)])
 
 
 def shape(dims, dtype):
@@ -414,6 +508,8 @@
 
     image_msg = call(pack_kernel, packed_b, [packed_f])(source)
     me = lax.axis_index("strip")
+    core = (me % CORES).reshape(1)
+    me = (me % CORES) * CHIPS + me // CORES
     own = jnp.arange(8)[:, None] * STRIPS + me == jnp.arange(C)[None, :]
     own = own.astype(BF16)
 
@@ -433,24 +529,20 @@
         [packed_f, edge, packed_f],
     )(image_ch, tall, wide_flipped)
     conv = messages(conv_ch)
-    output, d_conv_msg, grads, small = call(
+    output, theirs, mine, left, right, small = call(
         functools.partial(mlp_kernel, scale),
         (
             shape((CELLS, C), BF16),
-            packed_b,
-            shape((2 * C, FF), BF16),
+            shape((GRADS + CHIPS * MSG, 128), BF16),
+            shape((CHIPS * MSG, 128), BF16),
+            shape((2, CELLS, C), BF16),
+            shape((2, CELLS, FF), BF16),
             shape((16, 128), F32),
         ),
-        [
-            packed_f,
-            pltpu.VMEM((8, 128), F32),
-            pltpu.VMEM((8, 128), F32),
-            pltpu.VMEM((CELLS, C), BF16),
-            pltpu.VMEM((CELLS, FF), BF16),
-            pltpu.VMEM((CELLS, FF), BF16),
-            packed_f,
-        ],
+        [packed_f, packed_f],
+        9,
     )(
+        core,
         conv,
         source.reshape(CELLS, C),
         upstream.reshape(CELLS, C),
@@ -461,45 +553,53 @@
         w_out,
         b_out[None],
     )
-    d_conv = messages(d_conv_msg)
-    grad_parts = exchange(grads.reshape(STRIPS, 16, FF), "strip")
-    d_image_msg, own_grads = call(
+    got = between_cores(theirs)
+    chip_grads = call(
+        functools.partial(own_grads_kernel, scale), shape((GRADS, 128), F32), (), 2
+    )(core, left, right)
+    merged = call(merge_kernel, shape((CHIPS, DATA + OWN, 128), BF16), (), 3)(
+        core, mine, chip_grads, got
+    )
+    d_image_msg, share = call(
         functools.partial(backward_kernel, scale),
-        (packed_b, shape((64, 128), BF16)),
+        (packed_b, shape((SHARE, 128), BF16)),
         [packed_f, packed_f, edge, edge, packed_f, pltpu.VMEM((64, 128), F32)],
-    )(d_conv, image_ch, mixed, tall_flipped, wide, small)
-    d_image = messages(d_image_msg)
-    share = call(strip_sum_kernel, shape((SHARE, 128), BF16))(grad_parts, own_grads)
-    shares = exchange(jnp.broadcast_to(share[None], (slides, SHARE, 128)), "slide")
-    total = call(slide_sum_kernel, shape((SHARE, 128), BF16))(shares)
-    totals = exchange(jnp.broadcast_to(total[None], (STRIPS, SHARE, 128)), "strip")
-    long_tall, long_wide, small_sum, g_w_in, g_w_out = call(
+    )(between_chips(merged), image_ch, mixed, tall_flipped, wide, small)
+    got = lax.ppermute(share, "slide", [(i, i ^ 1) for i in range(slides)])
+    half = slides // 2
+    copies = call(pair_sum_kernel, shape((half, SHARE, 128), BF16))(share, got)
+    groups = [[2 * i + j for i in range(half)] for j in range(2)]
+    parts = lax.all_to_all(copies, "slide", 0, 0, axis_index_groups=groups, tiled=True)
+    last = call(gather_kernel, shape((CHIPS, LAST, 128), BF16))(parts, d_image_msg)
+    last = between_chips(last)
+    got = between_cores(last)
+    grad_image, g_tall, g_wide, g_gain, g_shift, g_w_in, g_b_in, g_w_out, g_b_out = call(
         finish_kernel,
         (
-            shape((SHORT, COLS, C), F32),
-            shape((SHORT, COLS, C), F32),
-            shape((16, 128), F32),
+            shape((ROWS, COLS, C), BF16),
+            shape((LONG, SHORT, C), F32),
+            shape((SHORT, LONG, C), F32),
+            shape((1, C), F32),
+            shape((1, C), F32),
             shape((C, FF), F32),
+            shape((1, FF), F32),
             shape((FF, C), F32),
+            shape((1, C), F32),
         ),
-        [pltpu.VMEM((STRIPS * SHARE, 128), F32), pltpu.VMEM((C, FF), F32)],
-    )(totals)
-    grad_image = call(residual_kernel, shape((ROWS, COLS, C), BF16), [packed_f])(d_image, upstream)
-    g_tall = jnp.transpose(long_tall[:, 7 : 7 + LONG], (1, 0, 2))
-    g_wide = long_wide[:, 7 : 7 + LONG]
-    g_b_in = small_sum[:8].reshape(FF)
-    g_gain, g_shift, g_b_out = (small_sum[8 + 2 * i : 10 + 2 * i].reshape(C) for i in range(3))
+        [pltpu.VMEM((CORES, CHIPS * LAST, 128), F32), pltpu.VMEM((C, FF), F32)],
+        3,
+    )(core, last, got, upstream)
     return (
         output.reshape(image.shape),
         grad_image[None],
         g_tall,
         g_wide,
-        g_gain,
-        g_shift,
+        g_gain[0],
+        g_shift[0],
         g_w_in,
-        g_b_in,
+        g_b_in[0],
         g_w_out,
-        g_b_out,
+        g_b_out[0],
     )
 
 

time: 195 us -> 148 us (0.76)
  waiting for transfers between devices: 83.6 us -> 38.7 us
  local copies, waits for them, and re-layouts: 5.47 us -> 1.98 us
  starting transfers between devices: 24.7 us -> 27.3 us
    all_to_all x4 -> x2, waiting for transfers between devices: 83.6 us -> 32.1 us  [the longest x1 21.8 us: between_chips(): lax.all_to_all(x, 'strip', 0, 0, axis_index_groups=groups, tiled=True)]
    ppermute x0 -> x3, starting transfers between devices: none -> 12.5 us  [the longest x2 10.6 us: between_cores(): return lax.ppermute(x, 'strip', [(i, i ^ 1) for i in range(STRIPS)])]
    all_to_all x4 -> x2, starting transfers between devices: 24.7 us -> 14.8 us  [the longest x1 11.2 us: messages(): x = lax.all_to_all(x.reshape(STRIPS, MSG, 128), 'strip', 0, 0, tiled=True)]
    ppermute x0 -> x3, waiting for transfers between devices: none -> 6.59 us  [the longest x2 3.69 us: between_cores(): return lax.ppermute(x, 'strip', [(i, i ^ 1) for i in range(STRIPS)])]
    pallas_call x6 -> x7, Pallas kernels: 12.3 us -> 12.2 us  [the longest x1 5.17 us: local(): call(functools.partial(backward_kernel, scale), (packed_b, shape((SHARE,...]
  transfers between devices with their start and end apart: 4 -> 5, of which waited for: 4 -> 5; matrix products, arithmetic and copies ran while one was open for 1% -> 1% of each run, Pallas kernels for 4% -> 0%
where the time goes in v1:
time: 148 us
  blocking collectives  62.5 us (42%)
  waiting for transfers between devices  38.7 us (26%)
  starting transfers between devices  27.3 us (18%)
  Pallas kernels  15.1 us (10%)
  local copies, waits for them, and re-layouts  1.98 us (1%)
    all_to_all x1, blocking collectives, between_chips(): lax.all_to_all(x, 'strip', 0, 0, axis_index_groups=groups, tiled=True)  25.4 us
    all_to_all x1, waiting for transfers between devices, between_chips(): lax.all_to_all(x, 'strip', 0, 0, axis_index_groups=groups, tiled=True)  21.8 us
    all_to_all x1, blocking collectives, local(): lax.all_to_all(copies, 'slide', 0, 0, axis_index_groups=groups, tiled=True)  21.1 us
    all_to_all x1, blocking collectives, messages(): x = lax.all_to_all(x.reshape(STRIPS, MSG, 128), 'strip', 0, 0, tiled=True)  16 us
    all_to_all x1, starting transfers between devices, messages(): x = lax.all_to_all(x.reshape(STRIPS, MSG, 128), 'strip', 0, 0, tiled=True)  11.2 us
    ppermute x2, starting transfers between devices, between_cores(): return lax.ppermute(x, 'strip', [(i, i ^ 1) for i in range(STRIPS)])  10.6 us
    all_to_all x1, waiting for transfers between devices, messages(): x = lax.all_to_all(x.reshape(STRIPS, MSG, 128), 'strip', 0, 0, tiled=True)  10.4 us
    pallas_call x1, Pallas kernels, local(): call(functools.partial(backward_kernel, scale), (packed_b, shape((SHARE,...  5.17 us
  transfers between devices with their start and end apart: 5, of which 5 were waited for; matrix products, arithmetic and copies ran while one was open for 1% of the time, Pallas kernels for 0%

profile of v1, /device:TPU:1, one launch (start us, length us, event | category | flops | bytes accessed | tf_op | source)
XLA Modules:
  0.0 147.8 jit_solution(9552669434226522984)
XLA Ops:
  0.6 0.0 copy-start
  0.7 0.0 copy-start.1
  0.7 0.0 copy-start.2
  0.7 1.0 copy-done.2
  1.7 0.0 copy-start.7
  1.7 0.0 copy-start.8
  1.7 0.9 shard_map.177
  2.6 11.2 %all-to-all-start = ((bf16[32,24,128]{2,1,0:T(8,128)(2,1)}), bf16[32,24,128]{2,1,0:T(8,128)(2,1)S(1)}, u32[]{:S(2)}, u32[]{:S(2)}) async-start(bf16[32,24,128]{2,1,0:T(8,128)(2,1)} %bitcast.2), calls=%async_computation | async-start | bytes 393216 | tf_op jit(solution)/shard_map/all_to_all | solution.py:472
  13.8 0.2 convolution_bitcast_fusion
  14.0 0.1 rev.6
  14.1 1.1 convolution_bitcast_fusion.1
  15.2 10.4 %all-to-all-done = bf16[32,24,128]{2,1,0:T(8,128)(2,1)S(1)} async-done(((bf16[32,24,128]{2,1,0:T(8,128)(2,1)}), bf16[32,24,128]{2,1,0:T(8,128)(2,1)S(1)}, u32[]{:S(2)}, u32[]{:S(2)}) %all-to-all-start) | async-done | bytes 196640 | tf_op jit(solution)/shard_map/all_to_all | solution.py:472
  25.6 2.0 %shard_map.178 = (bf16[768,128]{1,0:T(8,128)(2,1)S(1)}, bf16[4,192,128]{2,1,0:T(8,128)(2,1)S(1)}) custom-call(bf16[768,128]{1,0:T(8,128)(2,1)S(1)} %bitcast.33, f32[40,128]{1,0:T(8,128)S(1)} %pad.13.tall_ref, f32[40,128]{1,0:T(8,128)S(1)} %pad.14.wide_ref), custom_call_target="tpu_custom_call" | custom-call | tf_op jit(solution)/shard_map/pallas_call | solution.py:526
  27.6 16.0 %all_to_all.25 = bf16[32,24,128]{2,1,0:T(8,128)(2,1)S(1)} all-to-all(bf16[32,24,128]{2,1,0:T(8,128)(2,1)S(1)} %bitcast.40), channel_id=1, replica_groups=mesh['slide'=16,'strip'=32] {'strip'}, dimensions={0} | all-to-all | bytes 393216 | tf_op jit(solution)/shard_map/all_to_all | solution.py:472
  43.6 3.2 %shard_map.179 = (bf16[384,256]{1,0:T(8,128)(2,1)}, bf16[2432,128]{1,0:T(8,128)(2,1)S(1)}, bf16[384,128]{1,0:T(8,128)(2,1)S(1)}, bf16[2,384,256]{2,1,0:T(8,128)(...) custom-call(s32[1]{0:T(128)} %bitcast.core_ref, bf16[768,128]{1,0:T(8,128)(2,1)S(1)} %bitcast.39, ...), custom_call_target="tpu_custom_call" | custom-call | tf_op jit(solution)/shard_map/pallas_call | solution.py:532
  46.8 1.9 %collective-permute-start = (bf16[2432,128]{1,0:T(8,128)(2,1)S(1)}, bf16[2432,128]{1,0:T(8,128)(2,1)S(1)}, u32[]{:S(2)}, u32[]{:S(2)}) collective-permute-start(bf16[2432,128]{1,0:T(8,128)(2,1)S(1)} %get-tuple-element.34), channel_id=1, source_target_pairs={{0,1},{1,0},{2,3},{3,2},{4,5},{5,4},{6,7},{7,6},{8,9},{9,8},{10,11... | collective-permute-start | bytes 1867784 | tf_op jit(solution)/shard_map/ppermute | solution.py:482
  48.8 0.5 shard_map.180.grads_ref
  49.2 1.5 %collective-permute-done.got_ref = bf16[2432,128]{1,0:T(8,128)(2,1)S(1)} collective-permute-done((bf16[2432,128]{1,0:T(8,128)(2,1)S(1)}, bf16[2432,128]{1,0:T(8,128)(2,1)S(1)}, u32[]{:S(2)}, u32[]{:S(2)}) %collective-permute-start) | collective-permute-done | bytes 622624 | tf_op jit(solution)/shard_map/ppermute | solution.py:482
  50.8 1.0 shard_map.181
  51.8 3.6 %all-to-all-start.2 = ((bf16[16,176,128]{2,1,0:T(8,128)(2,1)}), bf16[16,176,128]{2,1,0:T(8,128)(2,1)S(1)}, u32[]{:S(2)}, u32[]{:S(2)}) async-start(bf16[16,176,128]{2,1,0:T(8,128)(2,1)} %shard_map.181), calls=%async_computation.2 | async-start | bytes 1441792 | tf_op jit(solution)/shard_map/all_to_all | solution.py:478
  55.4 0.1 rev.7
  55.5 21.8 %all-to-all-done.2.parts_ref = bf16[16,176,128]{2,1,0:T(8,128)(2,1)S(1)} async-done(((bf16[16,176,128]{2,1,0:T(8,128)(2,1)}), bf16[16,176,128]{2,1,0:T(8,128)(2,1)S(1)}, u32[]{:S(2)}, u32[]{:S(2)}) %all-to-all-start.2) | async-done | bytes 720928 | tf_op jit(solution)/shard_map/all_to_all | solution.py:478
  77.2 5.2 %shard_map.182 = (bf16[768,128]{1,0:T(8,128)(2,1)S(1)}, bf16[192,128]{1,0:T(8,128)(2,1)S(1)}) custom-call(bf16[16,176,128]{2,1,0:T(8,128)(2,1)S(1)} %all-to-all-done.2.parts_ref, bf16[768,128]{1,0:T(8,128)(2,1)S(1)} %bitcast.34, bf16[4,192,128]{2,1,0:T(8,128)(2,1)S(1)} %get-tuple-element.35.mixed_ref, f32[40,128]{1,0:T(8,128)S(1)} %pad.15.tall_ref, ...), custom_call_target="tpu_custom_call" | custom-call | tf_op jit(solution)/shard_map/pallas_call | solution.py:563
  82.4 1.9 %collective-permute-start.1 = (bf16[192,128]{1,0:T(8,128)(2,1)S(1)}, bf16[192,128]{1,0:T(8,128)(2,1)S(1)}, u32[]{:S(2)}, u32[]{:S(2)}) collective-permute-start(bf16[192,128]{1,0:T(8,128)(2,1)S(1)} %get-tuple-element.37.mine_ref), channel_id=1, source_target_pairs={{0,32},{32,0},{64,96},{96,64},{128,160},{160,128},{192,224},{224,1... | collective-permute-start | bytes 147464 | tf_op jit(solution)/shard_map/ppermute | solution.py:568
  84.3 2.9 %collective-permute-done.1.got_ref = bf16[192,128]{1,0:T(8,128)(2,1)S(1)} collective-permute-done((bf16[192,128]{1,0:T(8,128)(2,1)S(1)}, bf16[192,128]{1,0:T(8,128)(2,1)S(1)}, u32[]{:S(2)}, u32[]{:S(2)}) %collective-permute-start.1) | collective-permute-done | bytes 49184 | tf_op jit(solution)/shard_map/ppermute | solution.py:568
  87.3 21.1 %all_to_all.26.parts_ref = bf16[8,192,128]{2,1,0:T(8,128)(2,1)S(1)} all-to-all(bf16[8,192,128]{2,1,0:T(8,128)(2,1)S(1)} %shard_map.183), channel_id=1, replica_groups={{0,64,128,192,256,320,384,448},{32,96,160,224,288,352,416,480},{1,65,12..., dimensions={0} | all-to-all | bytes 786432 | tf_op jit(solution)/shard_map/all_to_all | solution.py:572
  108.4 0.1 shard_map.184
  108.5 25.4 %all_to_all.27.mine_ref = bf16[16,240,128]{2,1,0:T(8,128)(2,1)S(1)} all-to-all(bf16[16,240,128]{2,1,0:T(8,128)(2,1)S(1)} %shard_map.184), channel_id=1, replica_groups={{0,2,4,6,8,10,12,14,16,18,20,22,24,26,28,30},{1,3,5,7,9,11,13,15,17,19,..., dimensions={0} | all-to-all | bytes 1966080 | tf_op jit(solution)/shard_map/all_to_all | solution.py:478
  133.9 8.7 %collective-permute-start.2 = (bf16[16,240,128]{2,1,0:T(8,128)(2,1)S(1)}, bf16[16,240,128]{2,1,0:T(8,128)(2,1)S(1)}, u32[]{:S(2)}, u32[]{:S(2)}) collective-permute-start(bf16[16,240,128]{2,1,0:T(8,128)(2,1)S(1)} %all_to_all.27.mine_ref), channel_id=1, source_target_pairs={{0,1},{1,0},{2,3},{3,2},{4,5},{5,4},{6,7},{7,6},{8,9},{9,8},{10,11... | collective-permute-start | bytes 2949128 | tf_op jit(solution)/shard_map/ppermute | solution.py:482
  142.6 2.2 %collective-permute-done.2.got_ref = bf16[16,240,128]{2,1,0:T(8,128)(2,1)S(1)} collective-permute-done((bf16[16,240,128]{2,1,0:T(8,128)(2,1)S(1)}, bf16[16,240,128]{2,1,0:T(8,128)(2,1)S(1)}, u32[]{:S(2)}, u32[]{:S(2)}) %collective-permute-start.2) | collective-permute-done | bytes 983072 | tf_op jit(solution)/shard_map/ppermute | solution.py:482
  144.7 2.3 %shard_map.185 = (bf16[6,64,256]{2,1,0:T(8,128)(2,1)}, f32[51,5,256]{2,1,0:T(8,128)S(1)}, f32[5,51,256]{2,1,0:T(8,128)}, f32[1,256]{1,0:T(1,128)}, f32[1,256]{1,...) custom-call(s32[1]{0:T(128)} %bitcast.core_ref, ...), custom_call_target="tpu_custom_call" | custom-call | tf_op jit(solution)/shard_map/pallas_call | solution.py:576
  147.0 0.8 copy.20
  (20 shorter events, 0.1 us)
Async XLA Ops:
  0.6 13.2 %copy-start = (bf16[5,51,256]{2,1,0:T(8,128)(2,1)S(1)}, bf16[5,51,256]{2,1,0:T(8,128)(2,1)}, u32[]{:S(2)}) copy-start(bf16[5,51,256]{2,1,0:T(8,128)(2,1)} %param.13) | copy-start | bytes 391684
  0.7 42.9 %copy-start.1 = (bf16[1,6,64,256]{3,2,1,0:T(8,128)(2,1)S(1)}, bf16[1,6,64,256]{3,2,1,0:T(8,128)(2,1)}, u32[]{:S(2)}) copy-start(bf16[1,6,64,256]{3,2,1,0:T(8,128)(2,1)} %param.11) | copy-start | bytes 589828
  0.7 1.0 copy-start.2
  1.6 41.9 %copy-start.3 = (bf16[1,6,64,256]{3,2,1,0:T(8,128)(2,1)S(1)}, bf16[1,6,64,256]{3,2,1,0:T(8,128)(2,1)}, u32[]{:S(2)}) copy-start(bf16[1,6,64,256]{3,2,1,0:T(8,128)(2,1)} %param.10) | copy-start | bytes 589828
  1.6 41.9 %copy-start.4 = (bf16[256,1024]{1,0:T(8,128)(2,1)S(1)}, bf16[256,1024]{1,0:T(8,128)(2,1)}, u32[]{:S(2)}) copy-start(bf16[256,1024]{1,0:T(8,128)(2,1)} %w_in_ref.1) | copy-start | bytes 1572868
  1.6 42.0 %copy-start.5 = (bf16[1024,256]{1,0:T(8,128)(2,1)S(1)}, bf16[1024,256]{1,0:T(8,128)(2,1)}, u32[]{:S(2)}) copy-start(bf16[1024,256]{1,0:T(8,128)(2,1)} %w_out_ref.1) | copy-start | bytes 1572868
  1.7 42.0 %copy-start.6 = (f32[1024]{0:T(1024)S(1)}, f32[1024]{0:T(1024)}, u32[]{:S(2)}) copy-start(f32[1024]{0:T(1024)} %param.17) | copy-start | bytes 12292
  1.7 42.0 %copy-start.7 = (f32[256]{0:T(256)S(1)}, f32[256]{0:T(256)}, u32[]{:S(2)}) copy-start(f32[256]{0:T(256)} %param.14) | copy-start | bytes 3076
  1.7 42.0 %copy-start.8 = (f32[256]{0:T(256)S(1)}, f32[256]{0:T(256)}, u32[]{:S(2)}) copy-start(f32[256]{0:T(256)} %param.15) | copy-start | bytes 3076
  1.7 42.0 %copy-start.9 = (f32[256]{0:T(256)S(1)}, f32[256]{0:T(256)}, u32[]{:S(2)}) copy-start(f32[256]{0:T(256)} %param.19) | copy-start | bytes 3076
  2.6 23.0 %all-to-all-start = ((bf16[32,24,128]{2,1,0:T(8,128)(2,1)}), bf16[32,24,128]{2,1,0:T(8,128)(2,1)S(1)}, u32[]{:S(2)}, u32[]{:S(2)}) async-start(bf16[32,24,128]{2,1,0:T(8,128)(2,1)} %bitcast.2), calls=%async_computation | async-start | bytes 393216 | tf_op jit(solution)/shard_map/all_to_all | solution.py:472
  46.8 3.9 %collective-permute-start = (bf16[2432,128]{1,0:T(8,128)(2,1)S(1)}, bf16[2432,128]{1,0:T(8,128)(2,1)S(1)}, u32[]{:S(2)}, u32[]{:S(2)}) collective-permute-start(bf16[2432,128]{1,0:T(8,128)(2,1)S(1)} %get-tuple-element.34), channel_id=1, source_target_pairs={{0,1},{1,0},{2,3},{3,2},{4,5},{5,4},{6,7},{7,6},{8,9},{9,8},{10,11... | collective-permute-start | bytes 1867784 | tf_op jit(solution)/shard_map/ppermute | solution.py:482
  51.8 25.5 %all-to-all-start.2 = ((bf16[16,176,128]{2,1,0:T(8,128)(2,1)}), bf16[16,176,128]{2,1,0:T(8,128)(2,1)S(1)}, u32[]{:S(2)}, u32[]{:S(2)}) async-start(bf16[16,176,128]{2,1,0:T(8,128)(2,1)} %shard_map.181), calls=%async_computation.2 | async-start | bytes 1441792 | tf_op jit(solution)/shard_map/all_to_all | solution.py:478
  82.4 4.8 %collective-permute-start.1 = (bf16[192,128]{1,0:T(8,128)(2,1)S(1)}, bf16[192,128]{1,0:T(8,128)(2,1)S(1)}, u32[]{:S(2)}, u32[]{:S(2)}) collective-permute-start(bf16[192,128]{1,0:T(8,128)(2,1)S(1)} %get-tuple-element.37.mine_ref), channel_id=1, source_target_pairs={{0,32},{32,0},{64,96},{96,64},{128,160},{160,128},{192,224},{224,1... | collective-permute-start | bytes 147464 | tf_op jit(solution)/shard_map/ppermute | solution.py:568
  133.9 10.8 %collective-permute-start.2 = (bf16[16,240,128]{2,1,0:T(8,128)(2,1)S(1)}, bf16[16,240,128]{2,1,0:T(8,128)(2,1)S(1)}, u32[]{:S(2)}, u32[]{:S(2)}) collective-permute-start(bf16[16,240,128]{2,1,0:T(8,128)(2,1)S(1)} %all_to_all.27.mine_ref), channel_id=1, source_target_pairs={{0,1},{1,0},{2,3},{3,2},{4,5},{5,4},{6,7},{7,6},{8,9},{9,8},{10,11... | collective-permute-start | bytes 2949128 | tf_op jit(solution)/shard_map/ppermute | solution.py:482

commit v2 on v1

--- a/solution.py
+++ b/solution.py
@@ -27,25 +27,30 @@
 DATA = CORES * MSG
 GRADS = C * FF // 128
 OWN = GRADS // CHIPS
-SHARE = OWN + 64
+SHARE = OWN + 48
 LAST = DATA + SHARE
 epsilon = 1e-06
 
 PARAMS = pltpu.CompilerParams(vmem_limit_bytes=48 * 1024 * 1024)
 
 
-def call(kernel, out_shape, scratch=(), scalars=0):
-    extra = {}
-    if scalars:
-        vmem = pl.BlockSpec(memory_space=pltpu.VMEM)
-        smem = pl.BlockSpec(memory_space=pltpu.SMEM)
-        extra["in_specs"] = [smem] + [vmem] * scalars
+VMEM = pl.BlockSpec(memory_space=pltpu.VMEM)
+SMEM = pl.BlockSpec(memory_space=pltpu.SMEM)
+ANY = pl.BlockSpec(memory_space=pl.ANY)
+
+
+def call(kernel, out_shape, scratch=(), in_specs=None, out_specs=None):
+    specs = {}
+    if in_specs is not None:
+        specs["in_specs"] = in_specs
+    if out_specs is not None:
+        specs["out_specs"] = out_specs
     return pl.pallas_call(
         kernel,
         out_shape=out_shape,
-        **extra,
         scratch_shapes=list(scratch),
         compiler_params=PARAMS,
+        **specs,
     )
 
 
@@ -114,14 +119,7 @@
     return (row < COLS) == (lane < COLS)
 
 
-def tall_conv(padded, taps_ref, cp, sign):
-    matrix = jnp.concatenate(
-        [
-            jnp.concatenate([tall_matrix(taps_ref, q, c2 * 4 + cp) for c2 in range(2)], axis=1)
-            for q in range(SHORT)
-        ],
-        axis=0,
-    ).astype(BF16)
+def tall_conv(padded, matrix, sign):
     _, first = half_masks((128, 128))
     zero = jnp.zeros((128, 128), BF16)
     sides = []
@@ -142,15 +140,24 @@
     return jnp.concatenate(bands, axis=0)
 
 
-def wide_conv(scr, taps_ref, cp, sign, in_block):
-    source = jnp.concatenate(
+def moved_rows(scr, sign):
+    return jnp.concatenate(
         [scr[8 + sign * (p - 2) : 8 + sign * (p - 2) + H, :].astype(BF16) for p in range(SHORT)],
         axis=1,
     )
-    matrix = jnp.concatenate(
-        [wide_matrix(taps_ref, p, cp, in_block) for p in range(SHORT)], axis=0
-    ).astype(BF16)
-    return jnp.dot(source, matrix, preferred_element_type=F32)
+
+
+def matrix_kernel(tall_ref, wide_ref, tall_out, wide_out):
+    in_block = block_mask()
+    for cp in range(PAIRS):
+        for q in range(SHORT):
+            rows = slice(q * BAND, (q + 1) * BAND)
+            for c2 in range(2):
+                lanes = slice(c2 * 128, (c2 + 1) * 128)
+                tall_out[cp, rows, lanes] = tall_matrix(tall_ref, q, c2 * 4 + cp).astype(BF16)
+            wide_out[cp, q * 128 : (q + 1) * 128, :] = wide_matrix(
+                wide_ref, q, cp, in_block
+            ).astype(BF16)
 
 
 def pad_rows(x):
@@ -158,23 +165,29 @@
     return jnp.concatenate([zero, x, zero], axis=0)
 
 
-def pack_kernel(image_ref, out_ref, scr):
+def pack_kernel(image_ref, out_ref, rows, scr, sems):
+    copies = [pltpu.make_async_copy(image_ref.at[k], rows.at[k], sems.at[k]) for k in range(ROWS)]
+    for copy in copies:
+        copy.start()
     for k in range(ROWS):
-        put_by_strip(image_ref[k].astype(F32), k, scr)
+        copies[k].wait()
+        put_by_strip(rows[k].astype(F32), k, scr)
     out_ref[...] = scr[...].astype(BF16)
 
 
-def forward_kernel(image_ref, tall_ref, wide_ref, conv_ref, mixed_ref, scr, pad, out):
+def forward_kernel(image_ref, tall_ref, wide_ref, conv_ref, moved_ref, padded_ref, scr, pad, out):
     scr[...] = image_ref[...].astype(F32)
-    in_block = block_mask()
     pad[0:8, :] = jnp.zeros((8, 128), F32)
     pad[H + 8 : H + 16, :] = jnp.zeros((8, 128), F32)
     for cp in range(PAIRS):
-        source = scr[pl.ds(cp, H, stride=PAIRS), :].astype(BF16)
-        mixed = tall_conv(pad_rows(source), tall_ref, cp, 1).astype(BF16)
-        mixed_ref[cp] = mixed
-        pad[8 : H + 8, :] = mixed.astype(F32)
-        out[pl.ds(cp, H, stride=PAIRS), :] = wide_conv(pad, wide_ref, cp, 1, in_block)
+        padded = pad_rows(scr[pl.ds(cp, H, stride=PAIRS), :].astype(BF16))
+        padded_ref[cp] = padded
+        pad[8 : H + 8, :] = tall_conv(padded, tall_ref[cp], 1).astype(BF16).astype(F32)
+        moved = moved_rows(pad, 1)
+        moved_ref[cp] = moved
+        out[pl.ds(cp, H, stride=PAIRS), :] = jnp.dot(
+            moved, wide_ref[cp], preferred_element_type=F32
+        )
     conv_ref[...] = out[...].astype(BF16)
 
 
@@ -192,18 +205,14 @@
 def backward_kernel(
     scale,
     parts_ref,
-    image_ref,
-    mixed_ref,
-    tall_ref,
+    padded_ref,
+    moved_ref,
     wide_ref,
     small_ref,
-    d_image_ref,
+    d_mixed_ref,
     share_ref,
     d_scr,
-    i_scr,
     d_pad,
-    m_pad,
-    out,
     g_scr,
 ):
     total = None
@@ -212,26 +221,21 @@
         d_scr[i * DATA : (i + 1) * DATA, :] = part[:DATA]
         total = part[DATA:] if total is None else total + part[DATA:]
     share_ref[0:OWN, :] = total.astype(BF16)
-    i_scr[...] = image_ref[...].astype(F32)
     in_block = block_mask()
-    for ref in (d_pad, m_pad):
-        ref[0:8, :] = jnp.zeros((8, 128), F32)
-        ref[H + 8 : H + 16, :] = jnp.zeros((8, 128), F32)
-    g_scr[40:48, :] = jnp.zeros((8, 128), F32)
-    g_scr[48:64, :] = small_ref[...]
+    d_pad[0:8, :] = jnp.zeros((8, 128), F32)
+    d_pad[H + 8 : H + 16, :] = jnp.zeros((8, 128), F32)
+    g_scr[40:48, :] = small_ref[...]
     lane, first = half_masks((1, 128))
     lane_b, first_b = half_masks((BAND, 128))
     for cp in range(PAIRS):
         d_conv = d_scr[pl.ds(cp, H, stride=PAIRS), :]
         d_pad[8 : H + 8, :] = d_conv
-        m_pad[8 : H + 8, :] = mixed_ref[cp].astype(F32)
-        source = pad_rows(i_scr[pl.ds(cp, H, stride=PAIRS), :].astype(BF16))
-        d_mixed = wide_conv(d_pad, wide_ref, cp, -1, in_block).astype(BF16)
-        moved = jnp.concatenate(
-            [m_pad[6 + p : 6 + p + H, :].astype(BF16) for p in range(SHORT)], axis=1
-        )
+        d_mixed = jnp.dot(
+            moved_rows(d_pad, -1), wide_ref[cp], preferred_element_type=F32
+        ).astype(BF16)
+        d_mixed_ref[cp] = d_mixed
         corr = lax.dot_general(
-            d_conv.astype(BF16), moved, (((0,), (0,)), ((), ())), preferred_element_type=F32
+            d_conv.astype(BF16), moved_ref[cp], (((0,), (0,)), ((), ())), preferred_element_type=F32
         )
         for p in range(SHORT):
             part = jnp.where(in_block, corr[:, p * 128 : (p + 1) * 128], 0.0)
@@ -253,7 +257,7 @@
                 left.append(jnp.concatenate(bands, axis=1))
         left = jnp.concatenate(left, axis=0).astype(BF16)
         right = jnp.concatenate(
-            [source[b * BAND : b * BAND + 128] for b in range(H // BAND)], axis=1
+            [padded_ref[cp, b * BAND : b * BAND + 128, :] for b in range(H // BAND)], axis=1
         )
         corr = lax.dot_general(
             left, right, (((1,), (1,)), ((), ())), preferred_element_type=F32
@@ -263,9 +267,15 @@
             high = diagonal(corr[(SHORT + q) * BAND : (SHORT + q + 1) * BAND], COLS)
             row = q * PAIRS + cp
             g_scr[row : row + 1, :] = jnp.where(first, low, high) * scale
-        out[pl.ds(cp, H, stride=PAIRS), :] = tall_conv(pad_rows(d_mixed), tall_ref, cp, -1)
+    share_ref[OWN:SHARE, :] = g_scr[...].astype(BF16)
+
+
+def d_image_kernel(d_mixed_ref, tall_ref, d_image_ref, out):
+    for cp in range(PAIRS):
+        out[pl.ds(cp, H, stride=PAIRS), :] = tall_conv(
+            pad_rows(d_mixed_ref[cp]), tall_ref[cp], -1
+        )
     d_image_ref[...] = out[...].astype(BF16)
-    share_ref[OWN:SHARE, :] = g_scr[...].astype(BF16)
 
 
 def mlp_kernel(
@@ -288,6 +298,7 @@
     small_ref,
     scr,
     out,
+    small,
 ):
     core = core_ref[0]
     scr[...] = conv_ref[...].astype(F32)
@@ -348,13 +359,18 @@
     theirs_ref[GRADS : GRADS + half, :] = out[pl.ds((1 - core) * half, half), :].astype(BF16)
     mine_ref[...] = out[pl.ds(core * half, half), :].astype(BF16)
     weight_grads(scale, left_ref, right_ref, 1 - core, theirs_ref)
-    small_ref[...] = jnp.zeros((16, 128), F32)
+    small[...] = jnp.zeros((16, 128), F32)
     for i in range(FF // 128):
-        small_ref[i : i + 1, :] = g_b_in[:, i * 128 : (i + 1) * 128] * scale
+        small[i : i + 1, :] = g_b_in[:, i * 128 : (i + 1) * 128] * scale
     for n in range(3):
         for i in range(2):
             row = 8 + 2 * n + i
-            small_ref[row : row + 1, :] = sums[n][:, i * 128 : (i + 1) * 128] * scale
+            small[row : row + 1, :] = sums[n][:, i * 128 : (i + 1) * 128] * scale
+    small_ref[...] = small[pl.ds(core * 8, 8), :]
+    other = small[pl.ds((1 - core) * 8, 8), :]
+    theirs_ref[GRADS + half : GRADS + half + 16, :] = jnp.concatenate(
+        [other, jnp.zeros((8, 128), F32)], axis=0
+    ).astype(BF16)
 
 
 def weight_grads(scale, left_ref, right_ref, which, out_ref):
@@ -372,10 +388,12 @@
     weight_grads(scale, left_ref, right_ref, core_ref[0], out_ref)
 
 
-def merge_kernel(core_ref, mine_ref, grads_ref, got_ref, out_ref):
+def merge_kernel(core_ref, mine_ref, grads_ref, small_ref, got_ref, out_ref, small_out):
     half = CHIPS * MSG
     mine = mine_ref[...].astype(F32)
     got = got_ref[GRADS : GRADS + half, :].astype(F32)
+    other = got_ref[GRADS + half : GRADS + half + 16, :].astype(F32)
+    small_out[...] = small_ref[...] + other[:8]
     low = core_ref[0] == 0
     one, two = jnp.where(low, mine, got), jnp.where(low, got, mine)
     for i in range(CHIPS):
@@ -411,61 +429,69 @@
     wide_ref,
     gain_ref,
     shift_ref,
-    w_in_ref,
+    w_in_hbm,
     b_in_ref,
-    w_out_ref,
+    w_out_hbm,
     b_out_ref,
     scr,
     turn,
+    w_in,
+    w_out,
+    sems,
 ):
     core = core_ref[0]
+    low = core == 0
+    rest = LAST - OWN
+    totals = [None, None]
     for i in range(CHIPS):
-        rows = slice(i * LAST, (i + 1) * LAST)
-        scr[core, rows, :] = mine_ref[i].astype(F32)
-        scr[1 - core, rows, :] = got_ref[i].astype(F32)
+        mine, got = mine_ref[i].astype(F32), got_ref[i].astype(F32)
+        sides = (jnp.where(low, mine, got), jnp.where(low, got, mine))
+        for c, (side, into) in enumerate(zip(sides, (w_in, turn), strict=True)):
+            for j in range(FF // 128):
+                piece = side[DATA + j * 16 : DATA + (j + 1) * 16]
+                into[i * 16 : (i + 1) * 16, j * 128 : (j + 1) * 128] = piece
+            scr[c, i * rest : i * rest + DATA, :] = side[:DATA]
+            scr[c, i * rest + DATA : (i + 1) * rest, :] = side[DATA + OWN :]
+            part = side[LAST - 8 :]
+            totals[c] = part if totals[c] is None else totals[c] + part
+    copies = [pltpu.make_async_copy(w_in, w_in_hbm, sems.at[0])]
+    copies[0].start()
+    step = FF // 2
+    for n in range(2):
+        for j in range(n * step // 128, (n + 1) * step // 128):
+            for half in range(2):
+                w_out[j * 128 : (j + 1) * 128, half * 128 : (half + 1) * 128] = turn[
+                    half * 128 : (half + 1) * 128, j * 128 : (j + 1) * 128
+                ].T
+        rows = pl.ds(n * step, step)
+        copy = pltpu.make_async_copy(w_out.at[rows], w_out_hbm.at[rows], sems.at[n + 1])
+        copy.start()
+        copies.append(copy)
     for k in range(ROWS):
         d_image = untwisted(
             [
-                scr.at[c][pl.ds(core * MSG + k * PAIRS + cp, CHIPS, stride=LAST), :]
+                scr.at[c][pl.ds(core * MSG + k * PAIRS + cp, CHIPS, stride=rest), :]
                 for cp in range(PAIRS)
                 for c in range(CORES)
             ]
         )
         out_ref[k] = (cot_ref[k].astype(F32) + d_image).astype(BF16)
-    for i in range(CHIPS):
-        for j in range(FF // 128):
-            at = i * LAST + DATA + j * 16
-            w_in_ref[i * 16 : (i + 1) * 16, j * 128 : (j + 1) * 128] = scr[0, at : at + 16, :]
-            turn[i * 16 : (i + 1) * 16, j * 128 : (j + 1) * 128] = scr[1, at : at + 16, :]
-    for half in range(2):
-        for j in range(FF // 128):
-            w_out_ref[j * 128 : (j + 1) * 128, half * 128 : (half + 1) * 128] = turn[
-                half * 128 : (half + 1) * 128, j * 128 : (j + 1) * 128
-            ].T
     for q in range(SHORT):
-        for start, is_tall in ((0, True), (20, False)):
-            taps = untwisted(
+        for start, ref in ((0, tall_ref), (20, wide_ref)):
+            ref[q] = untwisted(
                 [
-                    scr.at[c][pl.ds(DATA + OWN + start + q * PAIRS + cp, CHIPS, stride=LAST), :]
+                    scr.at[c][pl.ds(DATA + start + q * PAIRS + cp, CHIPS, stride=rest), :]
                     for cp in range(PAIRS)
                     for c in range(CORES)
                 ]
             )[7 : 7 + LONG]
-            if is_tall:
-                tall_ref[:, q, :] = taps
-            else:
-                wide_ref[q] = taps
-    total = None
-    for c in range(CORES):
-        for i in range(CHIPS):
-            at = i * LAST + LAST - 16
-            part = scr[c, at : at + 16, :]
-            total = part if total is None else total + part
     for i in range(FF // 128):
-        b_in_ref[:, i * 128 : (i + 1) * 128] = total[i : i + 1]
+        b_in_ref[:, i * 128 : (i + 1) * 128] = totals[0][i : i + 1]
     for n, ref in enumerate((gain_ref, shift_ref, b_out_ref)):
         for i in range(2):
-            ref[:, i * 128 : (i + 1) * 128] = total[8 + 2 * n + i : 9 + 2 * n + i]
+            ref[:, i * 128 : (i + 1) * 128] = totals[1][2 * n + i : 2 * n + i + 1]
+    for copy in copies:
+        copy.wait()
 
 
 def messages(x):
@@ -506,7 +532,12 @@
     packed_b = shape((STRIPS * MSG, 128), BF16)
     edge = pltpu.VMEM((H + 16, 128), F32)
 
-    image_msg = call(pack_kernel, packed_b, [packed_f])(source)
+    image_msg = call(
+        pack_kernel,
+        packed_b,
+        [pltpu.VMEM((ROWS, COLS, C), BF16), packed_f, pltpu.SemaphoreType.DMA((ROWS,))],
+        [ANY],
+    )(source)
     me = lax.axis_index("strip")
     core = (me % CORES).reshape(1)
     me = (me % CORES) * CHIPS + me // CORES
@@ -522,25 +553,35 @@
     tall, tall_flipped = taps(kernel_tall, "pqc,kc->qkp")
     wide, wide_flipped = taps(kernel_wide, "pqc,kc->pkq")
 
+    matrices = call(
+        matrix_kernel, (shape((PAIRS, SHORT * BAND, C), BF16), shape((PAIRS, SHORT * 128, 128), BF16))
+    )
+    tall_fwd, wide_fwd = matrices(tall, wide_flipped)
+    tall_bwd, wide_bwd = matrices(tall_flipped, wide)
+
     image_ch = messages(image_msg)
-    conv_ch, mixed = call(
+    conv_ch, moved, padded = call(
         forward_kernel,
-        (packed_b, shape((PAIRS, H, 128), BF16)),
+        (
+            packed_b,
+            shape((PAIRS, H, SHORT * 128), BF16),
+            shape((PAIRS, H + 2 * REACH, 128), BF16),
+        ),
         [packed_f, edge, packed_f],
-    )(image_ch, tall, wide_flipped)
+    )(image_ch, tall_fwd, wide_fwd)
     conv = messages(conv_ch)
     output, theirs, mine, left, right, small = call(
         functools.partial(mlp_kernel, scale),
         (
             shape((CELLS, C), BF16),
-            shape((GRADS + CHIPS * MSG, 128), BF16),
+            shape((GRADS + CHIPS * MSG + 16, 128), BF16),
             shape((CHIPS * MSG, 128), BF16),
             shape((2, CELLS, C), BF16),
             shape((2, CELLS, FF), BF16),
-            shape((16, 128), F32),
+            shape((8, 128), F32),
         ),
-        [packed_f, packed_f],
-        9,
+        [packed_f, packed_f, pltpu.VMEM((16, 128), F32)],
+        [SMEM] + [VMEM] * 9,
     )(
         core,
         conv,
@@ -555,17 +596,21 @@
     )
     got = between_cores(theirs)
     chip_grads = call(
-        functools.partial(own_grads_kernel, scale), shape((GRADS, 128), F32), (), 2
+        functools.partial(own_grads_kernel, scale), shape((GRADS, 128), F32), (), [SMEM] + [VMEM] * 2
     )(core, left, right)
-    merged = call(merge_kernel, shape((CHIPS, DATA + OWN, 128), BF16), (), 3)(
-        core, mine, chip_grads, got
-    )
-    d_image_msg, share = call(
+    merged, small = call(
+        merge_kernel,
+        (shape((CHIPS, DATA + OWN, 128), BF16), shape((8, 128), F32)),
+        (),
+        [SMEM] + [VMEM] * 4,
+    )(core, mine, chip_grads, small, got)
+    d_mixed, share = call(
         functools.partial(backward_kernel, scale),
-        (packed_b, shape((SHARE, 128), BF16)),
-        [packed_f, packed_f, edge, edge, packed_f, pltpu.VMEM((64, 128), F32)],
-    )(between_chips(merged), image_ch, mixed, tall_flipped, wide, small)
+        (shape((PAIRS, H, 128), BF16), shape((SHARE, 128), BF16)),
+        [packed_f, edge, pltpu.VMEM((48, 128), F32)],
+    )(between_chips(merged), padded, moved, wide_bwd, small)
     got = lax.ppermute(share, "slide", [(i, i ^ 1) for i in range(slides)])
+    d_image_msg = call(d_image_kernel, packed_b, [packed_f])(d_mixed, tall_bwd)
     half = slides // 2
     copies = call(pair_sum_kernel, shape((half, SHARE, 128), BF16))(share, got)
     groups = [[2 * i + j for i in range(half)] for j in range(2)]
@@ -577,7 +622,7 @@
         finish_kernel,
         (
             shape((ROWS, COLS, C), BF16),
-            shape((LONG, SHORT, C), F32),
+            shape((SHORT, LONG, C), F32),
             shape((SHORT, LONG, C), F32),
             shape((1, C), F32),
             shape((1, C), F32),
@@ -586,13 +631,20 @@
             shape((FF, C), F32),
             shape((1, C), F32),
         ),
-        [pltpu.VMEM((CORES, CHIPS * LAST, 128), F32), pltpu.VMEM((C, FF), F32)],
-        3,
+        [
+            pltpu.VMEM((CORES, CHIPS * (LAST - OWN), 128), F32),
+            pltpu.VMEM((C, FF), F32),
+            pltpu.VMEM((C, FF), F32),
+            pltpu.VMEM((FF, C), F32),
+            pltpu.SemaphoreType.DMA((3,)),
+        ],
+        [SMEM] + [VMEM] * 3,
+        (VMEM,) * 5 + (ANY, VMEM, ANY, VMEM),
     )(core, last, got, upstream)
     return (
         output.reshape(image.shape),
         grad_image[None],
-        g_tall,
+        jnp.transpose(g_tall, (1, 0, 2)),
         g_wide,
         g_gain[0],
         g_shift[0],

time: 148 us -> 152 us (1.027)
  blocking collectives: 62.5 us -> 46.3 us
  Pallas kernels: 15.1 us -> 22.4 us
  starting transfers between devices: 27.3 us -> 33.1 us
  waiting for transfers between devices: 38.7 us -> 42.7 us
  local copies, waits for them, and re-layouts: 1.98 us -> 4.2 us
    all_to_all x1 -> x0, blocking collectives: 21.1 us -> none  [local(): lax.all_to_all(copies, 'slide', 0, 0, axis_index_groups=groups, tiled=True)]
    all_to_all x0 -> x1, starting transfers between devices: none -> 10 us  [local(): lax.all_to_all(copies, 'slide', 0, 0, axis_index_groups=groups, tiled=True)]
    all_to_all x0 -> x1, waiting for transfers between devices: none -> 9.7 us  [local(): lax.all_to_all(copies, 'slide', 0, 0, axis_index_groups=groups, tiled=True)]
    pallas_call x5 -> x8, Pallas kernels: 11.4 us -> 18.3 us  [the longest x1 5.39 us: local(): call(functools.partial(backward_kernel, scale), (shape((PAIRS, H, 128), B...]
    all_to_all x1, blocking collectives: 25.4 us -> 30.3 us  [between_chips(): lax.all_to_all(x, 'strip', 0, 0, axis_index_groups=groups, tiled=True)]
    ppermute x2, starting transfers between devices: 10.6 us -> 6.35 us  [between_cores(): return lax.ppermute(x, 'strip', [(i, i ^ 1) for i in range(STRIPS)])]
    all_to_all x1, waiting for transfers between devices: 10.4 us -> 7.55 us  [messages(): x = lax.all_to_all(x.reshape(STRIPS, MSG, 128), 'strip', 0, 0, tiled=True)]
    all_to_all x1, waiting for transfers between devices: 21.8 us -> 18.9 us  [between_chips(): lax.all_to_all(x, 'strip', 0, 0, axis_index_groups=groups, tiled=True)]
  transfers between devices with their start and end apart: 5 -> 6, of which waited for: 5 -> 6; matrix products, arithmetic and copies ran while one was open for 1% -> 1% of each run, Pallas kernels for 0% -> 4%
where the time goes in v2:
time: 152 us; the launch traced here: 151 us
  blocking collectives  46.3 us (30%)
  waiting for transfers between devices  42.7 us (28%)
  starting transfers between devices  33.1 us (22%)
  Pallas kernels  22.4 us (15%)
  local copies, waits for them, and re-layouts  4.2 us (3%)
    all_to_all x1, blocking collectives, between_chips(): lax.all_to_all(x, 'strip', 0, 0, axis_index_groups=groups, tiled=True)  30.3 us
    all_to_all x1, waiting for transfers between devices, between_chips(): lax.all_to_all(x, 'strip', 0, 0, axis_index_groups=groups, tiled=True)  18.9 us
    all_to_all x1, blocking collectives, messages(): x = lax.all_to_all(x.reshape(STRIPS, MSG, 128), 'strip', 0, 0, tiled=True)  16 us
    all_to_all x1, starting transfers between devices, messages(): x = lax.all_to_all(x.reshape(STRIPS, MSG, 128), 'strip', 0, 0, tiled=True)  11.2 us
    all_to_all x1, starting transfers between devices, local(): lax.all_to_all(copies, 'slide', 0, 0, axis_index_groups=groups, tiled=True)  10 us
    all_to_all x1, waiting for transfers between devices, local(): lax.all_to_all(copies, 'slide', 0, 0, axis_index_groups=groups, tiled=True)  9.7 us
    all_to_all x1, waiting for transfers between devices, messages(): x = lax.all_to_all(x.reshape(STRIPS, MSG, 128), 'strip', 0, 0, tiled=True)  7.55 us
    ppermute x2, starting transfers between devices, between_cores(): return lax.ppermute(x, 'strip', [(i, i ^ 1) for i in range(STRIPS)])  6.35 us
  transfers between devices with their start and end apart: 6, of which 6 were waited for; matrix products, arithmetic and copies ran while one was open for 1% of the time, Pallas kernels for 4%

profile of v2, /device:TPU:1, one launch (start us, length us, event | category | flops | bytes accessed | tf_op | source)
XLA Modules:
  0.0 150.8 jit_solution(11390439099404946944)
XLA Ops:
  0.7 1.0 copy-done.2
  1.7 1.6 %shard_map.177 = bf16[768,128]{1,0:T(8,128)(2,1)} custom-call(bf16[6,64,256]{2,1,0:T(8,128)(2,1)S(1)} %bitcast.36), custom_call_target="tpu_custom_call" | custom-call | tf_op jit(solution)/shard_map/pallas_call | solution.py:535
  3.3 11.2 %all-to-all-start = ((bf16[32,24,128]{2,1,0:T(8,128)(2,1)}), bf16[32,24,128]{2,1,0:T(8,128)(2,1)S(1)}, u32[]{:S(2)}, u32[]{:S(2)}) async-start(bf16[32,24,128]{2,1,0:T(8,128)(2,1)} %bitcast.2), calls=%async_computation | async-start | bytes 393216 | tf_op jit(solution)/shard_map/all_to_all | solution.py:498
  14.6 0.2 convolution_bitcast_fusion
  14.7 0.1 rev.6
  14.8 1.1 convolution_bitcast_fusion.1
  15.9 2.8 %shard_map.178 = (bf16[4,320,256]{2,1,0:T(8,128)(2,1)S(1)}, bf16[4,640,128]{2,1,0:T(8,128)(2,1)S(1)}) custom-call(f32[40,128]{1,0:T(8,128)S(1)} %pad.13.tall_ref, f32[40,128]{1,0:T(8,128)S(1)} %pad.14.wide_ref), custom_call_target="tpu_custom_call" | custom-call | tf_op jit(solution)/shard_map/pallas_call | solution.py:559
  18.8 7.5 %all-to-all-done = bf16[32,24,128]{2,1,0:T(8,128)(2,1)S(1)} async-done(((bf16[32,24,128]{2,1,0:T(8,128)(2,1)}), bf16[32,24,128]{2,1,0:T(8,128)(2,1)S(1)}, u32[]{:S(2)}, u32[]{:S(2)}) %all-to-all-start) | async-done | bytes 196640 | tf_op jit(solution)/shard_map/all_to_all | solution.py:498
  26.3 1.6 %shard_map.179 = (bf16[768,128]{1,0:T(8,128)(2,1)S(1)}, bf16[4,192,640]{2,1,0:T(8,128)(2,1)S(1)}, bf16[4,256,128]{2,1,0:T(8,128)(2,1)S(1)}) custom-call(bf16[768,128]{1,0:T(8,128)(2,1)S(1)} %bitcast.38, bf16[4,320,256]{2,1,0:T(8,128)(2,1)S(1)} %get-tuple-element.36.tall_ref, bf16[4,640,128]{2,1,0:T(8,128)(2,1)S(1)} %get-tuple-element.37.wide_ref), custom_call_target="tpu_custom_call" | custom-call | tf_op jit(solution)/shard_map/pallas_call | solution.py:563
  27.9 16.0 %all_to_all.25 = bf16[32,24,128]{2,1,0:T(8,128)(2,1)S(1)} all-to-all(bf16[32,24,128]{2,1,0:T(8,128)(2,1)S(1)} %bitcast.40), channel_id=1, replica_groups=mesh['slide'=16,'strip'=32] {'strip'}, dimensions={0} | all-to-all | bytes 393216 | tf_op jit(solution)/shard_map/all_to_all | solution.py:498
  44.0 1.0 copy-done.4
  45.0 1.0 copy-done.5
  46.1 2.8 %shard_map.180 = (bf16[384,256]{1,0:T(8,128)(2,1)}, bf16[2448,128]{1,0:T(8,128)(2,1)S(1)}, bf16[384,128]{1,0:T(8,128)(2,1)S(1)}, bf16[2,384,256]{2,1,0:T(8,128)(...) custom-call(s32[1]{0:T(128)} %bitcast.core_ref, bf16[768,128]{1,0:T(8,128)(2,1)S(1)} %bitcast.39, ...), custom_call_target="tpu_custom_call" | custom-call | tf_op jit(solution)/shard_map/pallas_call | solution.py:573
  48.8 1.9 %collective-permute-start = (bf16[2448,128]{1,0:T(8,128)(2,1)S(1)}, bf16[2448,128]{1,0:T(8,128)(2,1)S(1)}, u32[]{:S(2)}, u32[]{:S(2)}) collective-permute-start(bf16[2448,128]{1,0:T(8,128)(2,1)S(1)} %get-tuple-element.44), channel_id=1, source_target_pairs={{0,1},{1,0},{2,3},{3,2},{4,5},{5,4},{6,7},{7,6},{8,9},{9,8},{10,11... | collective-permute-start | bytes 1880072 | tf_op jit(solution)/shard_map/ppermute | solution.py:508
  50.8 0.5 shard_map.181.grads_ref
  51.3 1.5 %collective-permute-done.got_ref = bf16[2448,128]{1,0:T(8,128)(2,1)S(1)} collective-permute-done((bf16[2448,128]{1,0:T(8,128)(2,1)S(1)}, bf16[2448,128]{1,0:T(8,128)(2,1)S(1)}, u32[]{:S(2)}, u32[]{:S(2)}) %collective-permute-start) | collective-permute-done | bytes 626720 | tf_op jit(solution)/shard_map/ppermute | solution.py:508
  52.8 1.0 shard_map.182
  53.8 3.6 %all-to-all-start.2 = ((bf16[16,176,128]{2,1,0:T(8,128)(2,1)}), bf16[16,176,128]{2,1,0:T(8,128)(2,1)S(1)}, u32[]{:S(2)}, u32[]{:S(2)}) async-start(bf16[16,176,128]{2,1,0:T(8,128)(2,1)} %get-tuple-element.45), calls=%async_computation.2 | async-start | bytes 1441792 | tf_op jit(solution)/shard_map/all_to_all | solution.py:504
  57.5 2.8 %shard_map.183 = (bf16[4,320,256]{2,1,0:T(8,128)(2,1)S(1)}, bf16[4,640,128]{2,1,0:T(8,128)(2,1)S(1)}) custom-call(f32[40,128]{1,0:T(8,128)S(1)} %pad.15.tall_ref, f32[40,128]{1,0:T(8,128)S(1)} %pad.16.wide_ref), custom_call_target="tpu_custom_call" | custom-call | tf_op jit(solution)/shard_map/pallas_call | solution.py:560
  60.3 18.9 %all-to-all-done.2.parts_ref = bf16[16,176,128]{2,1,0:T(8,128)(2,1)S(1)} async-done(((bf16[16,176,128]{2,1,0:T(8,128)(2,1)}), bf16[16,176,128]{2,1,0:T(8,128)(2,1)S(1)}, u32[]{:S(2)}, u32[]{:S(2)}) %all-to-all-start.2) | async-done | bytes 720928 | tf_op jit(solution)/shard_map/all_to_all | solution.py:504
  79.3 0.9 copy-done.7
  80.2 5.4 %shard_map.184 = (bf16[4,192,128]{2,1,0:T(8,128)(2,1)S(1)}, bf16[176,128]{1,0:T(8,128)(2,1)S(1)}) custom-call(bf16[16,176,128]{2,1,0:T(8,128)(2,1)S(1)} %all-to-all-done.2.parts_ref, bf16[4,256,128]{2,1,0:T(8,128)(2,1)S(1)} %copy-done.7, bf16[4,192,640]{2,1,0:T(8,128)(2,1)S(1)} %get-tuple-element.47.moved_ref, ...), custom_call_target="tpu_custom_call" | custom-call | tf_op jit(solution)/shard_map/pallas_call | solution.py:607
  85.6 1.9 %collective-permute-start.1 = (bf16[176,128]{1,0:T(8,128)(2,1)S(1)}, bf16[176,128]{1,0:T(8,128)(2,1)S(1)}, u32[]{:S(2)}, u32[]{:S(2)}) collective-permute-start(bf16[176,128]{1,0:T(8,128)(2,1)S(1)} %get-tuple-element.50.mine_ref), channel_id=1, source_target_pairs={{0,32},{32,0},{64,96},{96,64},{128,160},{160,128},{192,224},{224,1... | collective-permute-start | bytes 135176 | tf_op jit(solution)/shard_map/ppermute | solution.py:612
  87.5 2.9 %collective-permute-done.1.got_ref = bf16[176,128]{1,0:T(8,128)(2,1)S(1)} collective-permute-done((bf16[176,128]{1,0:T(8,128)(2,1)S(1)}, bf16[176,128]{1,0:T(8,128)(2,1)S(1)}, u32[]{:S(2)}, u32[]{:S(2)}) %collective-permute-start.1) | collective-permute-done | bytes 45088 | tf_op jit(solution)/shard_map/ppermute | solution.py:612
  90.4 0.8 shard_map.185
  91.1 10.0 %all-to-all-start.3 = ((bf16[8,176,128]{2,1,0:T(8,128)(2,1)}), bf16[8,176,128]{2,1,0:T(8,128)(2,1)S(1)}, u32[]{:S(2)}, u32[]{:S(2)}) async-start(bf16[8,176,128]{2,1,0:T(8,128)(2,1)} %shard_map.185), calls=%async_computation.3 | async-start | bytes 720896 | tf_op jit(solution)/shard_map/all_to_all | solution.py:617
  101.2 0.7 shard_map.186.d_image_ref
  101.8 9.7 %all-to-all-done.3.parts_ref = bf16[8,176,128]{2,1,0:T(8,128)(2,1)S(1)} async-done(((bf16[8,176,128]{2,1,0:T(8,128)(2,1)}), bf16[8,176,128]{2,1,0:T(8,128)(2,1)S(1)}, u32[]{:S(2)}, u32[]{:S(2)}) %all-to-all-start.3) | async-done | bytes 360480 | tf_op jit(solution)/shard_map/all_to_all | solution.py:617
  111.6 30.3 %all_to_all.26.mine_ref = bf16[16,224,128]{2,1,0:T(8,128)(2,1)S(1)} all-to-all(bf16[16,224,128]{2,1,0:T(8,128)(2,1)S(1)} %shard_map.187), channel_id=1, replica_groups={{0,2,4,6,8,10,12,14,16,18,20,22,24,26,28,30},{1,3,5,7,9,11,13,15,17,19,..., dimensions={0} | all-to-all | bytes 1835008 | tf_op jit(solution)/shard_map/all_to_all | solution.py:504
  142.0 4.4 %collective-permute-start.2 = (bf16[16,224,128]{2,1,0:T(8,128)(2,1)S(1)}, bf16[16,224,128]{2,1,0:T(8,128)(2,1)S(1)}, u32[]{:S(2)}, u32[]{:S(2)}) collective-permute-start(bf16[16,224,128]{2,1,0:T(8,128)(2,1)S(1)} %all_to_all.26.mine_ref), channel_id=1, source_target_pairs={{0,1},{1,0},{2,3},{3,2},{4,5},{5,4},{6,7},{7,6},{8,9},{9,8},{10,11... | collective-permute-start | bytes 2752520 | tf_op jit(solution)/shard_map/ppermute | solution.py:508
  146.4 2.1 %collective-permute-done.2.got_ref = bf16[16,224,128]{2,1,0:T(8,128)(2,1)S(1)} collective-permute-done((bf16[16,224,128]{2,1,0:T(8,128)(2,1)S(1)}, bf16[16,224,128]{2,1,0:T(8,128)(2,1)S(1)}, u32[]{:S(2)}, u32[]{:S(2)}) %collective-permute-start.2) | collective-permute-done | bytes 917536 | tf_op jit(solution)/shard_map/ppermute | solution.py:508
  148.5 2.4 %shard_map.188 = (bf16[6,64,256]{2,1,0:T(8,128)(2,1)}, f32[5,51,256]{2,1,0:T(8,128)}, f32[5,51,256]{2,1,0:T(8,128)}, f32[1,256]{1,0:T(1,128)}, f32[1,256]{1,0:T(...) custom-call(s32[1]{0:T(128)} %bitcast.core_ref, ...), custom_call_target="tpu_custom_call" | custom-call | tf_op jit(solution)/shard_map/pallas_call | solution.py:621
  (27 shorter events, 0.2 us)
Async XLA Ops:
  0.6 13.9 %copy-start = (bf16[5,51,256]{2,1,0:T(8,128)(2,1)S(1)}, bf16[5,51,256]{2,1,0:T(8,128)(2,1)}, u32[]{:S(2)}) copy-start(bf16[5,51,256]{2,1,0:T(8,128)(2,1)} %param.13) | copy-start | bytes 391684
  0.7 1.0 copy-start.2
  1.6 42.3 %copy-start.1 = (bf16[1,6,64,256]{3,2,1,0:T(8,128)(2,1)S(1)}, bf16[1,6,64,256]{3,2,1,0:T(8,128)(2,1)}, u32[]{:S(2)}) copy-start(bf16[1,6,64,256]{3,2,1,0:T(8,128)(2,1)} %param.11) | copy-start | bytes 589828
  1.6 42.3 %copy-start.3 = (bf16[1,6,64,256]{3,2,1,0:T(8,128)(2,1)S(1)}, bf16[1,6,64,256]{3,2,1,0:T(8,128)(2,1)}, u32[]{:S(2)}) copy-start(bf16[1,6,64,256]{3,2,1,0:T(8,128)(2,1)} %param.10) | copy-start | bytes 589828
  1.6 42.3 %copy-start.8 = (f32[1024]{0:T(1024)S(1)}, f32[1024]{0:T(1024)}, u32[]{:S(2)}) copy-start(f32[1024]{0:T(1024)} %param.17) | copy-start | bytes 12292
  1.6 42.3 %copy-start.9 = (f32[256]{0:T(256)S(1)}, f32[256]{0:T(256)}, u32[]{:S(2)}) copy-start(f32[256]{0:T(256)} %param.14) | copy-start | bytes 3076
  1.6 42.3 %copy-start.10 = (f32[256]{0:T(256)S(1)}, f32[256]{0:T(256)}, u32[]{:S(2)}) copy-start(f32[256]{0:T(256)} %param.15) | copy-start | bytes 3076
  1.6 42.3 %copy-start.11 = (f32[256]{0:T(256)S(1)}, f32[256]{0:T(256)}, u32[]{:S(2)}) copy-start(f32[256]{0:T(256)} %param.19) | copy-start | bytes 3076
  3.3 23.0 %all-to-all-start = ((bf16[32,24,128]{2,1,0:T(8,128)(2,1)}), bf16[32,24,128]{2,1,0:T(8,128)(2,1)S(1)}, u32[]{:S(2)}, u32[]{:S(2)}) async-start(bf16[32,24,128]{2,1,0:T(8,128)(2,1)} %bitcast.2), calls=%async_computation | async-start | bytes 393216 | tf_op jit(solution)/shard_map/all_to_all | solution.py:498
  27.9 20.9 %copy-start.6 = (bf16[4,256,128]{2,1,0:T(8,128)(2,1)}, bf16[4,256,128]{2,1,0:T(8,128)(2,1)S(1)}, u32[]{:S(2)}) copy-start(bf16[4,256,128]{2,1,0:T(8,128)(2,1)S(1)} %get-tuple-element.46.padded_ref) | copy-start | bytes 786436
  44.0 1.0 copy-start.4
  45.0 1.0 copy-start.5
  48.8 3.9 %collective-permute-start = (bf16[2448,128]{1,0:T(8,128)(2,1)S(1)}, bf16[2448,128]{1,0:T(8,128)(2,1)S(1)}, u32[]{:S(2)}, u32[]{:S(2)}) collective-permute-start(bf16[2448,128]{1,0:T(8,128)(2,1)S(1)} %get-tuple-element.44), channel_id=1, source_target_pairs={{0,1},{1,0},{2,3},{3,2},{4,5},{5,4},{6,7},{7,6},{8,9},{9,8},{10,11... | collective-permute-start | bytes 1880072 | tf_op jit(solution)/shard_map/ppermute | solution.py:508
  53.8 25.5 %all-to-all-start.2 = ((bf16[16,176,128]{2,1,0:T(8,128)(2,1)}), bf16[16,176,128]{2,1,0:T(8,128)(2,1)S(1)}, u32[]{:S(2)}, u32[]{:S(2)}) async-start(bf16[16,176,128]{2,1,0:T(8,128)(2,1)} %get-tuple-element.45), calls=%async_computation.2 | async-start | bytes 1441792 | tf_op jit(solution)/shard_map/all_to_all | solution.py:504
  79.3 1.0 copy-start.7
  85.6 4.8 %collective-permute-start.1 = (bf16[176,128]{1,0:T(8,128)(2,1)S(1)}, bf16[176,128]{1,0:T(8,128)(2,1)S(1)}, u32[]{:S(2)}, u32[]{:S(2)}) collective-permute-start(bf16[176,128]{1,0:T(8,128)(2,1)S(1)} %get-tuple-element.50.mine_ref), channel_id=1, source_target_pairs={{0,32},{32,0},{64,96},{96,64},{128,160},{160,128},{192,224},{224,1... | collective-permute-start | bytes 135176 | tf_op jit(solution)/shard_map/ppermute | solution.py:612
  91.1 20.4 %all-to-all-start.3 = ((bf16[8,176,128]{2,1,0:T(8,128)(2,1)}), bf16[8,176,128]{2,1,0:T(8,128)(2,1)S(1)}, u32[]{:S(2)}, u32[]{:S(2)}) async-start(bf16[8,176,128]{2,1,0:T(8,128)(2,1)} %shard_map.185), calls=%async_computation.3 | async-start | bytes 720896 | tf_op jit(solution)/shard_map/all_to_all | solution.py:617
  142.0 6.5 %collective-permute-start.2 = (bf16[16,224,128]{2,1,0:T(8,128)(2,1)S(1)}, bf16[16,224,128]{2,1,0:T(8,128)(2,1)S(1)}, u32[]{:S(2)}, u32[]{:S(2)}) collective-permute-start(bf16[16,224,128]{2,1,0:T(8,128)(2,1)S(1)} %all_to_all.26.mine_ref), channel_id=1, source_target_pairs={{0,1},{1,0},{2,3},{3,2},{4,5},{5,4},{6,7},{7,6},{8,9},{9,8},{10,11... | collective-permute-start | bytes 2752520 | tf_op jit(solution)/shard_map/ppermute | solution.py:508

commit v3 on v2

--- a/solution.py
+++ b/solution.py
@@ -31,12 +31,12 @@
 LAST = DATA + SHARE
 epsilon = 1e-06
 
-PARAMS = pltpu.CompilerParams(vmem_limit_bytes=48 * 1024 * 1024)
+PARAMS = pltpu.CompilerParams(vmem_limit_bytes=24 * 1024 * 1024)
 
 
 VMEM = pl.BlockSpec(memory_space=pltpu.VMEM)
 SMEM = pl.BlockSpec(memory_space=pltpu.SMEM)
-ANY = pl.BlockSpec(memory_space=pl.ANY)
+HBM = pl.BlockSpec(memory_space=pltpu.HBM)
 
 
 def call(kernel, out_shape, scratch=(), in_specs=None, out_specs=None):
@@ -147,17 +147,35 @@
     )
 
 
+def flipped(taps_ref):
+    a = lax.broadcasted_iota(jnp.int32, (128, 128), 0)
+    b = lax.broadcasted_iota(jnp.int32, (128, 128), 1)
+    turn = (a + b == LONG - 1).astype(BF16)
+    return jnp.dot(taps_ref[...].astype(BF16), turn, preferred_element_type=F32)
+
+
+def tall_matrices(taps, cp):
+    return jnp.concatenate(
+        [
+            jnp.concatenate([tall_matrix(taps, q, c2 * 4 + cp) for c2 in range(2)], axis=1)
+            for q in range(SHORT)
+        ],
+        axis=0,
+    ).astype(BF16)
+
+
+def wide_matrices(taps, cp, in_block):
+    return jnp.concatenate(
+        [wide_matrix(taps, p, cp, in_block) for p in range(SHORT)], axis=0
+    ).astype(BF16)
+
+
 def matrix_kernel(tall_ref, wide_ref, tall_out, wide_out):
     in_block = block_mask()
+    tall, wide = tall_ref[...], flipped(wide_ref)
     for cp in range(PAIRS):
-        for q in range(SHORT):
-            rows = slice(q * BAND, (q + 1) * BAND)
-            for c2 in range(2):
-                lanes = slice(c2 * 128, (c2 + 1) * 128)
-                tall_out[cp, rows, lanes] = tall_matrix(tall_ref, q, c2 * 4 + cp).astype(BF16)
-            wide_out[cp, q * 128 : (q + 1) * 128, :] = wide_matrix(
-                wide_ref, q, cp, in_block
-            ).astype(BF16)
+        tall_out[cp] = tall_matrices(tall, cp)
+        wide_out[cp] = wide_matrices(wide, cp, in_block)
 
 
 def pad_rows(x):
@@ -165,55 +183,66 @@
     return jnp.concatenate([zero, x, zero], axis=0)
 
 
-def pack_kernel(image_ref, out_ref, rows, scr, sems):
-    copies = [pltpu.make_async_copy(image_ref.at[k], rows.at[k], sems.at[k]) for k in range(ROWS)]
-    for copy in copies:
-        copy.start()
+def pack_kernel(image_ref, out_ref, scr):
     for k in range(ROWS):
-        copies[k].wait()
-        put_by_strip(rows[k].astype(F32), k, scr)
+        put_by_strip(image_ref[k].astype(F32), k, scr)
     out_ref[...] = scr[...].astype(BF16)
 
 
-def forward_kernel(image_ref, tall_ref, wide_ref, conv_ref, moved_ref, padded_ref, scr, pad, out):
+def forward_kernel(image_ref, tall_ref, wide_ref, conv_ref, mixed_ref, padded_ref, scr, pad, out):
     scr[...] = image_ref[...].astype(F32)
     pad[0:8, :] = jnp.zeros((8, 128), F32)
     pad[H + 8 : H + 16, :] = jnp.zeros((8, 128), F32)
     for cp in range(PAIRS):
         padded = pad_rows(scr[pl.ds(cp, H, stride=PAIRS), :].astype(BF16))
         padded_ref[cp] = padded
-        pad[8 : H + 8, :] = tall_conv(padded, tall_ref[cp], 1).astype(BF16).astype(F32)
-        moved = moved_rows(pad, 1)
-        moved_ref[cp] = moved
+        mixed = tall_conv(padded, tall_ref[cp], 1).astype(BF16)
+        mixed_ref[cp] = mixed
+        pad[8 : H + 8, :] = mixed.astype(F32)
         out[pl.ds(cp, H, stride=PAIRS), :] = jnp.dot(
-            moved, wide_ref[cp], preferred_element_type=F32
+            moved_rows(pad, 1), wide_ref[cp], preferred_element_type=F32
         )
     conv_ref[...] = out[...].astype(BF16)
 
 
-def diagonal(x, offset):
+def beside_kernel(padded_ref, wide_ref, shifted_ref, wide_out):
+    in_block = block_mask()
+    wide = wide_ref[...]
+    for cp in range(PAIRS):
+        padded = padded_ref[cp].astype(F32)
+        for q in range(SHORT):
+            shifted_ref[cp, q] = shifted(padded, q - 2).astype(BF16)
+        wide_out[cp] = wide_matrices(wide, cp, in_block)
+
+
+def fold(x, offset):
     total = None
     for i in range(0, x.shape[0], 8):
         part = pltpu.roll(x[i : i + 8], (offset - i) % 128, 1)
         total = part if total is None else total + part
-    row = lax.broadcasted_iota(jnp.int32, (8, 128), 0)
-    for bit in (1, 2, 4):
-        total = jnp.where(row & bit != 0, pltpu.roll(total, 128 - bit, 1), total)
-    return jnp.sum(total, axis=0, keepdims=True)
+    return total
+
+
+def diagonal_sums(folds, count):
+    total = folds[pl.ds(0, count, stride=8), :]
+    for i in range(1, 8):
+        total = total + pltpu.roll(folds[pl.ds(i, count, stride=8), :], 128 - i, 1)
+    return total
 
 
 def backward_kernel(
     scale,
     parts_ref,
-    padded_ref,
-    moved_ref,
+    shifted_ref,
+    mixed_ref,
     wide_ref,
     small_ref,
     d_mixed_ref,
     share_ref,
     d_scr,
     d_pad,
-    g_scr,
+    m_pad,
+    folds,
 ):
     total = None
     for i in range(CHIPS):
@@ -221,59 +250,73 @@
         d_scr[i * DATA : (i + 1) * DATA, :] = part[:DATA]
         total = part[DATA:] if total is None else total + part[DATA:]
     share_ref[0:OWN, :] = total.astype(BF16)
-    in_block = block_mask()
-    d_pad[0:8, :] = jnp.zeros((8, 128), F32)
-    d_pad[H + 8 : H + 16, :] = jnp.zeros((8, 128), F32)
-    g_scr[40:48, :] = small_ref[...]
-    lane, first = half_masks((1, 128))
-    lane_b, first_b = half_masks((BAND, 128))
+    for ref in (d_pad, m_pad):
+        ref[0:8, :] = jnp.zeros((8, 128), F32)
+        ref[H + 8 : H + 16, :] = jnp.zeros((8, 128), F32)
+    row = lax.broadcasted_iota(jnp.int32, (BAND, 128), 0)
+    lane = lax.broadcasted_iota(jnp.int32, (BAND, 128), 1)
+    half = (LONG - 1) // 2
+    low_band = (lane - row >= 7) & (lane - row <= 57)
+    near = jnp.abs(lane % COLS - row) <= half
+    low_near = near & (lane < COLS)
+    high_near = near & (lane >= COLS)
+    first = lax.broadcasted_iota(jnp.int32, (H, 128), 1) < COLS
+    zero = jnp.zeros((H, 128), BF16)
     for cp in range(PAIRS):
         d_conv = d_scr[pl.ds(cp, H, stride=PAIRS), :]
         d_pad[8 : H + 8, :] = d_conv
+        m_pad[8 : H + 8, :] = mixed_ref[cp].astype(F32)
         d_mixed = jnp.dot(
             moved_rows(d_pad, -1), wide_ref[cp], preferred_element_type=F32
         ).astype(BF16)
         d_mixed_ref[cp] = d_mixed
         corr = lax.dot_general(
-            d_conv.astype(BF16), moved_ref[cp], (((0,), (0,)), ((), ())), preferred_element_type=F32
+            d_conv.astype(BF16),
+            moved_rows(m_pad, 1),
+            (((0,), (0,)), ((), ())),
+            preferred_element_type=F32,
         )
         for p in range(SHORT):
-            part = jnp.where(in_block, corr[:, p * 128 : (p + 1) * 128], 0.0)
-            low = diagonal(part[:COLS], 32)
-            high = diagonal(part[COLS:], 32)
-            row = 20 + p * PAIRS + cp
-            g_scr[row : row + 1, :] = jnp.where(first, low, high) * scale
-        parts = []
-        d_mixed_f = d_mixed.astype(F32)
+            part = corr[:, p * 128 : (p + 1) * 128]
+            part = jnp.where(low_near, part[:COLS], jnp.where(high_near, part[COLS:], 0.0))
+            at = (20 + p * PAIRS + cp) * 8
+            folds[at : at + 8, :] = fold(part, 7 + half)
+        sides = []
+        for c2 in range(2):
+            own = jnp.where(first, d_mixed, zero) if c2 == 0 else jnp.where(first, zero, d_mixed)
+            own = jnp.concatenate([own[b * BAND : (b + 1) * BAND] for b in range(H // BAND)], axis=1)
+            windows = jnp.concatenate(
+                [
+                    jnp.concatenate(
+                        [
+                            shifted_ref[cp, q, b * BAND + at : b * BAND + at + BAND, :]
+                            for b in range(H // BAND)
+                        ],
+                        axis=1,
+                    )
+                    for q in range(SHORT)
+                    for at in ((0, BAND) if c2 == 0 else (BAND, 0))
+                ],
+                axis=0,
+            )
+            sides.append(
+                lax.dot_general(
+                    own, windows, (((1,), (1,)), ((), ())), preferred_element_type=F32
+                )
+            )
         for q in range(SHORT):
-            parts.append(shifted(d_mixed_f, 2 - q))
-        left = []
-        for c2 in range(2):
-            for q in range(SHORT):
-                bands = []
-                for b in range(H // BAND):
-                    band = parts[q][b * BAND : (b + 1) * BAND]
-                    bands.append(jnp.where(first_b == (c2 == 0), band, 0.0))
-                left.append(jnp.concatenate(bands, axis=1))
-        left = jnp.concatenate(left, axis=0).astype(BF16)
-        right = jnp.concatenate(
-            [padded_ref[cp, b * BAND : b * BAND + 128, :] for b in range(H // BAND)], axis=1
-        )
-        corr = lax.dot_general(
-            left, right, (((1,), (1,)), ((), ())), preferred_element_type=F32
-        )
-        for q in range(SHORT):
-            low = diagonal(corr[q * BAND : (q + 1) * BAND], 0)
-            high = diagonal(corr[(SHORT + q) * BAND : (SHORT + q + 1) * BAND], COLS)
-            row = q * PAIRS + cp
-            g_scr[row : row + 1, :] = jnp.where(first, low, high) * scale
-    share_ref[OWN:SHARE, :] = g_scr[...].astype(BF16)
+            low, high = (side[:, q * 128 : (q + 1) * 128] for side in sides)
+            at = (q * PAIRS + cp) * 8
+            folds[at : at + 8, :] = fold(jnp.where(low_band, low, high), 0)
+    grads = diagonal_sums(folds, 40) * scale
+    share_ref[OWN:SHARE, :] = jnp.concatenate([grads, small_ref[...]], axis=0).astype(BF16)
 
 
 def d_image_kernel(d_mixed_ref, tall_ref, d_image_ref, out):
+    taps = flipped(tall_ref)
     for cp in range(PAIRS):
         out[pl.ds(cp, H, stride=PAIRS), :] = tall_conv(
-            pad_rows(d_mixed_ref[cp]), tall_ref[cp], -1
+            pad_rows(d_mixed_ref[cp]), tall_matrices(taps, cp), -1
         )
     d_image_ref[...] = out[...].astype(BF16)
 
@@ -535,8 +578,7 @@
     image_msg = call(
         pack_kernel,
         packed_b,
-        [pltpu.VMEM((ROWS, COLS, C), BF16), packed_f, pltpu.SemaphoreType.DMA((ROWS,))],
-        [ANY],
+        [packed_f],
     )(source)
     me = lax.axis_index("strip")
     core = (me % CORES).reshape(1)
@@ -547,24 +589,20 @@
     def taps(kernel, spec):
         picked = jnp.einsum(spec, kernel, own, preferred_element_type=F32)
         picked = picked.reshape(SHORT * 8, LONG)
-        pad = ((0, 0), (0, 128 - LONG))
-        return jnp.pad(picked, pad), jnp.pad(picked[:, ::-1], pad)
-
-    tall, tall_flipped = taps(kernel_tall, "pqc,kc->qkp")
-    wide, wide_flipped = taps(kernel_wide, "pqc,kc->pkq")
-
-    matrices = call(
+        return jnp.pad(picked, ((0, 0), (0, 128 - LONG)))
+
+    tall = taps(kernel_tall, "pqc,kc->qkp")
+    wide = taps(kernel_wide, "pqc,kc->pkq")
+    tall_fwd, wide_fwd = call(
         matrix_kernel, (shape((PAIRS, SHORT * BAND, C), BF16), shape((PAIRS, SHORT * 128, 128), BF16))
-    )
-    tall_fwd, wide_fwd = matrices(tall, wide_flipped)
-    tall_bwd, wide_bwd = matrices(tall_flipped, wide)
+    )(tall, wide)
 
     image_ch = messages(image_msg)
-    conv_ch, moved, padded = call(
+    conv_ch, mixed, padded = call(
         forward_kernel,
         (
             packed_b,
-            shape((PAIRS, H, SHORT * 128), BF16),
+            shape((PAIRS, H, 128), BF16),
             shape((PAIRS, H + 2 * REACH, 128), BF16),
         ),
         [packed_f, edge, packed_f],
@@ -604,13 +642,17 @@
         (),
         [SMEM] + [VMEM] * 4,
     )(core, mine, chip_grads, small, got)
+    shifts, wide_bwd = call(
+        beside_kernel,
+        (shape((PAIRS, SHORT, H + 2 * REACH, 128), BF16), shape((PAIRS, SHORT * 128, 128), BF16)),
+    )(padded, wide)
     d_mixed, share = call(
         functools.partial(backward_kernel, scale),
         (shape((PAIRS, H, 128), BF16), shape((SHARE, 128), BF16)),
-        [packed_f, edge, pltpu.VMEM((48, 128), F32)],
-    )(between_chips(merged), padded, moved, wide_bwd, small)
+        [packed_f, edge, edge, pltpu.VMEM((40 * 8, 128), F32)],
+    )(between_chips(merged), shifts, mixed, wide_bwd, small)
     got = lax.ppermute(share, "slide", [(i, i ^ 1) for i in range(slides)])
-    d_image_msg = call(d_image_kernel, packed_b, [packed_f])(d_mixed, tall_bwd)
+    d_image_msg = call(d_image_kernel, packed_b, [packed_f])(d_mixed, tall)
     half = slides // 2
     copies = call(pair_sum_kernel, shape((half, SHARE, 128), BF16))(share, got)
     groups = [[2 * i + j for i in range(half)] for j in range(2)]
@@ -639,7 +681,7 @@
             pltpu.SemaphoreType.DMA((3,)),
         ],
         [SMEM] + [VMEM] * 3,
-        (VMEM,) * 5 + (ANY, VMEM, ANY, VMEM),
+        (VMEM,) * 5 + (HBM, VMEM, HBM, VMEM),
     )(core, last, got, upstream)
     return (
         output.reshape(image.shape),

time: 152 us -> 145 us (0.954)
  Pallas kernels: 22.4 us -> 17.5 us
  local copies, waits for them, and re-layouts: 4.2 us -> 1.69 us
    pallas_call x1, Pallas kernels: 5.39 us -> 2.26 us  [local(): call(functools.partial(backward_kernel, scale), (shape((PAIRS, H, 128), B...]
    unnamed x24 -> x28, local copies, waits for them, and re-layouts: 4.02 us -> 1.68 us
    pallas_call x5, Pallas kernels: 9.52 us -> 7.71 us  [the longest x1 2.34 us: local(): call(matrix_kernel, (shape((PAIRS, SHORT * BAND, C), BF16), shape((PAIRS,...]
where the time goes in v3:
time: 145 us
  blocking collectives  46.3 us (32%)
  waiting for transfers between devices  43.9 us (30%)
  starting transfers between devices  33.1 us (23%)
  Pallas kernels  17.5 us (12%)
  local copies, waits for them, and re-layouts  1.69 us (1%)
    all_to_all x1, blocking collectives, between_chips(): lax.all_to_all(x, 'strip', 0, 0, axis_index_groups=groups, tiled=True)  30.3 us
    all_to_all x1, waiting for transfers between devices, between_chips(): lax.all_to_all(x, 'strip', 0, 0, axis_index_groups=groups, tiled=True)  20 us
    all_to_all x1, blocking collectives, messages(): x = lax.all_to_all(x.reshape(STRIPS, MSG, 128), 'strip', 0, 0, tiled=True)  16 us
    all_to_all x1, starting transfers between devices, messages(): x = lax.all_to_all(x.reshape(STRIPS, MSG, 128), 'strip', 0, 0, tiled=True)  11.2 us
    all_to_all x1, starting transfers between devices, local(): lax.all_to_all(copies, 'slide', 0, 0, axis_index_groups=groups, tiled=True)  10.1 us
    all_to_all x1, waiting for transfers between devices, local(): lax.all_to_all(copies, 'slide', 0, 0, axis_index_groups=groups, tiled=True)  9.34 us
    all_to_all x1, waiting for transfers between devices, messages(): x = lax.all_to_all(x.reshape(STRIPS, MSG, 128), 'strip', 0, 0, tiled=True)  8.12 us
    ppermute x2, starting transfers between devices, between_cores(): return lax.ppermute(x, 'strip', [(i, i ^ 1) for i in range(STRIPS)])  6.35 us
  transfers between devices with their start and end apart: 6, of which 6 were waited for; matrix products, arithmetic and copies ran while one was open for 1% of the time, Pallas kernels for 4%

profile of v3, /device:TPU:1, one launch (start us, length us, event | category | flops | bytes accessed | tf_op | source)
XLA Modules:
  0.0 144.6 jit_solution(10068202931685591406)
XLA Ops:
  0.6 0.0 copy-start
  0.7 1.0 copy-done.2
  1.7 0.9 shard_map.177
  2.6 11.2 %all-to-all-start = ((bf16[32,24,128]{2,1,0:T(8,128)(2,1)}), bf16[32,24,128]{2,1,0:T(8,128)(2,1)S(1)}, u32[]{:S(2)}, u32[]{:S(2)}) async-start(bf16[32,24,128]{2,1,0:T(8,128)(2,1)} %bitcast.2), calls=%async_computation | async-start | bytes 393216 | tf_op jit(solution)/shard_map/all_to_all | solution.py:541
  13.8 0.2 convolution_bitcast_fusion.1
  14.0 1.1 convolution_bitcast_fusion
  15.1 2.3 %shard_map.178 = (bf16[4,320,256]{2,1,0:T(8,128)(2,1)S(1)}, bf16[4,640,128]{2,1,0:T(8,128)(2,1)S(1)}) custom-call(f32[40,128]{1,0:T(8,128)S(1)} %pad.7.tall_ref, f32[40,128]{1,0:T(8,128)S(1)} %pad.8.wide_ref), custom_call_target="tpu_custom_call" | custom-call | tf_op jit(solution)/shard_map/pallas_call | solution.py:596
  17.5 8.1 %all-to-all-done = bf16[32,24,128]{2,1,0:T(8,128)(2,1)S(1)} async-done(((bf16[32,24,128]{2,1,0:T(8,128)(2,1)}), bf16[32,24,128]{2,1,0:T(8,128)(2,1)S(1)}, u32[]{:S(2)}, u32[]{:S(2)}) %all-to-all-start) | async-done | bytes 196640 | tf_op jit(solution)/shard_map/all_to_all | solution.py:541
  25.6 1.6 %shard_map.179 = (bf16[768,128]{1,0:T(8,128)(2,1)S(1)}, bf16[4,192,128]{2,1,0:T(8,128)(2,1)S(1)}, bf16[4,256,128]{2,1,0:T(8,128)(2,1)S(1)}) custom-call(bf16[768,128]{1,0:T(8,128)(2,1)S(1)} %bitcast.38, bf16[4,320,256]{2,1,0:T(8,128)(2,1)S(1)} %get-tuple-element.36.tall_ref, bf16[4,640,128]{2,1,0:T(8,128)(2,1)S(1)} %get-tuple-element.37.wide_ref), custom_call_target="tpu_custom_call" | custom-call | tf_op jit(solution)/shard_map/pallas_call | solution.py:601
  27.2 0.0 copy-start.8
  27.2 0.7 copy-done.8
  27.9 16.0 %all_to_all.25 = bf16[32,24,128]{2,1,0:T(8,128)(2,1)S(1)} all-to-all(bf16[32,24,128]{2,1,0:T(8,128)(2,1)S(1)} %bitcast.40), channel_id=1, replica_groups=mesh['slide'=16,'strip'=32] {'strip'}, dimensions={0} | all-to-all | bytes 393216 | tf_op jit(solution)/shard_map/all_to_all | solution.py:541
  43.9 2.8 %shard_map.180 = (bf16[384,256]{1,0:T(8,128)(2,1)}, bf16[2448,128]{1,0:T(8,128)(2,1)S(1)}, bf16[384,128]{1,0:T(8,128)(2,1)S(1)}, bf16[2,384,256]{2,1,0:T(8,128)(...) custom-call(s32[1]{0:T(128)} %bitcast.core_ref, bf16[768,128]{1,0:T(8,128)(2,1)S(1)} %bitcast.39, ...), custom_call_target="tpu_custom_call" | custom-call | tf_op jit(solution)/shard_map/pallas_call | solution.py:611
  46.7 1.9 %collective-permute-start = (bf16[2448,128]{1,0:T(8,128)(2,1)S(1)}, bf16[2448,128]{1,0:T(8,128)(2,1)S(1)}, u32[]{:S(2)}, u32[]{:S(2)}) collective-permute-start(bf16[2448,128]{1,0:T(8,128)(2,1)S(1)} %get-tuple-element.44), channel_id=1, source_target_pairs={{0,1},{1,0},{2,3},{3,2},{4,5},{5,4},{6,7},{7,6},{8,9},{9,8},{10,11... | collective-permute-start | bytes 1880072 | tf_op jit(solution)/shard_map/ppermute | solution.py:551
  48.7 0.5 shard_map.181.grads_ref
  49.1 1.5 %collective-permute-done.got_ref = bf16[2448,128]{1,0:T(8,128)(2,1)S(1)} collective-permute-done((bf16[2448,128]{1,0:T(8,128)(2,1)S(1)}, bf16[2448,128]{1,0:T(8,128)(2,1)S(1)}, u32[]{:S(2)}, u32[]{:S(2)}) %collective-permute-start) | collective-permute-done | bytes 626720 | tf_op jit(solution)/shard_map/ppermute | solution.py:551
  50.7 1.0 shard_map.182
  51.7 3.6 %all-to-all-start.2 = ((bf16[16,176,128]{2,1,0:T(8,128)(2,1)}), bf16[16,176,128]{2,1,0:T(8,128)(2,1)S(1)}, u32[]{:S(2)}, u32[]{:S(2)}) async-start(bf16[16,176,128]{2,1,0:T(8,128)(2,1)} %get-tuple-element.45), calls=%async_computation.2 | async-start | bytes 1441792 | tf_op jit(solution)/shard_map/all_to_all | solution.py:547
  55.3 1.9 %shard_map.183 = (bf16[4,5,256,128]{3,2,1,0:T(8,128)(2,1)S(1)}, bf16[4,640,128]{2,1,0:T(8,128)(2,1)S(1)}) custom-call(bf16[4,256,128]{2,1,0:T(8,128)(2,1)S(1)} %copy-done.7, f32[40,128]{1,0:T(8,128)S(1)} %pad.8.wide_ref), custom_call_target="tpu_custom_call" | custom-call | tf_op jit(solution)/shard_map/pallas_call | solution.py:645
  57.2 20.0 %all-to-all-done.2.parts_ref = bf16[16,176,128]{2,1,0:T(8,128)(2,1)S(1)} async-done(((bf16[16,176,128]{2,1,0:T(8,128)(2,1)}), bf16[16,176,128]{2,1,0:T(8,128)(2,1)S(1)}, u32[]{:S(2)}, u32[]{:S(2)}) %all-to-all-start.2) | async-done | bytes 720928 | tf_op jit(solution)/shard_map/all_to_all | solution.py:547
  77.1 2.3 %shard_map.184 = (bf16[4,192,128]{2,1,0:T(8,128)(2,1)S(1)}, bf16[176,128]{1,0:T(8,128)(2,1)S(1)}) custom-call(bf16[16,176,128]{2,1,0:T(8,128)(2,1)S(1)} %all-to-all-done.2.parts_ref, bf16[4,5,256,128]{3,2,1,0:T(8,128)(2,1)S(1)} %get-tuple-element.47.shifted_ref, bf16[4,192,128]{2,1,0:T(8,128)(2,1)S(1)} %copy-done.9, ...), custom_call_target="tpu_custom_call" | custom-call | tf_op jit(solution)/shard_map/pallas_call | solution.py:649
  79.4 1.9 %collective-permute-start.1 = (bf16[176,128]{1,0:T(8,128)(2,1)S(1)}, bf16[176,128]{1,0:T(8,128)(2,1)S(1)}, u32[]{:S(2)}, u32[]{:S(2)}) collective-permute-start(bf16[176,128]{1,0:T(8,128)(2,1)S(1)} %get-tuple-element.51.mine_ref), channel_id=1, source_target_pairs={{0,32},{32,0},{64,96},{96,64},{128,160},{160,128},{192,224},{224,1... | collective-permute-start | bytes 135176 | tf_op jit(solution)/shard_map/ppermute | solution.py:654
  81.3 2.9 %collective-permute-done.1.got_ref = bf16[176,128]{1,0:T(8,128)(2,1)S(1)} collective-permute-done((bf16[176,128]{1,0:T(8,128)(2,1)S(1)}, bf16[176,128]{1,0:T(8,128)(2,1)S(1)}, u32[]{:S(2)}, u32[]{:S(2)}) %collective-permute-start.1) | collective-permute-done | bytes 45088 | tf_op jit(solution)/shard_map/ppermute | solution.py:654
  84.2 0.8 shard_map.185
  84.9 10.1 %all-to-all-start.3 = ((bf16[8,176,128]{2,1,0:T(8,128)(2,1)}), bf16[8,176,128]{2,1,0:T(8,128)(2,1)S(1)}, u32[]{:S(2)}, u32[]{:S(2)}) async-start(bf16[8,176,128]{2,1,0:T(8,128)(2,1)} %shard_map.185), calls=%async_computation.3 | async-start | bytes 720896 | tf_op jit(solution)/shard_map/all_to_all | solution.py:659
  95.0 1.0 shard_map.186.d_image_ref
  96.0 9.3 %all-to-all-done.3.parts_ref = bf16[8,176,128]{2,1,0:T(8,128)(2,1)S(1)} async-done(((bf16[8,176,128]{2,1,0:T(8,128)(2,1)}), bf16[8,176,128]{2,1,0:T(8,128)(2,1)S(1)}, u32[]{:S(2)}, u32[]{:S(2)}) %all-to-all-start.3) | async-done | bytes 360480 | tf_op jit(solution)/shard_map/all_to_all | solution.py:659
  105.3 0.1 shard_map.187
  105.4 30.3 %all_to_all.26.mine_ref = bf16[16,224,128]{2,1,0:T(8,128)(2,1)S(1)} all-to-all(bf16[16,224,128]{2,1,0:T(8,128)(2,1)S(1)} %shard_map.187), channel_id=1, replica_groups={{0,2,4,6,8,10,12,14,16,18,20,22,24,26,28,30},{1,3,5,7,9,11,13,15,17,19,..., dimensions={0} | all-to-all | bytes 1835008 | tf_op jit(solution)/shard_map/all_to_all | solution.py:547
  135.8 4.4 %collective-permute-start.2 = (bf16[16,224,128]{2,1,0:T(8,128)(2,1)S(1)}, bf16[16,224,128]{2,1,0:T(8,128)(2,1)S(1)}, u32[]{:S(2)}, u32[]{:S(2)}) collective-permute-start(bf16[16,224,128]{2,1,0:T(8,128)(2,1)S(1)} %all_to_all.26.mine_ref), channel_id=1, source_target_pairs={{0,1},{1,0},{2,3},{3,2},{4,5},{5,4},{6,7},{7,6},{8,9},{9,8},{10,11... | collective-permute-start | bytes 2752520 | tf_op jit(solution)/shard_map/ppermute | solution.py:551
  140.2 2.1 %collective-permute-done.2.got_ref = bf16[16,224,128]{2,1,0:T(8,128)(2,1)S(1)} collective-permute-done((bf16[16,224,128]{2,1,0:T(8,128)(2,1)S(1)}, bf16[16,224,128]{2,1,0:T(8,128)(2,1)S(1)}, u32[]{:S(2)}, u32[]{:S(2)}) %collective-permute-start.2) | collective-permute-done | bytes 917536 | tf_op jit(solution)/shard_map/ppermute | solution.py:551
  142.3 2.4 %shard_map.188 = (bf16[6,64,256]{2,1,0:T(8,128)(2,1)}, f32[5,51,256]{2,1,0:T(8,128)}, f32[5,51,256]{2,1,0:T(8,128)}, f32[1,256]{1,0:T(1,128)}, f32[1,256]{1,0:T(...) custom-call(s32[1]{0:T(128)} %bitcast.core_ref, ...), custom_call_target="tpu_custom_call" | custom-call | tf_op jit(solution)/shard_map/pallas_call | solution.py:663
  (27 shorter events, 0.1 us)
Async XLA Ops:
  0.6 13.2 %copy-start = (bf16[51,5,256]{2,0,1:T(8,128)(2,1)S(1)}, bf16[51,5,256]{2,0,1:T(8,128)(2,1)}, u32[]{:S(2)}) copy-start(bf16[51,5,256]{2,0,1:T(8,128)(2,1)} %param.12) | copy-start | bytes 391684
  0.7 1.0 copy-start.2
  1.6 42.2 %copy-start.1 = (bf16[1,6,64,256]{3,2,1,0:T(8,128)(2,1)S(1)}, bf16[1,6,64,256]{3,2,1,0:T(8,128)(2,1)}, u32[]{:S(2)}) copy-start(bf16[1,6,64,256]{3,2,1,0:T(8,128)(2,1)} %param.11) | copy-start | bytes 589828
  1.6 42.2 %copy-start.3 = (bf16[1,6,64,256]{3,2,1,0:T(8,128)(2,1)S(1)}, bf16[1,6,64,256]{3,2,1,0:T(8,128)(2,1)}, u32[]{:S(2)}) copy-start(bf16[1,6,64,256]{3,2,1,0:T(8,128)(2,1)} %param.10) | copy-start | bytes 589828
  1.6 42.2 %copy-start.4 = (bf16[256,1024]{1,0:T(8,128)(2,1)S(1)}, bf16[256,1024]{1,0:T(8,128)(2,1)}, u32[]{:S(2)}) copy-start(bf16[256,1024]{1,0:T(8,128)(2,1)} %w_in_ref.1) | copy-start | bytes 1572868
  1.6 42.2 %copy-start.5 = (bf16[1024,256]{1,0:T(8,128)(2,1)S(1)}, bf16[1024,256]{1,0:T(8,128)(2,1)}, u32[]{:S(2)}) copy-start(bf16[1024,256]{1,0:T(8,128)(2,1)} %w_out_ref.1) | copy-start | bytes 1572868
  1.6 42.2 %copy-start.10 = (f32[1024]{0:T(1024)S(1)}, f32[1024]{0:T(1024)}, u32[]{:S(2)}) copy-start(f32[1024]{0:T(1024)} %param.17) | copy-start | bytes 12292
  1.6 42.2 %copy-start.11 = (f32[256]{0:T(256)S(1)}, f32[256]{0:T(256)}, u32[]{:S(2)}) copy-start(f32[256]{0:T(256)} %param.14) | copy-start | bytes 3076
  1.7 42.2 %copy-start.12 = (f32[256]{0:T(256)S(1)}, f32[256]{0:T(256)}, u32[]{:S(2)}) copy-start(f32[256]{0:T(256)} %param.15) | copy-start | bytes 3076
  1.7 42.2 %copy-start.13 = (f32[256]{0:T(256)S(1)}, f32[256]{0:T(256)}, u32[]{:S(2)}) copy-start(f32[256]{0:T(256)} %param.19) | copy-start | bytes 3076
  2.6 23.0 %all-to-all-start = ((bf16[32,24,128]{2,1,0:T(8,128)(2,1)}), bf16[32,24,128]{2,1,0:T(8,128)(2,1)S(1)}, u32[]{:S(2)}, u32[]{:S(2)}) async-start(bf16[32,24,128]{2,1,0:T(8,128)(2,1)} %bitcast.2), calls=%async_computation | async-start | bytes 393216 | tf_op jit(solution)/shard_map/all_to_all | solution.py:541
  27.2 0.7 copy-start.8
  27.9 21.3 %copy-start.6 = (bf16[4,256,128]{2,1,0:T(8,128)(2,1)}, bf16[4,256,128]{2,1,0:T(8,128)(2,1)S(1)}, u32[]{:S(2)}) copy-start(bf16[4,256,128]{2,1,0:T(8,128)(2,1)S(1)} %get-tuple-element.46.padded_ref) | copy-start | bytes 786436
  46.7 3.9 %collective-permute-start = (bf16[2448,128]{1,0:T(8,128)(2,1)S(1)}, bf16[2448,128]{1,0:T(8,128)(2,1)S(1)}, u32[]{:S(2)}, u32[]{:S(2)}) collective-permute-start(bf16[2448,128]{1,0:T(8,128)(2,1)S(1)} %get-tuple-element.44), channel_id=1, source_target_pairs={{0,1},{1,0},{2,3},{3,2},{4,5},{5,4},{6,7},{7,6},{8,9},{9,8},{10,11... | collective-permute-start | bytes 1880072 | tf_op jit(solution)/shard_map/ppermute | solution.py:551
  50.7 4.6 %copy-start.7 = (bf16[4,256,128]{2,1,0:T(8,128)(2,1)S(1)}, bf16[4,256,128]{2,1,0:T(8,128)(2,1)}, u32[]{:S(2)}) copy-start(bf16[4,256,128]{2,1,0:T(8,128)(2,1)} %copy-done.6) | copy-start | bytes 786436
  50.7 26.5 %copy-start.9 = (bf16[4,192,128]{2,1,0:T(8,128)(2,1)S(1)}, bf16[4,192,128]{2,1,0:T(8,128)(2,1)}, u32[]{:S(2)}) copy-start(bf16[4,192,128]{2,1,0:T(8,128)(2,1)} %copy-done.8) | copy-start | bytes 589828
  51.7 25.5 %all-to-all-start.2 = ((bf16[16,176,128]{2,1,0:T(8,128)(2,1)}), bf16[16,176,128]{2,1,0:T(8,128)(2,1)S(1)}, u32[]{:S(2)}, u32[]{:S(2)}) async-start(bf16[16,176,128]{2,1,0:T(8,128)(2,1)} %get-tuple-element.45), calls=%async_computation.2 | async-start | bytes 1441792 | tf_op jit(solution)/shard_map/all_to_all | solution.py:547
  79.4 4.8 %collective-permute-start.1 = (bf16[176,128]{1,0:T(8,128)(2,1)S(1)}, bf16[176,128]{1,0:T(8,128)(2,1)S(1)}, u32[]{:S(2)}, u32[]{:S(2)}) collective-permute-start(bf16[176,128]{1,0:T(8,128)(2,1)S(1)} %get-tuple-element.51.mine_ref), channel_id=1, source_target_pairs={{0,32},{32,0},{64,96},{96,64},{128,160},{160,128},{192,224},{224,1... | collective-permute-start | bytes 135176 | tf_op jit(solution)/shard_map/ppermute | solution.py:654
  84.9 20.4 %all-to-all-start.3 = ((bf16[8,176,128]{2,1,0:T(8,128)(2,1)}), bf16[8,176,128]{2,1,0:T(8,128)(2,1)S(1)}, u32[]{:S(2)}, u32[]{:S(2)}) async-start(bf16[8,176,128]{2,1,0:T(8,128)(2,1)} %shard_map.185), calls=%async_computation.3 | async-start | bytes 720896 | tf_op jit(solution)/shard_map/all_to_all | solution.py:659
  135.8 6.5 %collective-permute-start.2 = (bf16[16,224,128]{2,1,0:T(8,128)(2,1)S(1)}, bf16[16,224,128]{2,1,0:T(8,128)(2,1)S(1)}, u32[]{:S(2)}, u32[]{:S(2)}) collective-permute-start(bf16[16,224,128]{2,1,0:T(8,128)(2,1)S(1)} %all_to_all.26.mine_ref), channel_id=1, source_target_pairs={{0,1},{1,0},{2,3},{3,2},{4,5},{5,4},{6,7},{7,6},{8,9},{9,8},{10,11... | collective-permute-start | bytes 2752520 | tf_op jit(solution)/shard_map/ppermute | solution.py:551

commit v4 on v3

--- a/solution.py
+++ b/solution.py
@@ -185,17 +185,16 @@
 
 def pack_kernel(image_ref, out_ref, scr):
     for k in range(ROWS):
-        put_by_strip(image_ref[k].astype(F32), k, scr)
+        put_by_strip(image_ref[0, k].astype(F32), k, scr)
     out_ref[...] = scr[...].astype(BF16)
 
 
-def forward_kernel(image_ref, tall_ref, wide_ref, conv_ref, mixed_ref, padded_ref, scr, pad, out):
+def forward_kernel(image_ref, tall_ref, wide_ref, conv_ref, mixed_ref, scr, pad, out):
     scr[...] = image_ref[...].astype(F32)
     pad[0:8, :] = jnp.zeros((8, 128), F32)
     pad[H + 8 : H + 16, :] = jnp.zeros((8, 128), F32)
     for cp in range(PAIRS):
         padded = pad_rows(scr[pl.ds(cp, H, stride=PAIRS), :].astype(BF16))
-        padded_ref[cp] = padded
         mixed = tall_conv(padded, tall_ref[cp], 1).astype(BF16)
         mixed_ref[cp] = mixed
         pad[8 : H + 8, :] = mixed.astype(F32)
@@ -205,11 +204,12 @@
     conv_ref[...] = out[...].astype(BF16)
 
 
-def beside_kernel(padded_ref, wide_ref, shifted_ref, wide_out):
+def beside_kernel(image_ref, wide_ref, shifted_ref, wide_out, scr):
     in_block = block_mask()
     wide = wide_ref[...]
+    scr[...] = image_ref[...].astype(F32)
     for cp in range(PAIRS):
-        padded = padded_ref[cp].astype(F32)
+        padded = pad_rows(scr[pl.ds(cp, H, stride=PAIRS), :])
         for q in range(SHORT):
             shifted_ref[cp, q] = shifted(padded, q - 2).astype(BF16)
         wide_out[cp] = wide_matrices(wide, cp, in_block)
@@ -336,7 +336,7 @@
     output_ref,
     theirs_ref,
     mine_ref,
-    left_ref,
+    normed_ref,
     right_ref,
     small_ref,
     scr,
@@ -368,14 +368,13 @@
         inverse = lax.rsqrt(jnp.mean(centred * centred, axis=1, keepdims=True) + epsilon)
         xhat = centred * inverse
         normed = (xhat * gain + bias).astype(BF16)
-        left_ref[0, rows, :] = normed
+        normed_ref[rows, :] = normed
         pre_act = jnp.dot(normed, w_in_ref[...], preferred_element_type=F32) + b_in_ref[...]
         cdf = 0.5 * (1.0 + lax.erf(pre_act * 0.7071067811865476))
         hidden = (pre_act * cdf).astype(BF16)
         right_ref[1, rows, :] = hidden
         branch = jnp.dot(hidden, w_out_ref[...], preferred_element_type=F32) + b_out_ref[...]
         cot = cot_ref[rows, :]
-        left_ref[1, rows, :] = cot
         output_ref[rows, :] = (image_ref[rows, :].astype(F32) + branch).astype(BF16)
         d_hidden = lax.dot_general(
             cot, w_out_ref[...], (((1,), (1,)), ((), ())), preferred_element_type=F32
@@ -401,7 +400,7 @@
     half = CHIPS * MSG
     theirs_ref[GRADS : GRADS + half, :] = out[pl.ds((1 - core) * half, half), :].astype(BF16)
     mine_ref[...] = out[pl.ds(core * half, half), :].astype(BF16)
-    weight_grads(scale, left_ref, right_ref, 1 - core, theirs_ref)
+    weight_grads(scale, normed_ref, cot_ref, right_ref, 1 - core, theirs_ref)
     small[...] = jnp.zeros((16, 128), F32)
     for i in range(FF // 128):
         small[i : i + 1, :] = g_b_in[:, i * 128 : (i + 1) * 128] * scale
@@ -416,9 +415,12 @@
     ).astype(BF16)
 
 
-def weight_grads(scale, left_ref, right_ref, which, out_ref):
+def weight_grads(scale, normed_ref, cot_ref, right_ref, which, out_ref):
     grads = lax.dot_general(
-        left_ref[which], right_ref[which], (((0,), (0,)), ((), ())), preferred_element_type=F32
+        jnp.where(which == 0, normed_ref[...], cot_ref[...]),
+        right_ref[which],
+        (((0,), (0,)), ((), ())),
+        preferred_element_type=F32,
     )
     grads = (grads * scale).astype(out_ref.dtype)
     for i in range(CHIPS):
@@ -427,8 +429,8 @@
             out_ref[at : at + 16, :] = grads[i * 16 : (i + 1) * 16, j * 128 : (j + 1) * 128]
 
 
-def own_grads_kernel(scale, core_ref, left_ref, right_ref, out_ref):
-    weight_grads(scale, left_ref, right_ref, core_ref[0], out_ref)
+def own_grads_kernel(scale, core_ref, normed_ref, cot_ref, right_ref, out_ref):
+    weight_grads(scale, normed_ref, cot_ref, right_ref, core_ref[0], out_ref)
 
 
 def merge_kernel(core_ref, mine_ref, grads_ref, small_ref, got_ref, out_ref, small_out):
@@ -446,10 +448,14 @@
         out_ref[i, DATA : DATA + OWN, :] = (grads_ref[rows, :] + got_ref[rows, :].astype(F32)).astype(BF16)
 
 
-def pair_sum_kernel(mine_ref, got_ref, out_ref):
-    total = (mine_ref[...].astype(F32) + got_ref[...].astype(F32)).astype(BF16)
-    for i in range(out_ref.shape[0]):
-        out_ref[i] = total
+def pair_sum_kernel(mine_ref, got_ref, out_ref, total, sems):
+    total[...] = (mine_ref[...].astype(F32) + got_ref[...].astype(F32)).astype(BF16)
+    count = out_ref.shape[0]
+    copies = [pltpu.make_async_copy(total, out_ref.at[i], sems.at[i]) for i in range(count)]
+    for copy in copies:
+        copy.start()
+    for copy in copies:
+        copy.wait()
 
 
 def gather_kernel(parts_ref, d_image_ref, out_ref):
@@ -483,20 +489,26 @@
     sems,
 ):
     core = core_ref[0]
-    low = core == 0
     rest = LAST - OWN
-    totals = [None, None]
-    for i in range(CHIPS):
-        mine, got = mine_ref[i].astype(F32), got_ref[i].astype(F32)
-        sides = (jnp.where(low, mine, got), jnp.where(low, got, mine))
-        for c, (side, into) in enumerate(zip(sides, (w_in, turn), strict=True)):
-            for j in range(FF // 128):
-                piece = side[DATA + j * 16 : DATA + (j + 1) * 16]
-                into[i * 16 : (i + 1) * 16, j * 128 : (j + 1) * 128] = piece
-            scr[c, i * rest : i * rest + DATA, :] = side[:DATA]
-            scr[c, i * rest + DATA : (i + 1) * rest, :] = side[DATA + OWN :]
-            part = side[LAST - 8 :]
-            totals[c] = part if totals[c] is None else totals[c] + part
+
+    def place(core_0_ref, core_1_ref):
+        for i in range(CHIPS):
+            for c, (ref, into) in enumerate(((core_0_ref, w_in), (core_1_ref, turn))):
+                side = ref[i].astype(F32)
+                for j in range(FF // 128):
+                    piece = side[DATA + j * 16 : DATA + (j + 1) * 16]
+                    into[i * 16 : (i + 1) * 16, j * 128 : (j + 1) * 128] = piece
+                scr[c, i * rest : i * rest + DATA, :] = side[:DATA]
+                scr[c, i * rest + DATA : (i + 1) * rest, :] = side[DATA + OWN :]
+
+    @pl.when(core == 0)
+    def _():
+        place(mine_ref, got_ref)
+
+    @pl.when(core == 1)
+    def _():
+        place(got_ref, mine_ref)
+
     copies = [pltpu.make_async_copy(w_in, w_in_hbm, sems.at[0])]
     copies[0].start()
     step = FF // 2
@@ -528,6 +540,13 @@
                     for c in range(CORES)
                 ]
             )[7 : 7 + LONG]
+    totals = []
+    for c in range(CORES):
+        total = None
+        for i in range(CHIPS):
+            part = scr[c, (i + 1) * rest - 8 : (i + 1) * rest, :]
+            total = part if total is None else total + part
+        totals.append(total)
     for i in range(FF // 128):
         b_in_ref[:, i * 128 : (i + 1) * 128] = totals[0][i : i + 1]
     for n, ref in enumerate((gain_ref, shift_ref, b_out_ref)):
@@ -579,7 +598,7 @@
         pack_kernel,
         packed_b,
         [packed_f],
-    )(source)
+    )(image)
     me = lax.axis_index("strip")
     core = (me % CORES).reshape(1)
     me = (me % CORES) * CHIPS + me // CORES
@@ -598,23 +617,22 @@
     )(tall, wide)
 
     image_ch = messages(image_msg)
-    conv_ch, mixed, padded = call(
+    conv_ch, mixed = call(
         forward_kernel,
         (
             packed_b,
             shape((PAIRS, H, 128), BF16),
-            shape((PAIRS, H + 2 * REACH, 128), BF16),
         ),
         [packed_f, edge, packed_f],
     )(image_ch, tall_fwd, wide_fwd)
     conv = messages(conv_ch)
-    output, theirs, mine, left, right, small = call(
+    output, theirs, mine, normed, right, small = call(
         functools.partial(mlp_kernel, scale),
         (
             shape((CELLS, C), BF16),
             shape((GRADS + CHIPS * MSG + 16, 128), BF16),
             shape((CHIPS * MSG, 128), BF16),
-            shape((2, CELLS, C), BF16),
+            shape((CELLS, C), BF16),
             shape((2, CELLS, FF), BF16),
             shape((8, 128), F32),
         ),
@@ -634,8 +652,8 @@
     )
     got = between_cores(theirs)
     chip_grads = call(
-        functools.partial(own_grads_kernel, scale), shape((GRADS, 128), F32), (), [SMEM] + [VMEM] * 2
-    )(core, left, right)
+        functools.partial(own_grads_kernel, scale), shape((GRADS, 128), F32), (), [SMEM] + [VMEM] * 3
+    )(core, normed, upstream.reshape(CELLS, C), right)
     merged, small = call(
         merge_kernel,
         (shape((CHIPS, DATA + OWN, 128), BF16), shape((8, 128), F32)),
@@ -645,7 +663,8 @@
     shifts, wide_bwd = call(
         beside_kernel,
         (shape((PAIRS, SHORT, H + 2 * REACH, 128), BF16), shape((PAIRS, SHORT * 128, 128), BF16)),
-    )(padded, wide)
+        [packed_f],
+    )(image_ch, wide)
     d_mixed, share = call(
         functools.partial(backward_kernel, scale),
         (shape((PAIRS, H, 128), BF16), shape((SHARE, 128), BF16)),
@@ -654,7 +673,13 @@
     got = lax.ppermute(share, "slide", [(i, i ^ 1) for i in range(slides)])
     d_image_msg = call(d_image_kernel, packed_b, [packed_f])(d_mixed, tall)
     half = slides // 2
-    copies = call(pair_sum_kernel, shape((half, SHARE, 128), BF16))(share, got)
+    copies = call(
+        pair_sum_kernel,
+        shape((half, SHARE, 128), BF16),
+        [pltpu.VMEM((SHARE, 128), BF16), pltpu.SemaphoreType.DMA((half,))],
+        [VMEM, VMEM],
+        HBM,
+    )(share, got)
     groups = [[2 * i + j for i in range(half)] for j in range(2)]
     parts = lax.all_to_all(copies, "slide", 0, 0, axis_index_groups=groups, tiled=True)
     last = call(gather_kernel, shape((CHIPS, LAST, 128), BF16))(parts, d_image_msg)

time: 145 us -> 145 us (level)
  no operation moved by 1% of the time
where the time goes in v4:
time: 145 us
  blocking collectives  45.9 us (32%)
  waiting for transfers between devices  44 us (30%)
  starting transfers between devices  33.4 us (23%)
  Pallas kernels  18 us (12%)
    all_to_all x1, blocking collectives, between_chips(): lax.all_to_all(x, 'strip', 0, 0, axis_index_groups=groups, tiled=True)  30 us
    all_to_all x1, waiting for transfers between devices, between_chips(): lax.all_to_all(x, 'strip', 0, 0, axis_index_groups=groups, tiled=True)  20 us
    all_to_all x1, blocking collectives, messages(): x = lax.all_to_all(x.reshape(STRIPS, MSG, 128), 'strip', 0, 0, tiled=True)  16 us
    all_to_all x1, starting transfers between devices, messages(): x = lax.all_to_all(x.reshape(STRIPS, MSG, 128), 'strip', 0, 0, tiled=True)  11.2 us
    all_to_all x1, starting transfers between devices, local(): lax.all_to_all(copies, 'slide', 0, 0, axis_index_groups=groups, tiled=True)  10.3 us
    all_to_all x1, waiting for transfers between devices, local(): lax.all_to_all(copies, 'slide', 0, 0, axis_index_groups=groups, tiled=True)  9.48 us
    all_to_all x1, waiting for transfers between devices, messages(): x = lax.all_to_all(x.reshape(STRIPS, MSG, 128), 'strip', 0, 0, tiled=True)  8.12 us
    ppermute x2, starting transfers between devices, between_cores(): return lax.ppermute(x, 'strip', [(i, i ^ 1) for i in range(STRIPS)])  6.34 us
  transfers between devices with their start and end apart: 6, of which 6 were waited for; matrix products, arithmetic and copies ran while one was open for 1% of the time, Pallas kernels for 4%

profile of v4, /device:TPU:1, one launch (start us, length us, event | category | flops | bytes accessed | tf_op | source)
XLA Modules:
  0.0 144.6 jit_solution(4016436763243765736)
XLA Ops:
  0.6 0.0 copy-start
  0.7 0.0 copy-start.1
  0.7 0.0 copy-start.2
  0.7 1.0 copy-done.2
  1.7 0.9 shard_map.177
  2.6 11.2 %all-to-all-start = ((bf16[32,24,128]{2,1,0:T(8,128)(2,1)}), bf16[32,24,128]{2,1,0:T(8,128)(2,1)S(1)}, u32[]{:S(2)}, u32[]{:S(2)}) async-start(bf16[32,24,128]{2,1,0:T(8,128)(2,1)} %bitcast.1), calls=%async_computation | async-start | bytes 393216 | tf_op jit(solution)/shard_map/all_to_all | solution.py:560
  13.8 0.2 convolution_bitcast_fusion.1
  14.0 1.1 convolution_bitcast_fusion
  15.1 2.3 %shard_map.178 = (bf16[4,320,256]{2,1,0:T(8,128)(2,1)S(1)}, bf16[4,640,128]{2,1,0:T(8,128)(2,1)S(1)}) custom-call(f32[40,128]{1,0:T(8,128)S(1)} %pad.7.tall_ref, f32[40,128]{1,0:T(8,128)S(1)} %pad.8.wide_ref), custom_call_target="tpu_custom_call" | custom-call | tf_op jit(solution)/shard_map/pallas_call | solution.py:615
  17.5 8.1 %all-to-all-done = bf16[32,24,128]{2,1,0:T(8,128)(2,1)S(1)} async-done(((bf16[32,24,128]{2,1,0:T(8,128)(2,1)}), bf16[32,24,128]{2,1,0:T(8,128)(2,1)S(1)}, u32[]{:S(2)}, u32[]{:S(2)}) %all-to-all-start) | async-done | bytes 196640 | tf_op jit(solution)/shard_map/all_to_all | solution.py:560
  25.6 1.6 %shard_map.179 = (bf16[768,128]{1,0:T(8,128)(2,1)S(1)}, bf16[4,192,128]{2,1,0:T(8,128)(2,1)S(1)}) custom-call(bf16[768,128]{1,0:T(8,128)(2,1)S(1)} %bitcast.36, bf16[4,320,256]{2,1,0:T(8,128)(2,1)S(1)} %get-tuple-element.35.tall_ref, bf16[4,640,128]{2,1,0:T(8,128)(2,1)S(1)} %get-tuple-element.36.wide_ref), custom_call_target="tpu_custom_call" | custom-call | tf_op jit(solution)/shard_map/pallas_call | solution.py:620
  27.2 16.0 %all_to_all.25 = bf16[32,24,128]{2,1,0:T(8,128)(2,1)S(1)} all-to-all(bf16[32,24,128]{2,1,0:T(8,128)(2,1)S(1)} %bitcast.40), channel_id=1, replica_groups=mesh['slide'=16,'strip'=32] {'strip'}, dimensions={0} | all-to-all | bytes 393216 | tf_op jit(solution)/shard_map/all_to_all | solution.py:560
  43.2 3.2 %shard_map.180 = (bf16[384,256]{1,0:T(8,128)(2,1)}, bf16[2448,128]{1,0:T(8,128)(2,1)S(1)}, bf16[384,128]{1,0:T(8,128)(2,1)S(1)}, bf16[384,256]{1,0:T(8,128)(2,1)...) custom-call(s32[1]{0:T(128)} %bitcast.core_ref, bf16[768,128]{1,0:T(8,128)(2,1)S(1)} %bitcast.39, ...), custom_call_target="tpu_custom_call" | custom-call | tf_op jit(solution)/shard_map/pallas_call | solution.py:629
  46.4 1.9 %collective-permute-start = (bf16[2448,128]{1,0:T(8,128)(2,1)S(1)}, bf16[2448,128]{1,0:T(8,128)(2,1)S(1)}, u32[]{:S(2)}, u32[]{:S(2)}) collective-permute-start(bf16[2448,128]{1,0:T(8,128)(2,1)S(1)} %get-tuple-element.43), channel_id=1, source_target_pairs={{0,1},{1,0},{2,3},{3,2},{4,5},{5,4},{6,7},{7,6},{8,9},{9,8},{10,11... | collective-permute-start | bytes 1880072 | tf_op jit(solution)/shard_map/ppermute | solution.py:570
  48.4 0.5 shard_map.181.grads_ref
  48.9 1.5 %collective-permute-done.got_ref = bf16[2448,128]{1,0:T(8,128)(2,1)S(1)} collective-permute-done((bf16[2448,128]{1,0:T(8,128)(2,1)S(1)}, bf16[2448,128]{1,0:T(8,128)(2,1)S(1)}, u32[]{:S(2)}, u32[]{:S(2)}) %collective-permute-start) | collective-permute-done | bytes 626720 | tf_op jit(solution)/shard_map/ppermute | solution.py:570
  50.4 1.0 shard_map.182
  51.4 3.6 %all-to-all-start.2 = ((bf16[16,176,128]{2,1,0:T(8,128)(2,1)}), bf16[16,176,128]{2,1,0:T(8,128)(2,1)S(1)}, u32[]{:S(2)}, u32[]{:S(2)}) async-start(bf16[16,176,128]{2,1,0:T(8,128)(2,1)} %get-tuple-element.44), calls=%async_computation.2 | async-start | bytes 1441792 | tf_op jit(solution)/shard_map/all_to_all | solution.py:566
  55.0 1.8 %shard_map.183 = (bf16[4,5,256,128]{3,2,1,0:T(8,128)(2,1)S(1)}, bf16[4,640,128]{2,1,0:T(8,128)(2,1)S(1)}) custom-call(bf16[768,128]{1,0:T(8,128)(2,1)S(1)} %bitcast.37, f32[40,128]{1,0:T(8,128)S(1)} %pad.8.wide_ref), custom_call_target="tpu_custom_call" | custom-call | tf_op jit(solution)/shard_map/pallas_call | solution.py:663
  56.9 20.0 %all-to-all-done.2.parts_ref = bf16[16,176,128]{2,1,0:T(8,128)(2,1)S(1)} async-done(((bf16[16,176,128]{2,1,0:T(8,128)(2,1)}), bf16[16,176,128]{2,1,0:T(8,128)(2,1)S(1)}, u32[]{:S(2)}, u32[]{:S(2)}) %all-to-all-start.2) | async-done | bytes 720928 | tf_op jit(solution)/shard_map/all_to_all | solution.py:566
  76.8 2.3 %shard_map.184 = (bf16[4,192,128]{2,1,0:T(8,128)(2,1)S(1)}, bf16[176,128]{1,0:T(8,128)(2,1)S(1)}) custom-call(bf16[16,176,128]{2,1,0:T(8,128)(2,1)S(1)} %all-to-all-done.2.parts_ref, bf16[4,5,256,128]{3,2,1,0:T(8,128)(2,1)S(1)} %get-tuple-element.45.shifted_ref, bf16[4,192,128]{2,1,0:T(8,128)(2,1)S(1)} %get-tuple-element.46.mixed_ref, ...), custom_call_target="tpu_custom_call" | custom-call | tf_op jit(solution)/shard_map/pallas_call | solution.py:668
  79.1 1.9 %collective-permute-start.1 = (bf16[176,128]{1,0:T(8,128)(2,1)S(1)}, bf16[176,128]{1,0:T(8,128)(2,1)S(1)}, u32[]{:S(2)}, u32[]{:S(2)}) collective-permute-start(bf16[176,128]{1,0:T(8,128)(2,1)S(1)} %get-tuple-element.49.mine_ref), channel_id=1, source_target_pairs={{0,32},{32,0},{64,96},{96,64},{128,160},{160,128},{192,224},{224,1... | collective-permute-start | bytes 135176 | tf_op jit(solution)/shard_map/ppermute | solution.py:673
  81.0 2.9 %collective-permute-done.1.got_ref = bf16[176,128]{1,0:T(8,128)(2,1)S(1)} collective-permute-done((bf16[176,128]{1,0:T(8,128)(2,1)S(1)}, bf16[176,128]{1,0:T(8,128)(2,1)S(1)}, u32[]{:S(2)}, u32[]{:S(2)}) %collective-permute-start.1) | collective-permute-done | bytes 45088 | tf_op jit(solution)/shard_map/ppermute | solution.py:673
  83.9 0.8 shard_map.185
  84.7 10.3 %all-to-all-start.3 = ((bf16[8,176,128]{2,1,0:T(8,128)(2,1)}), bf16[8,176,128]{2,1,0:T(8,128)(2,1)S(1)}, u32[]{:S(2)}, u32[]{:S(2)}) async-start(bf16[8,176,128]{2,1,0:T(8,128)(2,1)} %shard_map.185), calls=%async_computation.3 | async-start | bytes 720896 | tf_op jit(solution)/shard_map/all_to_all | solution.py:684
  95.0 1.0 shard_map.186.d_image_ref
  96.1 9.5 %all-to-all-done.3.parts_ref = bf16[8,176,128]{2,1,0:T(8,128)(2,1)S(1)} async-done(((bf16[8,176,128]{2,1,0:T(8,128)(2,1)}), bf16[8,176,128]{2,1,0:T(8,128)(2,1)S(1)}, u32[]{:S(2)}, u32[]{:S(2)}) %all-to-all-start.3) | async-done | bytes 360480 | tf_op jit(solution)/shard_map/all_to_all | solution.py:684
  105.5 0.1 shard_map.187
  105.6 30.0 %all_to_all.26.mine_ref = bf16[16,224,128]{2,1,0:T(8,128)(2,1)S(1)} all-to-all(bf16[16,224,128]{2,1,0:T(8,128)(2,1)S(1)} %shard_map.187), channel_id=1, replica_groups={{0,2,4,6,8,10,12,14,16,18,20,22,24,26,28,30},{1,3,5,7,9,11,13,15,17,19,..., dimensions={0} | all-to-all | bytes 1835008 | tf_op jit(solution)/shard_map/all_to_all | solution.py:566
  135.6 4.4 %collective-permute-start.2 = (bf16[16,224,128]{2,1,0:T(8,128)(2,1)S(1)}, bf16[16,224,128]{2,1,0:T(8,128)(2,1)S(1)}, u32[]{:S(2)}, u32[]{:S(2)}) collective-permute-start(bf16[16,224,128]{2,1,0:T(8,128)(2,1)S(1)} %all_to_all.26.mine_ref), channel_id=1, source_target_pairs={{0,1},{1,0},{2,3},{3,2},{4,5},{5,4},{6,7},{7,6},{8,9},{9,8},{10,11... | collective-permute-start | bytes 2752520 | tf_op jit(solution)/shard_map/ppermute | solution.py:570
  140.0 2.1 %collective-permute-done.2.got_ref = bf16[16,224,128]{2,1,0:T(8,128)(2,1)S(1)} collective-permute-done((bf16[16,224,128]{2,1,0:T(8,128)(2,1)S(1)}, bf16[16,224,128]{2,1,0:T(8,128)(2,1)S(1)}, u32[]{:S(2)}, u32[]{:S(2)}) %collective-permute-start.2) | collective-permute-done | bytes 917536 | tf_op jit(solution)/shard_map/ppermute | solution.py:570
  142.1 2.6 %shard_map.188 = (bf16[6,64,256]{2,1,0:T(8,128)(2,1)}, f32[5,51,256]{2,1,0:T(8,128)}, f32[5,51,256]{2,1,0:T(8,128)}, f32[1,256]{1,0:T(1,128)}, f32[1,256]{1,0:T(...) custom-call(s32[1]{0:T(128)} %bitcast.core_ref, ...), custom_call_target="tpu_custom_call" | custom-call | tf_op jit(solution)/shard_map/pallas_call | solution.py:688
  (19 shorter events, 0.1 us)
Async XLA Ops:
  0.6 13.2 %copy-start = (bf16[51,5,256]{2,0,1:T(8,128)(2,1)S(1)}, bf16[51,5,256]{2,0,1:T(8,128)(2,1)}, u32[]{:S(2)}) copy-start(bf16[51,5,256]{2,0,1:T(8,128)(2,1)} %param.12) | copy-start | bytes 391684
  0.7 42.5 %copy-start.1 = (bf16[1,6,64,256]{3,2,1,0:T(8,128)(2,1)S(1)}, bf16[1,6,64,256]{3,2,1,0:T(8,128)(2,1)}, u32[]{:S(2)}) copy-start(bf16[1,6,64,256]{3,2,1,0:T(8,128)(2,1)} %param.11) | copy-start | bytes 589828
  0.7 1.0 copy-start.2
  1.6 41.5 %copy-start.3 = (bf16[1,6,64,256]{3,2,1,0:T(8,128)(2,1)S(1)}, bf16[1,6,64,256]{3,2,1,0:T(8,128)(2,1)}, u32[]{:S(2)}) copy-start(bf16[1,6,64,256]{3,2,1,0:T(8,128)(2,1)} %image_ref.1) | copy-start | bytes 589828
  1.6 41.5 %copy-start.4 = (bf16[256,1024]{1,0:T(8,128)(2,1)S(1)}, bf16[256,1024]{1,0:T(8,128)(2,1)}, u32[]{:S(2)}) copy-start(bf16[256,1024]{1,0:T(8,128)(2,1)} %w_in_ref.1) | copy-start | bytes 1572868
  1.6 41.5 %copy-start.5 = (bf16[1024,256]{1,0:T(8,128)(2,1)S(1)}, bf16[1024,256]{1,0:T(8,128)(2,1)}, u32[]{:S(2)}) copy-start(bf16[1024,256]{1,0:T(8,128)(2,1)} %w_out_ref.1) | copy-start | bytes 1572868
  1.7 41.5 %copy-start.6 = (f32[1024]{0:T(1024)S(1)}, f32[1024]{0:T(1024)}, u32[]{:S(2)}) copy-start(f32[1024]{0:T(1024)} %param.17) | copy-start | bytes 12292
  1.7 41.5 %copy-start.7 = (f32[256]{0:T(256)S(1)}, f32[256]{0:T(256)}, u32[]{:S(2)}) copy-start(f32[256]{0:T(256)} %param.14) | copy-start | bytes 3076
  1.7 41.5 %copy-start.8 = (f32[256]{0:T(256)S(1)}, f32[256]{0:T(256)}, u32[]{:S(2)}) copy-start(f32[256]{0:T(256)} %param.15) | copy-start | bytes 3076
  1.7 41.5 %copy-start.9 = (f32[256]{0:T(256)S(1)}, f32[256]{0:T(256)}, u32[]{:S(2)}) copy-start(f32[256]{0:T(256)} %param.19) | copy-start | bytes 3076
  2.6 23.0 %all-to-all-start = ((bf16[32,24,128]{2,1,0:T(8,128)(2,1)}), bf16[32,24,128]{2,1,0:T(8,128)(2,1)S(1)}, u32[]{:S(2)}, u32[]{:S(2)}) async-start(bf16[32,24,128]{2,1,0:T(8,128)(2,1)} %bitcast.1), calls=%async_computation | async-start | bytes 393216 | tf_op jit(solution)/shard_map/all_to_all | solution.py:560
  46.4 3.9 %collective-permute-start = (bf16[2448,128]{1,0:T(8,128)(2,1)S(1)}, bf16[2448,128]{1,0:T(8,128)(2,1)S(1)}, u32[]{:S(2)}, u32[]{:S(2)}) collective-permute-start(bf16[2448,128]{1,0:T(8,128)(2,1)S(1)} %get-tuple-element.43), channel_id=1, source_target_pairs={{0,1},{1,0},{2,3},{3,2},{4,5},{5,4},{6,7},{7,6},{8,9},{9,8},{10,11... | collective-permute-start | bytes 1880072 | tf_op jit(solution)/shard_map/ppermute | solution.py:570
  51.4 25.4 %all-to-all-start.2 = ((bf16[16,176,128]{2,1,0:T(8,128)(2,1)}), bf16[16,176,128]{2,1,0:T(8,128)(2,1)S(1)}, u32[]{:S(2)}, u32[]{:S(2)}) async-start(bf16[16,176,128]{2,1,0:T(8,128)(2,1)} %get-tuple-element.44), calls=%async_computation.2 | async-start | bytes 1441792 | tf_op jit(solution)/shard_map/all_to_all | solution.py:566
  79.1 4.8 %collective-permute-start.1 = (bf16[176,128]{1,0:T(8,128)(2,1)S(1)}, bf16[176,128]{1,0:T(8,128)(2,1)S(1)}, u32[]{:S(2)}, u32[]{:S(2)}) collective-permute-start(bf16[176,128]{1,0:T(8,128)(2,1)S(1)} %get-tuple-element.49.mine_ref), channel_id=1, source_target_pairs={{0,32},{32,0},{64,96},{96,64},{128,160},{160,128},{192,224},{224,1... | collective-permute-start | bytes 135176 | tf_op jit(solution)/shard_map/ppermute | solution.py:673
  84.7 20.8 %all-to-all-start.3 = ((bf16[8,176,128]{2,1,0:T(8,128)(2,1)}), bf16[8,176,128]{2,1,0:T(8,128)(2,1)S(1)}, u32[]{:S(2)}, u32[]{:S(2)}) async-start(bf16[8,176,128]{2,1,0:T(8,128)(2,1)} %shard_map.185), calls=%async_computation.3 | async-start | bytes 720896 | tf_op jit(solution)/shard_map/all_to_all | solution.py:684
  135.6 6.5 %collective-permute-start.2 = (bf16[16,224,128]{2,1,0:T(8,128)(2,1)S(1)}, bf16[16,224,128]{2,1,0:T(8,128)(2,1)S(1)}, u32[]{:S(2)}, u32[]{:S(2)}) collective-permute-start(bf16[16,224,128]{2,1,0:T(8,128)(2,1)S(1)} %all_to_all.26.mine_ref), channel_id=1, source_target_pairs={{0,1},{1,0},{2,3},{3,2},{4,5},{5,4},{6,7},{7,6},{8,9},{9,8},{10,11... | collective-permute-start | bytes 2752520 | tf_op jit(solution)/shard_map/ppermute | solution.py:570

commit v5 on v4

--- a/solution.py
+++ b/solution.py
@@ -39,12 +39,14 @@
 HBM = pl.BlockSpec(memory_space=pltpu.HBM)
 
 
-def call(kernel, out_shape, scratch=(), in_specs=None, out_specs=None):
+def call(kernel, out_shape, scratch=(), in_specs=None, out_specs=None, aliases=None):
     specs = {}
     if in_specs is not None:
         specs["in_specs"] = in_specs
     if out_specs is not None:
         specs["out_specs"] = out_specs
+    if aliases is not None:
+        specs["input_output_aliases"] = aliases
     return pl.pallas_call(
         kernel,
         out_shape=out_shape,
@@ -416,24 +418,25 @@
 
 
 def weight_grads(scale, normed_ref, cot_ref, right_ref, which, out_ref):
-    grads = lax.dot_general(
-        jnp.where(which == 0, normed_ref[...], cot_ref[...]),
-        right_ref[which],
-        (((0,), (0,)), ((), ())),
-        preferred_element_type=F32,
-    )
-    grads = (grads * scale).astype(out_ref.dtype)
-    for i in range(CHIPS):
-        for j in range(FF // 128):
-            at = (i * (FF // 128) + j) * 16
-            out_ref[at : at + 16, :] = grads[i * 16 : (i + 1) * 16, j * 128 : (j + 1) * 128]
+    for n, left_ref in enumerate((normed_ref, cot_ref)):
+
+        @pl.when(which == n)
+        def _(n=n, left_ref=left_ref):
+            grads = lax.dot_general(
+                left_ref[...], right_ref[n], (((0,), (0,)), ((), ())), preferred_element_type=F32
+            )
+            grads = (grads * scale).astype(out_ref.dtype)
+            for i in range(CHIPS):
+                for j in range(FF // 128):
+                    at = (i * (FF // 128) + j) * 16
+                    out_ref[at : at + 16, :] = grads[i * 16 : (i + 1) * 16, j * 128 : (j + 1) * 128]
 
 
 def own_grads_kernel(scale, core_ref, normed_ref, cot_ref, right_ref, out_ref):
     weight_grads(scale, normed_ref, cot_ref, right_ref, core_ref[0], out_ref)
 
 
-def merge_kernel(core_ref, mine_ref, grads_ref, small_ref, got_ref, out_ref, small_out):
+def merge_kernel(core_ref, mine_ref, grads_ref, small_ref, got_ref, out_hbm, small_out, rows_scr, sems):
     half = CHIPS * MSG
     mine = mine_ref[...].astype(F32)
     got = got_ref[GRADS : GRADS + half, :].astype(F32)
@@ -441,21 +444,26 @@
     small_out[...] = small_ref[...] + other[:8]
     low = core_ref[0] == 0
     one, two = jnp.where(low, mine, got), jnp.where(low, got, mine)
+    copies = []
     for i in range(CHIPS):
         rows = slice(i * MSG, (i + 1) * MSG)
-        out_ref[i, 0:DATA, :] = jnp.concatenate([one[rows], two[rows]], axis=0).astype(BF16)
+        rows_scr[i, 0:DATA, :] = jnp.concatenate([one[rows], two[rows]], axis=0).astype(BF16)
         rows = slice(i * OWN, (i + 1) * OWN)
-        out_ref[i, DATA : DATA + OWN, :] = (grads_ref[rows, :] + got_ref[rows, :].astype(F32)).astype(BF16)
-
-
-def pair_sum_kernel(mine_ref, got_ref, out_ref, total, sems):
-    total[...] = (mine_ref[...].astype(F32) + got_ref[...].astype(F32)).astype(BF16)
-    count = out_ref.shape[0]
-    copies = [pltpu.make_async_copy(total, out_ref.at[i], sems.at[i]) for i in range(count)]
-    for copy in copies:
-        copy.start()
+        rows_scr[i, DATA : DATA + OWN, :] = (
+            grads_ref[rows, :] + got_ref[rows, :].astype(F32)
+        ).astype(BF16)
+        if i % 4 == 3:
+            part = pl.ds(i - 3, 4)
+            copies.append(pltpu.make_async_copy(rows_scr.at[part], out_hbm.at[part], sems.at[i // 4]))
+            copies[-1].start()
     for copy in copies:
         copy.wait()
+
+
+def pair_sum_kernel(mine_ref, got_ref, out_ref):
+    total = (mine_ref[...].astype(F32) + got_ref[...].astype(F32)).astype(BF16)
+    for i in range(out_ref.shape[0]):
+        out_ref[i] = total
 
 
 def gather_kernel(parts_ref, d_image_ref, out_ref):
@@ -468,11 +476,46 @@
         out_ref[i, DATA : DATA + SHARE, :] = total
 
 
+def place_share(core, ref, w_in_hbm, w_out_hbm, held, w_out, sems):
+    lanes = FF // 128
+    for i in range(CHIPS):
+        part = ref[i, DATA : DATA + OWN, :].astype(F32)
+        for j in range(lanes):
+            held[i * 16 : (i + 1) * 16, j * 128 : (j + 1) * 128] = part[j * 16 : (j + 1) * 16]
+
+    @pl.when(core == 0)
+    def _():
+        copy = pltpu.make_async_copy(held, w_in_hbm, sems.at[0])
+        copy.start()
+        copy.wait()
+
+    @pl.when(core == 1)
+    def _():
+        copies = []
+        for n in range(2):
+            for j in range(n * lanes // 2, (n + 1) * lanes // 2):
+                for half in range(2):
+                    w_out[j * 128 : (j + 1) * 128, half * 128 : (half + 1) * 128] = held[
+                        half * 128 : (half + 1) * 128, j * 128 : (j + 1) * 128
+                    ].T
+            rows = pl.ds(n * FF // 2, FF // 2)
+            copies.append(pltpu.make_async_copy(w_out.at[rows], w_out_hbm.at[rows], sems.at[n]))
+            copies[-1].start()
+        for copy in copies:
+            copy.wait()
+
+
+def own_share_kernel(core_ref, mine_ref, w_in_hbm, w_out_hbm, held, w_out, sems):
+    place_share(core_ref[0], mine_ref, w_in_hbm, w_out_hbm, held, w_out, sems)
+
+
 def finish_kernel(
     core_ref,
     mine_ref,
     got_ref,
     cot_ref,
+    w_in_in,
+    w_out_in,
     out_ref,
     tall_ref,
     wide_ref,
@@ -483,45 +526,18 @@
     w_out_hbm,
     b_out_ref,
     scr,
-    turn,
-    w_in,
+    held,
     w_out,
     sems,
 ):
+    del w_in_in, w_out_in
     core = core_ref[0]
     rest = LAST - OWN
-
-    def place(core_0_ref, core_1_ref):
-        for i in range(CHIPS):
-            for c, (ref, into) in enumerate(((core_0_ref, w_in), (core_1_ref, turn))):
-                side = ref[i].astype(F32)
-                for j in range(FF // 128):
-                    piece = side[DATA + j * 16 : DATA + (j + 1) * 16]
-                    into[i * 16 : (i + 1) * 16, j * 128 : (j + 1) * 128] = piece
-                scr[c, i * rest : i * rest + DATA, :] = side[:DATA]
-                scr[c, i * rest + DATA : (i + 1) * rest, :] = side[DATA + OWN :]
-
-    @pl.when(core == 0)
-    def _():
-        place(mine_ref, got_ref)
-
-    @pl.when(core == 1)
-    def _():
-        place(got_ref, mine_ref)
-
-    copies = [pltpu.make_async_copy(w_in, w_in_hbm, sems.at[0])]
-    copies[0].start()
-    step = FF // 2
-    for n in range(2):
-        for j in range(n * step // 128, (n + 1) * step // 128):
-            for half in range(2):
-                w_out[j * 128 : (j + 1) * 128, half * 128 : (half + 1) * 128] = turn[
-                    half * 128 : (half + 1) * 128, j * 128 : (j + 1) * 128
-                ].T
-        rows = pl.ds(n * step, step)
-        copy = pltpu.make_async_copy(w_out.at[rows], w_out_hbm.at[rows], sems.at[n + 1])
-        copy.start()
-        copies.append(copy)
+    for i in range(CHIPS):
+        for c, ref in ((core, mine_ref), (1 - core, got_ref)):
+            at = i * rest
+            scr[c, at : at + DATA, :] = ref[i, 0:DATA, :].astype(F32)
+            scr[c, at + DATA : at + rest, :] = ref[i, DATA + OWN : LAST, :].astype(F32)
     for k in range(ROWS):
         d_image = untwisted(
             [
@@ -552,8 +568,7 @@
     for n, ref in enumerate((gain_ref, shift_ref, b_out_ref)):
         for i in range(2):
             ref[:, i * 128 : (i + 1) * 128] = totals[1][2 * n + i : 2 * n + i + 1]
-    for copy in copies:
-        copy.wait()
+    place_share(1 - core, got_ref, w_in_hbm, w_out_hbm, held, w_out, sems)
 
 
 def messages(x):
@@ -657,8 +672,9 @@
     merged, small = call(
         merge_kernel,
         (shape((CHIPS, DATA + OWN, 128), BF16), shape((8, 128), F32)),
-        (),
+        [pltpu.VMEM((CHIPS, DATA + OWN, 128), BF16), pltpu.SemaphoreType.DMA((4,))],
         [SMEM] + [VMEM] * 4,
+        (HBM, VMEM),
     )(core, mine, chip_grads, small, got)
     shifts, wide_bwd = call(
         beside_kernel,
@@ -673,18 +689,21 @@
     got = lax.ppermute(share, "slide", [(i, i ^ 1) for i in range(slides)])
     d_image_msg = call(d_image_kernel, packed_b, [packed_f])(d_mixed, tall)
     half = slides // 2
-    copies = call(
-        pair_sum_kernel,
-        shape((half, SHARE, 128), BF16),
-        [pltpu.VMEM((SHARE, 128), BF16), pltpu.SemaphoreType.DMA((half,))],
-        [VMEM, VMEM],
-        HBM,
-    )(share, got)
+    got, d_image_msg = lax.optimization_barrier((got, d_image_msg))
+    copies = call(pair_sum_kernel, shape((half, SHARE, 128), BF16))(share, got)
     groups = [[2 * i + j for i in range(half)] for j in range(2)]
     parts = lax.all_to_all(copies, "slide", 0, 0, axis_index_groups=groups, tiled=True)
     last = call(gather_kernel, shape((CHIPS, LAST, 128), BF16))(parts, d_image_msg)
     last = between_chips(last)
     got = between_cores(last)
+    held = [pltpu.VMEM((C, FF), F32), pltpu.VMEM((FF, C), F32), pltpu.SemaphoreType.DMA((2,))]
+    g_w_in, g_w_out = call(
+        own_share_kernel,
+        (shape((C, FF), F32), shape((FF, C), F32)),
+        held,
+        [SMEM, VMEM],
+        (HBM, HBM),
+    )(core, last)
     grad_image, g_tall, g_wide, g_gain, g_shift, g_w_in, g_b_in, g_w_out, g_b_out = call(
         finish_kernel,
         (
@@ -698,16 +717,11 @@
             shape((FF, C), F32),
             shape((1, C), F32),
         ),
-        [
-            pltpu.VMEM((CORES, CHIPS * (LAST - OWN), 128), F32),
-            pltpu.VMEM((C, FF), F32),
-            pltpu.VMEM((C, FF), F32),
-            pltpu.VMEM((FF, C), F32),
-            pltpu.SemaphoreType.DMA((3,)),
-        ],
-        [SMEM] + [VMEM] * 3,
+        [pltpu.VMEM((CORES, CHIPS * (LAST - OWN), 128), F32)] + held,
+        [SMEM] + [VMEM] * 3 + [HBM] * 2,
         (VMEM,) * 5 + (HBM, VMEM, HBM, VMEM),
-    )(core, last, got, upstream)
+        {4: 5, 5: 7},
+    )(core, last, got, upstream, g_w_in, g_w_out)
     return (
         output.reshape(image.shape),
         grad_image[None],

time: 145 us -> 144 us (level)
  blocking collectives: 45.9 us -> 65.8 us
  waiting for transfers between devices: 44 us -> 32.3 us
  starting transfers between devices: 33.4 us -> 23.3 us
    all_to_all x0 -> x1, blocking collectives: none -> 20.5 us  [local(): lax.all_to_all(copies, 'slide', 0, 0, axis_index_groups=groups, tiled=True)]
    all_to_all x1 -> x0, starting transfers between devices: 10.3 us -> none  [local(): lax.all_to_all(copies, 'slide', 0, 0, axis_index_groups=groups, tiled=True)]
    all_to_all x1 -> x0, waiting for transfers between devices: 9.48 us -> none  [local(): lax.all_to_all(copies, 'slide', 0, 0, axis_index_groups=groups, tiled=True)]
  transfers between devices with their start and end apart: 6 -> 5, of which waited for: 6 -> 5; matrix products, arithmetic and copies ran while one was open for 1% -> 1% of each run, Pallas kernels for 4% -> 5%
where the time goes in v5:
time: 144 us
  blocking collectives  65.8 us (46%)
  waiting for transfers between devices  32.3 us (22%)
  starting transfers between devices  23.3 us (16%)
  Pallas kernels  19 us (13%)
    all_to_all x1, blocking collectives, between_chips(): lax.all_to_all(x, 'strip', 0, 0, axis_index_groups=groups, tiled=True)  29.4 us
    all_to_all x1, blocking collectives, local(): lax.all_to_all(copies, 'slide', 0, 0, axis_index_groups=groups, tiled=True)  20.5 us
    all_to_all x1, waiting for transfers between devices, between_chips(): lax.all_to_all(x, 'strip', 0, 0, axis_index_groups=groups, tiled=True)  20 us
    all_to_all x1, blocking collectives, messages(): x = lax.all_to_all(x.reshape(STRIPS, MSG, 128), 'strip', 0, 0, tiled=True)  16 us
    all_to_all x1, starting transfers between devices, messages(): x = lax.all_to_all(x.reshape(STRIPS, MSG, 128), 'strip', 0, 0, tiled=True)  11.2 us
    all_to_all x1, waiting for transfers between devices, messages(): x = lax.all_to_all(x.reshape(STRIPS, MSG, 128), 'strip', 0, 0, tiled=True)  8.12 us
    ppermute x2, starting transfers between devices, between_cores(): return lax.ppermute(x, 'strip', [(i, i ^ 1) for i in range(STRIPS)])  6.6 us
    pallas_call x1, Pallas kernels, local(): call(functools.partial(mlp_kernel, scale), (shape((CELLS, C), BF16), shap...  3.66 us
  transfers between devices with their start and end apart: 5, of which 5 were waited for; matrix products, arithmetic and copies ran while one was open for 1% of the time, Pallas kernels for 5%

profile of v5, /device:TPU:1, one launch (start us, length us, event | category | flops | bytes accessed | tf_op | source)
XLA Modules:
  0.0 143.6 jit_solution(12714007508074129405)
XLA Ops:
  0.6 0.0 copy-start
  0.7 0.0 copy-start.1
  0.7 0.0 copy-start.2
  0.7 1.0 copy-done.2
  1.7 0.9 shard_map.177
  2.6 11.2 %all-to-all-start = ((bf16[32,24,128]{2,1,0:T(8,128)(2,1)}), bf16[32,24,128]{2,1,0:T(8,128)(2,1)S(1)}, u32[]{:S(2)}, u32[]{:S(2)}) async-start(bf16[32,24,128]{2,1,0:T(8,128)(2,1)} %bitcast.1), calls=%async_computation | async-start | bytes 393216 | tf_op jit(solution)/shard_map/all_to_all | solution.py:575
  13.8 0.2 convolution_bitcast_fusion.1
  14.0 1.1 convolution_bitcast_fusion
  15.1 2.3 %shard_map.178 = (bf16[4,320,256]{2,1,0:T(8,128)(2,1)S(1)}, bf16[4,640,128]{2,1,0:T(8,128)(2,1)S(1)}) custom-call(f32[40,128]{1,0:T(8,128)S(1)} %pad.7.tall_ref, f32[40,128]{1,0:T(8,128)S(1)} %pad.8.wide_ref), custom_call_target="tpu_custom_call" | custom-call | tf_op jit(solution)/shard_map/pallas_call | solution.py:630
  17.5 8.1 %all-to-all-done = bf16[32,24,128]{2,1,0:T(8,128)(2,1)S(1)} async-done(((bf16[32,24,128]{2,1,0:T(8,128)(2,1)}), bf16[32,24,128]{2,1,0:T(8,128)(2,1)S(1)}, u32[]{:S(2)}, u32[]{:S(2)}) %all-to-all-start) | async-done | bytes 196640 | tf_op jit(solution)/shard_map/all_to_all | solution.py:575
  25.6 1.6 %shard_map.179 = (bf16[768,128]{1,0:T(8,128)(2,1)S(1)}, bf16[4,192,128]{2,1,0:T(8,128)(2,1)S(1)}) custom-call(bf16[768,128]{1,0:T(8,128)(2,1)S(1)} %bitcast.36, bf16[4,320,256]{2,1,0:T(8,128)(2,1)S(1)} %get-tuple-element.39.tall_ref, bf16[4,640,128]{2,1,0:T(8,128)(2,1)S(1)} %get-tuple-element.40.wide_ref), custom_call_target="tpu_custom_call" | custom-call | tf_op jit(solution)/shard_map/pallas_call | solution.py:635
  27.2 16.0 %all_to_all.25 = bf16[32,24,128]{2,1,0:T(8,128)(2,1)S(1)} all-to-all(bf16[32,24,128]{2,1,0:T(8,128)(2,1)S(1)} %bitcast.40), channel_id=1, replica_groups=mesh['slide'=16,'strip'=32] {'strip'}, dimensions={0} | all-to-all | bytes 393216 | tf_op jit(solution)/shard_map/all_to_all | solution.py:575
  43.2 0.0 copy-done.5
  43.2 3.7 %shard_map.180 = (bf16[384,256]{1,0:T(8,128)(2,1)}, bf16[2448,128]{1,0:T(8,128)(2,1)S(1)}, bf16[384,128]{1,0:T(8,128)(2,1)S(1)}, bf16[384,256]{1,0:T(8,128)(2,1)...) custom-call(s32[1]{0:T(128)} %bitcast.core_ref, bf16[768,128]{1,0:T(8,128)(2,1)S(1)} %bitcast.39, ...), custom_call_target="tpu_custom_call" | custom-call | tf_op jit(solution)/shard_map/pallas_call | solution.py:644
  46.9 1.9 %collective-permute-start = (bf16[2448,128]{1,0:T(8,128)(2,1)S(1)}, bf16[2448,128]{1,0:T(8,128)(2,1)S(1)}, u32[]{:S(2)}, u32[]{:S(2)}) collective-permute-start(bf16[2448,128]{1,0:T(8,128)(2,1)S(1)} %get-tuple-element.47), channel_id=1, source_target_pairs={{0,1},{1,0},{2,3},{3,2},{4,5},{5,4},{6,7},{7,6},{8,9},{9,8},{10,11... | collective-permute-start | bytes 1880072 | tf_op jit(solution)/shard_map/ppermute | solution.py:585
  48.8 0.5 shard_map.181.grads_ref
  49.3 1.5 %collective-permute-done.got_ref = bf16[2448,128]{1,0:T(8,128)(2,1)S(1)} collective-permute-done((bf16[2448,128]{1,0:T(8,128)(2,1)S(1)}, bf16[2448,128]{1,0:T(8,128)(2,1)S(1)}, u32[]{:S(2)}, u32[]{:S(2)}) %collective-permute-start) | collective-permute-done | bytes 626720 | tf_op jit(solution)/shard_map/ppermute | solution.py:585
  50.8 0.9 shard_map.182
  51.8 3.6 %all-to-all-start.2 = ((bf16[16,176,128]{2,1,0:T(8,128)(2,1)}), bf16[16,176,128]{2,1,0:T(8,128)(2,1)S(1)}, u32[]{:S(2)}, u32[]{:S(2)}) async-start(bf16[16,176,128]{2,1,0:T(8,128)(2,1)} %get-tuple-element.48), calls=%async_computation.2 | async-start | bytes 1441792 | tf_op jit(solution)/shard_map/all_to_all | solution.py:581
  55.4 1.8 %shard_map.183 = (bf16[4,5,256,128]{3,2,1,0:T(8,128)(2,1)S(1)}, bf16[4,640,128]{2,1,0:T(8,128)(2,1)S(1)}) custom-call(bf16[768,128]{1,0:T(8,128)(2,1)S(1)} %bitcast.37, f32[40,128]{1,0:T(8,128)S(1)} %pad.8.wide_ref), custom_call_target="tpu_custom_call" | custom-call | tf_op jit(solution)/shard_map/pallas_call | solution.py:679
  57.2 20.0 %all-to-all-done.2.parts_ref = bf16[16,176,128]{2,1,0:T(8,128)(2,1)S(1)} async-done(((bf16[16,176,128]{2,1,0:T(8,128)(2,1)}), bf16[16,176,128]{2,1,0:T(8,128)(2,1)S(1)}, u32[]{:S(2)}, u32[]{:S(2)}) %all-to-all-start.2) | async-done | bytes 720928 | tf_op jit(solution)/shard_map/all_to_all | solution.py:581
  77.2 2.3 %shard_map.184 = (bf16[4,192,128]{2,1,0:T(8,128)(2,1)S(1)}, bf16[176,128]{1,0:T(8,128)(2,1)S(1)}) custom-call(bf16[16,176,128]{2,1,0:T(8,128)(2,1)S(1)} %all-to-all-done.2.parts_ref, bf16[4,5,256,128]{3,2,1,0:T(8,128)(2,1)S(1)} %get-tuple-element.49.shifted_ref, bf16[4,192,128]{2,1,0:T(8,128)(2,1)S(1)} %get-tuple-element.50.mixed_ref, ...), custom_call_target="tpu_custom_call" | custom-call | tf_op jit(solution)/shard_map/pallas_call | solution.py:684
  79.5 1.9 %collective-permute-start.1 = (bf16[176,128]{1,0:T(8,128)(2,1)S(1)}, bf16[176,128]{1,0:T(8,128)(2,1)S(1)}, u32[]{:S(2)}, u32[]{:S(2)}) collective-permute-start(bf16[176,128]{1,0:T(8,128)(2,1)S(1)} %get-tuple-element.53.mine_ref), channel_id=1, source_target_pairs={{0,32},{32,0},{64,96},{96,64},{128,160},{160,128},{192,224},{224,1... | collective-permute-start | bytes 135176 | tf_op jit(solution)/shard_map/ppermute | solution.py:689
  81.4 1.0 shard_map.185.d_image_ref
  82.4 1.8 %collective-permute-done.1.got_ref = bf16[176,128]{1,0:T(8,128)(2,1)S(1)} collective-permute-done((bf16[176,128]{1,0:T(8,128)(2,1)S(1)}, bf16[176,128]{1,0:T(8,128)(2,1)S(1)}, u32[]{:S(2)}, u32[]{:S(2)}) %collective-permute-start.1) | collective-permute-done | bytes 45088 | tf_op jit(solution)/shard_map/ppermute | solution.py:689
  84.3 20.5 %all_to_all.26.parts_ref = bf16[8,176,128]{2,1,0:T(8,128)(2,1)S(1)} all-to-all(bf16[8,176,128]{2,1,0:T(8,128)(2,1)S(1)} %shard_map.186), channel_id=1, replica_groups={{0,64,128,192,256,320,384,448},{32,96,160,224,288,352,416,480},{1,65,12..., dimensions={0} | all-to-all | bytes 720896 | tf_op jit(solution)/shard_map/all_to_all | solution.py:695
  104.8 0.1 shard_map.187
  104.9 29.4 %all_to_all.27.mine_ref = bf16[16,224,128]{2,1,0:T(8,128)(2,1)S(1)} all-to-all(bf16[16,224,128]{2,1,0:T(8,128)(2,1)S(1)} %shard_map.187), channel_id=1, replica_groups={{0,2,4,6,8,10,12,14,16,18,20,22,24,26,28,30},{1,3,5,7,9,11,13,15,17,19,..., dimensions={0} | all-to-all | bytes 1835008 | tf_op jit(solution)/shard_map/all_to_all | solution.py:581
  134.2 4.7 %collective-permute-start.2 = (bf16[16,224,128]{2,1,0:T(8,128)(2,1)S(1)}, bf16[16,224,128]{2,1,0:T(8,128)(2,1)S(1)}, u32[]{:S(2)}, u32[]{:S(2)}) collective-permute-start(bf16[16,224,128]{2,1,0:T(8,128)(2,1)S(1)} %all_to_all.27.mine_ref), channel_id=1, source_target_pairs={{0,1},{1,0},{2,3},{3,2},{4,5},{5,4},{6,7},{7,6},{8,9},{9,8},{10,11... | collective-permute-start | bytes 2752520 | tf_op jit(solution)/shard_map/ppermute | solution.py:585
  138.9 1.3 shard_map.188
  140.2 0.8 collective-permute-done.2.got_ref
  141.0 2.6 %shard_map.189 = (bf16[6,64,256]{2,1,0:T(8,128)(2,1)}, f32[5,51,256]{2,1,0:T(8,128)}, f32[5,51,256]{2,1,0:T(8,128)}, f32[1,256]{1,0:T(1,128)}, f32[1,256]{1,0:T(...) custom-call(s32[1]{0:T(128)} %bitcast.core_ref, ...), custom_call_target="tpu_custom_call", output_to_operand_aliasing={{5}: (4, {}), {7}: (5, {})} | custom-call | tf_op jit(solution)/shard_map/pallas_call | solution.py:707
  (19 shorter events, 0.1 us)
Async XLA Ops:
  0.6 13.2 %copy-start = (bf16[51,5,256]{2,0,1:T(8,128)(2,1)S(1)}, bf16[51,5,256]{2,0,1:T(8,128)(2,1)}, u32[]{:S(2)}) copy-start(bf16[51,5,256]{2,0,1:T(8,128)(2,1)} %param.12) | copy-start | bytes 391684
  0.7 42.5 %copy-start.1 = (bf16[1,6,64,256]{3,2,1,0:T(8,128)(2,1)S(1)}, bf16[1,6,64,256]{3,2,1,0:T(8,128)(2,1)}, u32[]{:S(2)}) copy-start(bf16[1,6,64,256]{3,2,1,0:T(8,128)(2,1)} %param.11) | copy-start | bytes 589828
  0.7 1.0 copy-start.2
  1.6 41.5 %copy-start.3 = (bf16[1,6,64,256]{3,2,1,0:T(8,128)(2,1)S(1)}, bf16[1,6,64,256]{3,2,1,0:T(8,128)(2,1)}, u32[]{:S(2)}) copy-start(bf16[1,6,64,256]{3,2,1,0:T(8,128)(2,1)} %image_ref.1) | copy-start | bytes 589828
  1.6 41.5 %copy-start.4 = (bf16[256,1024]{1,0:T(8,128)(2,1)S(1)}, bf16[256,1024]{1,0:T(8,128)(2,1)}, u32[]{:S(2)}) copy-start(bf16[256,1024]{1,0:T(8,128)(2,1)} %w_in_ref.1) | copy-start | bytes 1572868
  1.6 41.5 %copy-start.5 = (bf16[1024,256]{1,0:T(8,128)(2,1)S(1)}, bf16[1024,256]{1,0:T(8,128)(2,1)}, u32[]{:S(2)}) copy-start(bf16[1024,256]{1,0:T(8,128)(2,1)} %w_out_ref.1) | copy-start | bytes 1572868
  1.7 41.5 %copy-start.6 = (f32[1024]{0:T(1024)S(1)}, f32[1024]{0:T(1024)}, u32[]{:S(2)}) copy-start(f32[1024]{0:T(1024)} %param.17) | copy-start | bytes 12292
  1.7 41.6 %copy-start.7 = (f32[256]{0:T(256)S(1)}, f32[256]{0:T(256)}, u32[]{:S(2)}) copy-start(f32[256]{0:T(256)} %param.14) | copy-start | bytes 3076
  1.7 41.6 %copy-start.8 = (f32[256]{0:T(256)S(1)}, f32[256]{0:T(256)}, u32[]{:S(2)}) copy-start(f32[256]{0:T(256)} %param.15) | copy-start | bytes 3076
  1.7 41.6 %copy-start.9 = (f32[256]{0:T(256)S(1)}, f32[256]{0:T(256)}, u32[]{:S(2)}) copy-start(f32[256]{0:T(256)} %param.19) | copy-start | bytes 3076
  2.6 23.0 %all-to-all-start = ((bf16[32,24,128]{2,1,0:T(8,128)(2,1)}), bf16[32,24,128]{2,1,0:T(8,128)(2,1)S(1)}, u32[]{:S(2)}, u32[]{:S(2)}) async-start(bf16[32,24,128]{2,1,0:T(8,128)(2,1)} %bitcast.1), calls=%async_computation | async-start | bytes 393216 | tf_op jit(solution)/shard_map/all_to_all | solution.py:575
  46.9 3.9 %collective-permute-start = (bf16[2448,128]{1,0:T(8,128)(2,1)S(1)}, bf16[2448,128]{1,0:T(8,128)(2,1)S(1)}, u32[]{:S(2)}, u32[]{:S(2)}) collective-permute-start(bf16[2448,128]{1,0:T(8,128)(2,1)S(1)} %get-tuple-element.47), channel_id=1, source_target_pairs={{0,1},{1,0},{2,3},{3,2},{4,5},{5,4},{6,7},{7,6},{8,9},{9,8},{10,11... | collective-permute-start | bytes 1880072 | tf_op jit(solution)/shard_map/ppermute | solution.py:585
  51.8 25.5 %all-to-all-start.2 = ((bf16[16,176,128]{2,1,0:T(8,128)(2,1)}), bf16[16,176,128]{2,1,0:T(8,128)(2,1)S(1)}, u32[]{:S(2)}, u32[]{:S(2)}) async-start(bf16[16,176,128]{2,1,0:T(8,128)(2,1)} %get-tuple-element.48), calls=%async_computation.2 | async-start | bytes 1441792 | tf_op jit(solution)/shard_map/all_to_all | solution.py:581
  79.5 4.8 %collective-permute-start.1 = (bf16[176,128]{1,0:T(8,128)(2,1)S(1)}, bf16[176,128]{1,0:T(8,128)(2,1)S(1)}, u32[]{:S(2)}, u32[]{:S(2)}) collective-permute-start(bf16[176,128]{1,0:T(8,128)(2,1)S(1)} %get-tuple-element.53.mine_ref), channel_id=1, source_target_pairs={{0,32},{32,0},{64,96},{96,64},{128,160},{160,128},{192,224},{224,1... | collective-permute-start | bytes 135176 | tf_op jit(solution)/shard_map/ppermute | solution.py:689
  134.2 6.7 %collective-permute-start.2 = (bf16[16,224,128]{2,1,0:T(8,128)(2,1)S(1)}, bf16[16,224,128]{2,1,0:T(8,128)(2,1)S(1)}, u32[]{:S(2)}, u32[]{:S(2)}) collective-permute-start(bf16[16,224,128]{2,1,0:T(8,128)(2,1)S(1)} %all_to_all.27.mine_ref), channel_id=1, source_target_pairs={{0,1},{1,0},{2,3},{3,2},{4,5},{5,4},{6,7},{7,6},{8,9},{9,8},{10,11... | collective-permute-start | bytes 2752520 | tf_op jit(solution)/shard_map/ppermute | solution.py:585

commit v6 on v5

--- a/solution.py
+++ b/solution.py
@@ -344,6 +344,7 @@
     scr,
     out,
     small,
+    left,
 ):
     core = core_ref[0]
     scr[...] = conv_ref[...].astype(F32)
@@ -371,12 +372,14 @@
         xhat = centred * inverse
         normed = (xhat * gain + bias).astype(BF16)
         normed_ref[rows, :] = normed
+        left[0, rows, :] = normed
         pre_act = jnp.dot(normed, w_in_ref[...], preferred_element_type=F32) + b_in_ref[...]
         cdf = 0.5 * (1.0 + lax.erf(pre_act * 0.7071067811865476))
         hidden = (pre_act * cdf).astype(BF16)
         right_ref[1, rows, :] = hidden
         branch = jnp.dot(hidden, w_out_ref[...], preferred_element_type=F32) + b_out_ref[...]
         cot = cot_ref[rows, :]
+        left[1, rows, :] = cot
         output_ref[rows, :] = (image_ref[rows, :].astype(F32) + branch).astype(BF16)
         d_hidden = lax.dot_general(
             cot, w_out_ref[...], (((1,), (1,)), ((), ())), preferred_element_type=F32
@@ -402,7 +405,7 @@
     half = CHIPS * MSG
     theirs_ref[GRADS : GRADS + half, :] = out[pl.ds((1 - core) * half, half), :].astype(BF16)
     mine_ref[...] = out[pl.ds(core * half, half), :].astype(BF16)
-    weight_grads(scale, normed_ref, cot_ref, right_ref, 1 - core, theirs_ref)
+    put_grads(over_cells(left[1 - core], right_ref[1 - core]), scale, theirs_ref)
     small[...] = jnp.zeros((16, 128), F32)
     for i in range(FF // 128):
         small[i : i + 1, :] = g_b_in[:, i * 128 : (i + 1) * 128] * scale
@@ -417,23 +420,24 @@
     ).astype(BF16)
 
 
-def weight_grads(scale, normed_ref, cot_ref, right_ref, which, out_ref):
+def put_grads(grads, scale, out_ref):
+    grads = (grads * scale).astype(out_ref.dtype)
+    for i in range(CHIPS):
+        for j in range(FF // 128):
+            at = (i * (FF // 128) + j) * 16
+            out_ref[at : at + 16, :] = grads[i * 16 : (i + 1) * 16, j * 128 : (j + 1) * 128]
+
+
+def over_cells(left, right):
+    return lax.dot_general(left, right, (((0,), (0,)), ((), ())), preferred_element_type=F32)
+
+
+def own_grads_kernel(scale, core_ref, normed_ref, cot_ref, right_ref, out_ref):
     for n, left_ref in enumerate((normed_ref, cot_ref)):
 
-        @pl.when(which == n)
+        @pl.when(core_ref[0] == n)
         def _(n=n, left_ref=left_ref):
-            grads = lax.dot_general(
-                left_ref[...], right_ref[n], (((0,), (0,)), ((), ())), preferred_element_type=F32
-            )
-            grads = (grads * scale).astype(out_ref.dtype)
-            for i in range(CHIPS):
-                for j in range(FF // 128):
-                    at = (i * (FF // 128) + j) * 16
-                    out_ref[at : at + 16, :] = grads[i * 16 : (i + 1) * 16, j * 128 : (j + 1) * 128]
-
-
-def own_grads_kernel(scale, core_ref, normed_ref, cot_ref, right_ref, out_ref):
-    weight_grads(scale, normed_ref, cot_ref, right_ref, core_ref[0], out_ref)
+            put_grads(over_cells(left_ref[...], right_ref[n]), scale, out_ref)
 
 
 def merge_kernel(core_ref, mine_ref, grads_ref, small_ref, got_ref, out_hbm, small_out, rows_scr, sems):
@@ -485,13 +489,10 @@
 
     @pl.when(core == 0)
     def _():
-        copy = pltpu.make_async_copy(held, w_in_hbm, sems.at[0])
-        copy.start()
-        copy.wait()
+        pltpu.make_async_copy(held, w_in_hbm, sems.at[0]).start()
 
     @pl.when(core == 1)
     def _():
-        copies = []
         for n in range(2):
             for j in range(n * lanes // 2, (n + 1) * lanes // 2):
                 for half in range(2):
@@ -499,14 +500,24 @@
                         half * 128 : (half + 1) * 128, j * 128 : (j + 1) * 128
                     ].T
             rows = pl.ds(n * FF // 2, FF // 2)
-            copies.append(pltpu.make_async_copy(w_out.at[rows], w_out_hbm.at[rows], sems.at[n]))
-            copies[-1].start()
-        for copy in copies:
-            copy.wait()
+            pltpu.make_async_copy(w_out.at[rows], w_out_hbm.at[rows], sems.at[n]).start()
+
+
+def placed_share(core, w_in_hbm, w_out_hbm, held, w_out, sems):
+    @pl.when(core == 0)
+    def _():
+        pltpu.make_async_copy(held, w_in_hbm, sems.at[0]).wait()
+
+    @pl.when(core == 1)
+    def _():
+        for n in range(2):
+            rows = pl.ds(n * FF // 2, FF // 2)
+            pltpu.make_async_copy(w_out.at[rows], w_out_hbm.at[rows], sems.at[n]).wait()
 
 
 def own_share_kernel(core_ref, mine_ref, w_in_hbm, w_out_hbm, held, w_out, sems):
     place_share(core_ref[0], mine_ref, w_in_hbm, w_out_hbm, held, w_out, sems)
+    placed_share(core_ref[0], w_in_hbm, w_out_hbm, held, w_out, sems)
 
 
 def finish_kernel(
@@ -532,6 +543,7 @@
 ):
     del w_in_in, w_out_in
     core = core_ref[0]
+    place_share(1 - core, got_ref, w_in_hbm, w_out_hbm, held, w_out, sems)
     rest = LAST - OWN
     for i in range(CHIPS):
         for c, ref in ((core, mine_ref), (1 - core, got_ref)):
@@ -568,7 +580,7 @@
     for n, ref in enumerate((gain_ref, shift_ref, b_out_ref)):
         for i in range(2):
             ref[:, i * 128 : (i + 1) * 128] = totals[1][2 * n + i : 2 * n + i + 1]
-    place_share(1 - core, got_ref, w_in_hbm, w_out_hbm, held, w_out, sems)
+    placed_share(1 - core, w_in_hbm, w_out_hbm, held, w_out, sems)
 
 
 def messages(x):
@@ -651,7 +663,7 @@
             shape((2, CELLS, FF), BF16),
             shape((8, 128), F32),
         ),
-        [packed_f, packed_f, pltpu.VMEM((16, 128), F32)],
+        [packed_f, packed_f, pltpu.VMEM((16, 128), F32), pltpu.VMEM((2, CELLS, C), BF16)],
         [SMEM] + [VMEM] * 9,
     )(
         core,

time: 144 us -> 143 us (level)
  Pallas kernels: 19 us -> 17.4 us
where the time goes in v6:
time: 143 us; the launch traced here: 142 us
  blocking collectives  65.8 us (46%)
  waiting for transfers between devices  32.3 us (23%)
  starting transfers between devices  23.3 us (16%)
  Pallas kernels  17.4 us (12%)
    all_to_all x1, blocking collectives, between_chips(): lax.all_to_all(x, 'strip', 0, 0, axis_index_groups=groups, tiled=True)  29.3 us
    all_to_all x1, blocking collectives, local(): lax.all_to_all(copies, 'slide', 0, 0, axis_index_groups=groups, tiled=True)  20.5 us
    all_to_all x1, waiting for transfers between devices, between_chips(): lax.all_to_all(x, 'strip', 0, 0, axis_index_groups=groups, tiled=True)  20 us
    all_to_all x1, blocking collectives, messages(): x = lax.all_to_all(x.reshape(STRIPS, MSG, 128), 'strip', 0, 0, tiled=True)  16 us
    all_to_all x1, starting transfers between devices, messages(): x = lax.all_to_all(x.reshape(STRIPS, MSG, 128), 'strip', 0, 0, tiled=True)  11.2 us
    all_to_all x1, waiting for transfers between devices, messages(): x = lax.all_to_all(x.reshape(STRIPS, MSG, 128), 'strip', 0, 0, tiled=True)  8.12 us
    ppermute x2, starting transfers between devices, between_cores(): return lax.ppermute(x, 'strip', [(i, i ^ 1) for i in range(STRIPS)])  6.56 us
    all_to_all x1, starting transfers between devices, between_chips(): lax.all_to_all(x, 'strip', 0, 0, axis_index_groups=groups, tiled=True)  3.62 us
  transfers between devices with their start and end apart: 5, of which 5 were waited for; matrix products, arithmetic and copies ran while one was open for 1% of the time, Pallas kernels for 5%

profile of v6, /device:TPU:1, one launch (start us, length us, event | category | flops | bytes accessed | tf_op | source)
XLA Modules:
  0.0 142.0 jit_solution(6343351190201688019)
XLA Ops:
  0.6 0.0 copy-start
  0.7 0.0 copy-start.1
  0.7 0.0 copy-start.2
  0.7 1.0 copy-done.2
  1.7 0.9 shard_map.177
  2.6 11.2 %all-to-all-start = ((bf16[32,24,128]{2,1,0:T(8,128)(2,1)}), bf16[32,24,128]{2,1,0:T(8,128)(2,1)S(1)}, u32[]{:S(2)}, u32[]{:S(2)}) async-start(bf16[32,24,128]{2,1,0:T(8,128)(2,1)} %bitcast.1), calls=%async_computation | async-start | bytes 393216 | tf_op jit(solution)/shard_map/all_to_all | solution.py:587
  13.8 0.2 convolution_bitcast_fusion.1
  14.0 1.1 convolution_bitcast_fusion
  15.1 2.3 %shard_map.178 = (bf16[4,320,256]{2,1,0:T(8,128)(2,1)S(1)}, bf16[4,640,128]{2,1,0:T(8,128)(2,1)S(1)}) custom-call(f32[40,128]{1,0:T(8,128)S(1)} %pad.7.tall_ref, f32[40,128]{1,0:T(8,128)S(1)} %pad.8.wide_ref), custom_call_target="tpu_custom_call" | custom-call | tf_op jit(solution)/shard_map/pallas_call | solution.py:642
  17.5 8.1 %all-to-all-done = bf16[32,24,128]{2,1,0:T(8,128)(2,1)S(1)} async-done(((bf16[32,24,128]{2,1,0:T(8,128)(2,1)}), bf16[32,24,128]{2,1,0:T(8,128)(2,1)S(1)}, u32[]{:S(2)}, u32[]{:S(2)}) %all-to-all-start) | async-done | bytes 196640 | tf_op jit(solution)/shard_map/all_to_all | solution.py:587
  25.6 1.6 %shard_map.179 = (bf16[768,128]{1,0:T(8,128)(2,1)S(1)}, bf16[4,192,128]{2,1,0:T(8,128)(2,1)S(1)}) custom-call(bf16[768,128]{1,0:T(8,128)(2,1)S(1)} %bitcast.36, bf16[4,320,256]{2,1,0:T(8,128)(2,1)S(1)} %get-tuple-element.39.tall_ref, bf16[4,640,128]{2,1,0:T(8,128)(2,1)S(1)} %get-tuple-element.40.wide_ref), custom_call_target="tpu_custom_call" | custom-call | tf_op jit(solution)/shard_map/pallas_call | solution.py:647
  27.2 16.0 %all_to_all.25 = bf16[32,24,128]{2,1,0:T(8,128)(2,1)S(1)} all-to-all(bf16[32,24,128]{2,1,0:T(8,128)(2,1)S(1)} %bitcast.40), channel_id=1, replica_groups=mesh['slide'=16,'strip'=32] {'strip'}, dimensions={0} | all-to-all | bytes 393216 | tf_op jit(solution)/shard_map/all_to_all | solution.py:587
  43.2 0.0 copy-done.5
  43.2 2.8 %shard_map.180 = (bf16[384,256]{1,0:T(8,128)(2,1)}, bf16[2448,128]{1,0:T(8,128)(2,1)S(1)}, bf16[384,128]{1,0:T(8,128)(2,1)S(1)}, bf16[384,256]{1,0:T(8,128)(2,1)...) custom-call(s32[1]{0:T(128)} %bitcast.core_ref, bf16[768,128]{1,0:T(8,128)(2,1)S(1)} %bitcast.39, ...), custom_call_target="tpu_custom_call" | custom-call | tf_op jit(solution)/shard_map/pallas_call | solution.py:656
  46.1 1.9 %collective-permute-start = (bf16[2448,128]{1,0:T(8,128)(2,1)S(1)}, bf16[2448,128]{1,0:T(8,128)(2,1)S(1)}, u32[]{:S(2)}, u32[]{:S(2)}) collective-permute-start(bf16[2448,128]{1,0:T(8,128)(2,1)S(1)} %get-tuple-element.47), channel_id=1, source_target_pairs={{0,1},{1,0},{2,3},{3,2},{4,5},{5,4},{6,7},{7,6},{8,9},{9,8},{10,11... | collective-permute-start | bytes 1880072 | tf_op jit(solution)/shard_map/ppermute | solution.py:597
  48.0 0.5 shard_map.181.grads_ref
  48.5 1.5 %collective-permute-done.got_ref = bf16[2448,128]{1,0:T(8,128)(2,1)S(1)} collective-permute-done((bf16[2448,128]{1,0:T(8,128)(2,1)S(1)}, bf16[2448,128]{1,0:T(8,128)(2,1)S(1)}, u32[]{:S(2)}, u32[]{:S(2)}) %collective-permute-start) | collective-permute-done | bytes 626720 | tf_op jit(solution)/shard_map/ppermute | solution.py:597
  50.0 0.9 shard_map.182
  50.9 3.6 %all-to-all-start.2 = ((bf16[16,176,128]{2,1,0:T(8,128)(2,1)}), bf16[16,176,128]{2,1,0:T(8,128)(2,1)S(1)}, u32[]{:S(2)}, u32[]{:S(2)}) async-start(bf16[16,176,128]{2,1,0:T(8,128)(2,1)} %get-tuple-element.48), calls=%async_computation.2 | async-start | bytes 1441792 | tf_op jit(solution)/shard_map/all_to_all | solution.py:593
  54.5 1.8 %shard_map.183 = (bf16[4,5,256,128]{3,2,1,0:T(8,128)(2,1)S(1)}, bf16[4,640,128]{2,1,0:T(8,128)(2,1)S(1)}) custom-call(bf16[768,128]{1,0:T(8,128)(2,1)S(1)} %bitcast.37, f32[40,128]{1,0:T(8,128)S(1)} %pad.8.wide_ref), custom_call_target="tpu_custom_call" | custom-call | tf_op jit(solution)/shard_map/pallas_call | solution.py:691
  56.4 20.0 %all-to-all-done.2.parts_ref = bf16[16,176,128]{2,1,0:T(8,128)(2,1)S(1)} async-done(((bf16[16,176,128]{2,1,0:T(8,128)(2,1)}), bf16[16,176,128]{2,1,0:T(8,128)(2,1)S(1)}, u32[]{:S(2)}, u32[]{:S(2)}) %all-to-all-start.2) | async-done | bytes 720928 | tf_op jit(solution)/shard_map/all_to_all | solution.py:593
  76.4 2.3 %shard_map.184 = (bf16[4,192,128]{2,1,0:T(8,128)(2,1)S(1)}, bf16[176,128]{1,0:T(8,128)(2,1)S(1)}) custom-call(bf16[16,176,128]{2,1,0:T(8,128)(2,1)S(1)} %all-to-all-done.2.parts_ref, bf16[4,5,256,128]{3,2,1,0:T(8,128)(2,1)S(1)} %get-tuple-element.49.shifted_ref, bf16[4,192,128]{2,1,0:T(8,128)(2,1)S(1)} %get-tuple-element.50.mixed_ref, ...), custom_call_target="tpu_custom_call" | custom-call | tf_op jit(solution)/shard_map/pallas_call | solution.py:696
  78.7 1.9 %collective-permute-start.1 = (bf16[176,128]{1,0:T(8,128)(2,1)S(1)}, bf16[176,128]{1,0:T(8,128)(2,1)S(1)}, u32[]{:S(2)}, u32[]{:S(2)}) collective-permute-start(bf16[176,128]{1,0:T(8,128)(2,1)S(1)} %get-tuple-element.53.mine_ref), channel_id=1, source_target_pairs={{0,32},{32,0},{64,96},{96,64},{128,160},{160,128},{192,224},{224,1... | collective-permute-start | bytes 135176 | tf_op jit(solution)/shard_map/ppermute | solution.py:701
  80.6 1.0 shard_map.185.d_image_ref
  81.6 1.8 %collective-permute-done.1.got_ref = bf16[176,128]{1,0:T(8,128)(2,1)S(1)} collective-permute-done((bf16[176,128]{1,0:T(8,128)(2,1)S(1)}, bf16[176,128]{1,0:T(8,128)(2,1)S(1)}, u32[]{:S(2)}, u32[]{:S(2)}) %collective-permute-start.1) | collective-permute-done | bytes 45088 | tf_op jit(solution)/shard_map/ppermute | solution.py:701
  83.5 20.5 %all_to_all.26.parts_ref = bf16[8,176,128]{2,1,0:T(8,128)(2,1)S(1)} all-to-all(bf16[8,176,128]{2,1,0:T(8,128)(2,1)S(1)} %shard_map.186), channel_id=1, replica_groups={{0,64,128,192,256,320,384,448},{32,96,160,224,288,352,416,480},{1,65,12..., dimensions={0} | all-to-all | bytes 720896 | tf_op jit(solution)/shard_map/all_to_all | solution.py:707
  103.9 0.1 shard_map.187
  104.0 29.3 %all_to_all.27.mine_ref = bf16[16,224,128]{2,1,0:T(8,128)(2,1)S(1)} all-to-all(bf16[16,224,128]{2,1,0:T(8,128)(2,1)S(1)} %shard_map.187), channel_id=1, replica_groups={{0,2,4,6,8,10,12,14,16,18,20,22,24,26,28,30},{1,3,5,7,9,11,13,15,17,19,..., dimensions={0} | all-to-all | bytes 1835008 | tf_op jit(solution)/shard_map/all_to_all | solution.py:593
  133.4 4.6 %collective-permute-start.2 = (bf16[16,224,128]{2,1,0:T(8,128)(2,1)S(1)}, bf16[16,224,128]{2,1,0:T(8,128)(2,1)S(1)}, u32[]{:S(2)}, u32[]{:S(2)}) collective-permute-start(bf16[16,224,128]{2,1,0:T(8,128)(2,1)S(1)} %all_to_all.27.mine_ref), channel_id=1, source_target_pairs={{0,1},{1,0},{2,3},{3,2},{4,5},{5,4},{6,7},{7,6},{8,9},{9,8},{10,11... | collective-permute-start | bytes 2752520 | tf_op jit(solution)/shard_map/ppermute | solution.py:597
  138.0 1.3 shard_map.188
  139.3 0.8 collective-permute-done.2.got_ref
  140.1 1.9 %shard_map.189 = (bf16[6,64,256]{2,1,0:T(8,128)(2,1)}, f32[5,51,256]{2,1,0:T(8,128)}, f32[5,51,256]{2,1,0:T(8,128)}, f32[1,256]{1,0:T(1,128)}, f32[1,256]{1,0:T(...) custom-call(s32[1]{0:T(128)} %bitcast.core_ref, ...), custom_call_target="tpu_custom_call", output_to_operand_aliasing={{5}: (4, {}), {7}: (5, {})} | custom-call | tf_op jit(solution)/shard_map/pallas_call | solution.py:719
  (19 shorter events, 0.1 us)
Async XLA Ops:
  0.6 13.2 %copy-start = (bf16[51,5,256]{2,0,1:T(8,128)(2,1)S(1)}, bf16[51,5,256]{2,0,1:T(8,128)(2,1)}, u32[]{:S(2)}) copy-start(bf16[51,5,256]{2,0,1:T(8,128)(2,1)} %param.12) | copy-start | bytes 391684
  0.7 42.5 %copy-start.1 = (bf16[1,6,64,256]{3,2,1,0:T(8,128)(2,1)S(1)}, bf16[1,6,64,256]{3,2,1,0:T(8,128)(2,1)}, u32[]{:S(2)}) copy-start(bf16[1,6,64,256]{3,2,1,0:T(8,128)(2,1)} %param.11) | copy-start | bytes 589828
  0.7 1.0 copy-start.2
  1.6 41.5 %copy-start.3 = (bf16[1,6,64,256]{3,2,1,0:T(8,128)(2,1)S(1)}, bf16[1,6,64,256]{3,2,1,0:T(8,128)(2,1)}, u32[]{:S(2)}) copy-start(bf16[1,6,64,256]{3,2,1,0:T(8,128)(2,1)} %image_ref.1) | copy-start | bytes 589828
  1.6 41.5 %copy-start.4 = (bf16[256,1024]{1,0:T(8,128)(2,1)S(1)}, bf16[256,1024]{1,0:T(8,128)(2,1)}, u32[]{:S(2)}) copy-start(bf16[256,1024]{1,0:T(8,128)(2,1)} %w_in_ref.1) | copy-start | bytes 1572868
  1.6 41.5 %copy-start.5 = (bf16[1024,256]{1,0:T(8,128)(2,1)S(1)}, bf16[1024,256]{1,0:T(8,128)(2,1)}, u32[]{:S(2)}) copy-start(bf16[1024,256]{1,0:T(8,128)(2,1)} %w_out_ref.1) | copy-start | bytes 1572868
  1.7 41.5 %copy-start.6 = (f32[1024]{0:T(1024)S(1)}, f32[1024]{0:T(1024)}, u32[]{:S(2)}) copy-start(f32[1024]{0:T(1024)} %param.17) | copy-start | bytes 12292
  1.7 41.6 %copy-start.7 = (f32[256]{0:T(256)S(1)}, f32[256]{0:T(256)}, u32[]{:S(2)}) copy-start(f32[256]{0:T(256)} %param.14) | copy-start | bytes 3076
  1.7 41.6 %copy-start.8 = (f32[256]{0:T(256)S(1)}, f32[256]{0:T(256)}, u32[]{:S(2)}) copy-start(f32[256]{0:T(256)} %param.15) | copy-start | bytes 3076
  1.7 41.6 %copy-start.9 = (f32[256]{0:T(256)S(1)}, f32[256]{0:T(256)}, u32[]{:S(2)}) copy-start(f32[256]{0:T(256)} %param.19) | copy-start | bytes 3076
  2.6 23.0 %all-to-all-start = ((bf16[32,24,128]{2,1,0:T(8,128)(2,1)}), bf16[32,24,128]{2,1,0:T(8,128)(2,1)S(1)}, u32[]{:S(2)}, u32[]{:S(2)}) async-start(bf16[32,24,128]{2,1,0:T(8,128)(2,1)} %bitcast.1), calls=%async_computation | async-start | bytes 393216 | tf_op jit(solution)/shard_map/all_to_all | solution.py:587
  46.1 3.9 %collective-permute-start = (bf16[2448,128]{1,0:T(8,128)(2,1)S(1)}, bf16[2448,128]{1,0:T(8,128)(2,1)S(1)}, u32[]{:S(2)}, u32[]{:S(2)}) collective-permute-start(bf16[2448,128]{1,0:T(8,128)(2,1)S(1)} %get-tuple-element.47), channel_id=1, source_target_pairs={{0,1},{1,0},{2,3},{3,2},{4,5},{5,4},{6,7},{7,6},{8,9},{9,8},{10,11... | collective-permute-start | bytes 1880072 | tf_op jit(solution)/shard_map/ppermute | solution.py:597
  50.9 25.5 %all-to-all-start.2 = ((bf16[16,176,128]{2,1,0:T(8,128)(2,1)}), bf16[16,176,128]{2,1,0:T(8,128)(2,1)S(1)}, u32[]{:S(2)}, u32[]{:S(2)}) async-start(bf16[16,176,128]{2,1,0:T(8,128)(2,1)} %get-tuple-element.48), calls=%async_computation.2 | async-start | bytes 1441792 | tf_op jit(solution)/shard_map/all_to_all | solution.py:593
  78.7 4.8 %collective-permute-start.1 = (bf16[176,128]{1,0:T(8,128)(2,1)S(1)}, bf16[176,128]{1,0:T(8,128)(2,1)S(1)}, u32[]{:S(2)}, u32[]{:S(2)}) collective-permute-start(bf16[176,128]{1,0:T(8,128)(2,1)S(1)} %get-tuple-element.53.mine_ref), channel_id=1, source_target_pairs={{0,32},{32,0},{64,96},{96,64},{128,160},{160,128},{192,224},{224,1... | collective-permute-start | bytes 135176 | tf_op jit(solution)/shard_map/ppermute | solution.py:701
  133.4 6.7 %collective-permute-start.2 = (bf16[16,224,128]{2,1,0:T(8,128)(2,1)S(1)}, bf16[16,224,128]{2,1,0:T(8,128)(2,1)S(1)}, u32[]{:S(2)}, u32[]{:S(2)}) collective-permute-start(bf16[16,224,128]{2,1,0:T(8,128)(2,1)S(1)} %all_to_all.27.mine_ref), channel_id=1, source_target_pairs={{0,1},{1,0},{2,3},{3,2},{4,5},{5,4},{6,7},{7,6},{8,9},{9,8},{10,11... | collective-permute-start | bytes 2752520 | tf_op jit(solution)/shard_map/ppermute | solution.py:597

commit v7 on v6

--- a/solution.py
+++ b/solution.py
@@ -351,7 +351,7 @@
     gain, bias = gain_ref[...], bias_ref[...]
     sums = [jnp.zeros((1, C), F32), jnp.zeros((1, C), F32), jnp.zeros((1, C), F32)]
     g_b_in = jnp.zeros((1, FF), F32)
-    step = 2
+    step = 6
     for k in range(0, ROWS, step):
         rows = slice(k * COLS, (k + step) * COLS)
         conv = jnp.concatenate(

time: 143 us -> 142 us (level)
  no operation moved by 1% of the time
where the time goes in v7:
time: 142 us
  blocking collectives  65.8 us (46%)
  waiting for transfers between devices  32.3 us (23%)
  starting transfers between devices  23.3 us (16%)
  Pallas kernels  17.3 us (12%)
    all_to_all x1, blocking collectives, between_chips(): lax.all_to_all(x, 'strip', 0, 0, axis_index_groups=groups, tiled=True)  29.3 us
    all_to_all x1, blocking collectives, local(): lax.all_to_all(copies, 'slide', 0, 0, axis_index_groups=groups, tiled=True)  20.5 us
    all_to_all x1, waiting for transfers between devices, between_chips(): lax.all_to_all(x, 'strip', 0, 0, axis_index_groups=groups, tiled=True)  20 us
    all_to_all x1, blocking collectives, messages(): x = lax.all_to_all(x.reshape(STRIPS, MSG, 128), 'strip', 0, 0, tiled=True)  16 us
    all_to_all x1, starting transfers between devices, messages(): x = lax.all_to_all(x.reshape(STRIPS, MSG, 128), 'strip', 0, 0, tiled=True)  11.2 us
    all_to_all x1, waiting for transfers between devices, messages(): x = lax.all_to_all(x.reshape(STRIPS, MSG, 128), 'strip', 0, 0, tiled=True)  8.12 us
    ppermute x2, starting transfers between devices, between_cores(): return lax.ppermute(x, 'strip', [(i, i ^ 1) for i in range(STRIPS)])  6.51 us
    all_to_all x1, starting transfers between devices, between_chips(): lax.all_to_all(x, 'strip', 0, 0, axis_index_groups=groups, tiled=True)  3.62 us
  transfers between devices with their start and end apart: 5, of which 5 were waited for; matrix products, arithmetic and copies ran while one was open for 1% of the time, Pallas kernels for 5%

profile of v7, /device:TPU:1, one launch (start us, length us, event | category | flops | bytes accessed | tf_op | source)
XLA Modules:
  0.0 141.8 jit_solution(7778696043836236521)
XLA Ops:
  0.6 0.0 copy-start
  0.7 0.0 copy-start.1
  0.7 0.0 copy-start.2
  0.7 1.0 copy-done.2
  1.7 0.0 copy-start.7
  1.7 0.9 shard_map.177
  2.6 11.2 %all-to-all-start = ((bf16[32,24,128]{2,1,0:T(8,128)(2,1)}), bf16[32,24,128]{2,1,0:T(8,128)(2,1)S(1)}, u32[]{:S(2)}, u32[]{:S(2)}) async-start(bf16[32,24,128]{2,1,0:T(8,128)(2,1)} %bitcast.1), calls=%async_computation | async-start | bytes 393216 | tf_op jit(solution)/shard_map/all_to_all | solution.py:587
  13.8 0.2 convolution_bitcast_fusion.1
  14.0 1.1 convolution_bitcast_fusion
  15.1 2.3 %shard_map.178 = (bf16[4,320,256]{2,1,0:T(8,128)(2,1)S(1)}, bf16[4,640,128]{2,1,0:T(8,128)(2,1)S(1)}) custom-call(f32[40,128]{1,0:T(8,128)S(1)} %pad.7.tall_ref, f32[40,128]{1,0:T(8,128)S(1)} %pad.8.wide_ref), custom_call_target="tpu_custom_call" | custom-call | tf_op jit(solution)/shard_map/pallas_call | solution.py:642
  17.5 8.1 %all-to-all-done = bf16[32,24,128]{2,1,0:T(8,128)(2,1)S(1)} async-done(((bf16[32,24,128]{2,1,0:T(8,128)(2,1)}), bf16[32,24,128]{2,1,0:T(8,128)(2,1)S(1)}, u32[]{:S(2)}, u32[]{:S(2)}) %all-to-all-start) | async-done | bytes 196640 | tf_op jit(solution)/shard_map/all_to_all | solution.py:587
  25.6 1.6 %shard_map.179 = (bf16[768,128]{1,0:T(8,128)(2,1)S(1)}, bf16[4,192,128]{2,1,0:T(8,128)(2,1)S(1)}) custom-call(bf16[768,128]{1,0:T(8,128)(2,1)S(1)} %bitcast.36, bf16[4,320,256]{2,1,0:T(8,128)(2,1)S(1)} %get-tuple-element.39.tall_ref, bf16[4,640,128]{2,1,0:T(8,128)(2,1)S(1)} %get-tuple-element.40.wide_ref), custom_call_target="tpu_custom_call" | custom-call | tf_op jit(solution)/shard_map/pallas_call | solution.py:647
  27.2 16.0 %all_to_all.25 = bf16[32,24,128]{2,1,0:T(8,128)(2,1)S(1)} all-to-all(bf16[32,24,128]{2,1,0:T(8,128)(2,1)S(1)} %bitcast.40), channel_id=1, replica_groups=mesh['slide'=16,'strip'=32] {'strip'}, dimensions={0} | all-to-all | bytes 393216 | tf_op jit(solution)/shard_map/all_to_all | solution.py:587
  43.2 2.7 %shard_map.180 = (bf16[384,256]{1,0:T(8,128)(2,1)}, bf16[2448,128]{1,0:T(8,128)(2,1)S(1)}, bf16[384,128]{1,0:T(8,128)(2,1)S(1)}, bf16[384,256]{1,0:T(8,128)(2,1)...) custom-call(s32[1]{0:T(128)} %bitcast.core_ref, bf16[768,128]{1,0:T(8,128)(2,1)S(1)} %bitcast.39, ...), custom_call_target="tpu_custom_call" | custom-call | tf_op jit(solution)/shard_map/pallas_call | solution.py:656
  45.9 1.9 %collective-permute-start = (bf16[2448,128]{1,0:T(8,128)(2,1)S(1)}, bf16[2448,128]{1,0:T(8,128)(2,1)S(1)}, u32[]{:S(2)}, u32[]{:S(2)}) collective-permute-start(bf16[2448,128]{1,0:T(8,128)(2,1)S(1)} %get-tuple-element.47), channel_id=1, source_target_pairs={{0,1},{1,0},{2,3},{3,2},{4,5},{5,4},{6,7},{7,6},{8,9},{9,8},{10,11... | collective-permute-start | bytes 1880072 | tf_op jit(solution)/shard_map/ppermute | solution.py:597
  47.9 0.5 shard_map.181.grads_ref
  48.3 1.5 %collective-permute-done.got_ref = bf16[2448,128]{1,0:T(8,128)(2,1)S(1)} collective-permute-done((bf16[2448,128]{1,0:T(8,128)(2,1)S(1)}, bf16[2448,128]{1,0:T(8,128)(2,1)S(1)}, u32[]{:S(2)}, u32[]{:S(2)}) %collective-permute-start) | collective-permute-done | bytes 626720 | tf_op jit(solution)/shard_map/ppermute | solution.py:597
  49.8 0.9 shard_map.182
  50.8 3.6 %all-to-all-start.2 = ((bf16[16,176,128]{2,1,0:T(8,128)(2,1)}), bf16[16,176,128]{2,1,0:T(8,128)(2,1)S(1)}, u32[]{:S(2)}, u32[]{:S(2)}) async-start(bf16[16,176,128]{2,1,0:T(8,128)(2,1)} %get-tuple-element.48), calls=%async_computation.2 | async-start | bytes 1441792 | tf_op jit(solution)/shard_map/all_to_all | solution.py:593
  54.4 1.8 %shard_map.183 = (bf16[4,5,256,128]{3,2,1,0:T(8,128)(2,1)S(1)}, bf16[4,640,128]{2,1,0:T(8,128)(2,1)S(1)}) custom-call(bf16[768,128]{1,0:T(8,128)(2,1)S(1)} %bitcast.37, f32[40,128]{1,0:T(8,128)S(1)} %pad.8.wide_ref), custom_call_target="tpu_custom_call" | custom-call | tf_op jit(solution)/shard_map/pallas_call | solution.py:691
  56.3 20.0 %all-to-all-done.2.parts_ref = bf16[16,176,128]{2,1,0:T(8,128)(2,1)S(1)} async-done(((bf16[16,176,128]{2,1,0:T(8,128)(2,1)}), bf16[16,176,128]{2,1,0:T(8,128)(2,1)S(1)}, u32[]{:S(2)}, u32[]{:S(2)}) %all-to-all-start.2) | async-done | bytes 720928 | tf_op jit(solution)/shard_map/all_to_all | solution.py:593
  76.3 2.3 %shard_map.184 = (bf16[4,192,128]{2,1,0:T(8,128)(2,1)S(1)}, bf16[176,128]{1,0:T(8,128)(2,1)S(1)}) custom-call(bf16[16,176,128]{2,1,0:T(8,128)(2,1)S(1)} %all-to-all-done.2.parts_ref, bf16[4,5,256,128]{3,2,1,0:T(8,128)(2,1)S(1)} %get-tuple-element.49.shifted_ref, bf16[4,192,128]{2,1,0:T(8,128)(2,1)S(1)} %get-tuple-element.50.mixed_ref, ...), custom_call_target="tpu_custom_call" | custom-call | tf_op jit(solution)/shard_map/pallas_call | solution.py:696
  78.5 1.9 %collective-permute-start.1 = (bf16[176,128]{1,0:T(8,128)(2,1)S(1)}, bf16[176,128]{1,0:T(8,128)(2,1)S(1)}, u32[]{:S(2)}, u32[]{:S(2)}) collective-permute-start(bf16[176,128]{1,0:T(8,128)(2,1)S(1)} %get-tuple-element.53.mine_ref), channel_id=1, source_target_pairs={{0,32},{32,0},{64,96},{96,64},{128,160},{160,128},{192,224},{224,1... | collective-permute-start | bytes 135176 | tf_op jit(solution)/shard_map/ppermute | solution.py:701
  80.4 1.0 shard_map.185.d_image_ref
  81.5 1.8 %collective-permute-done.1.got_ref = bf16[176,128]{1,0:T(8,128)(2,1)S(1)} collective-permute-done((bf16[176,128]{1,0:T(8,128)(2,1)S(1)}, bf16[176,128]{1,0:T(8,128)(2,1)S(1)}, u32[]{:S(2)}, u32[]{:S(2)}) %collective-permute-start.1) | collective-permute-done | bytes 45088 | tf_op jit(solution)/shard_map/ppermute | solution.py:701
  83.3 20.5 %all_to_all.26.parts_ref = bf16[8,176,128]{2,1,0:T(8,128)(2,1)S(1)} all-to-all(bf16[8,176,128]{2,1,0:T(8,128)(2,1)S(1)} %shard_map.186), channel_id=1, replica_groups={{0,64,128,192,256,320,384,448},{32,96,160,224,288,352,416,480},{1,65,12..., dimensions={0} | all-to-all | bytes 720896 | tf_op jit(solution)/shard_map/all_to_all | solution.py:707
  103.8 0.1 shard_map.187
  103.9 29.3 %all_to_all.27.mine_ref = bf16[16,224,128]{2,1,0:T(8,128)(2,1)S(1)} all-to-all(bf16[16,224,128]{2,1,0:T(8,128)(2,1)S(1)} %shard_map.187), channel_id=1, replica_groups={{0,2,4,6,8,10,12,14,16,18,20,22,24,26,28,30},{1,3,5,7,9,11,13,15,17,19,..., dimensions={0} | all-to-all | bytes 1835008 | tf_op jit(solution)/shard_map/all_to_all | solution.py:593
  133.2 4.6 %collective-permute-start.2 = (bf16[16,224,128]{2,1,0:T(8,128)(2,1)S(1)}, bf16[16,224,128]{2,1,0:T(8,128)(2,1)S(1)}, u32[]{:S(2)}, u32[]{:S(2)}) collective-permute-start(bf16[16,224,128]{2,1,0:T(8,128)(2,1)S(1)} %all_to_all.27.mine_ref), channel_id=1, source_target_pairs={{0,1},{1,0},{2,3},{3,2},{4,5},{5,4},{6,7},{7,6},{8,9},{9,8},{10,11... | collective-permute-start | bytes 2752520 | tf_op jit(solution)/shard_map/ppermute | solution.py:597
  137.8 1.3 shard_map.188
  139.1 0.8 collective-permute-done.2.got_ref
  139.9 1.9 %shard_map.189 = (bf16[6,64,256]{2,1,0:T(8,128)(2,1)}, f32[5,51,256]{2,1,0:T(8,128)}, f32[5,51,256]{2,1,0:T(8,128)}, f32[1,256]{1,0:T(1,128)}, f32[1,256]{1,0:T(...) custom-call(s32[1]{0:T(128)} %bitcast.core_ref, ...), custom_call_target="tpu_custom_call", output_to_operand_aliasing={{5}: (4, {}), {7}: (5, {})} | custom-call | tf_op jit(solution)/shard_map/pallas_call | solution.py:719
  (19 shorter events, 0.1 us)
Async XLA Ops:
  0.6 13.2 %copy-start = (bf16[51,5,256]{2,0,1:T(8,128)(2,1)S(1)}, bf16[51,5,256]{2,0,1:T(8,128)(2,1)}, u32[]{:S(2)}) copy-start(bf16[51,5,256]{2,0,1:T(8,128)(2,1)} %param.12) | copy-start | bytes 391684
  0.7 42.5 %copy-start.1 = (bf16[1,6,64,256]{3,2,1,0:T(8,128)(2,1)S(1)}, bf16[1,6,64,256]{3,2,1,0:T(8,128)(2,1)}, u32[]{:S(2)}) copy-start(bf16[1,6,64,256]{3,2,1,0:T(8,128)(2,1)} %param.11) | copy-start | bytes 589828
  0.7 1.0 copy-start.2
  1.6 41.5 %copy-start.3 = (bf16[1,6,64,256]{3,2,1,0:T(8,128)(2,1)S(1)}, bf16[1,6,64,256]{3,2,1,0:T(8,128)(2,1)}, u32[]{:S(2)}) copy-start(bf16[1,6,64,256]{3,2,1,0:T(8,128)(2,1)} %image_ref.1) | copy-start | bytes 589828
  1.6 41.5 %copy-start.4 = (bf16[256,1024]{1,0:T(8,128)(2,1)S(1)}, bf16[256,1024]{1,0:T(8,128)(2,1)}, u32[]{:S(2)}) copy-start(bf16[256,1024]{1,0:T(8,128)(2,1)} %w_in_ref.1) | copy-start | bytes 1572868
  1.6 41.5 %copy-start.5 = (bf16[1024,256]{1,0:T(8,128)(2,1)S(1)}, bf16[1024,256]{1,0:T(8,128)(2,1)}, u32[]{:S(2)}) copy-start(bf16[1024,256]{1,0:T(8,128)(2,1)} %w_out_ref.1) | copy-start | bytes 1572868
  1.7 41.5 %copy-start.6 = (f32[1024]{0:T(1024)S(1)}, f32[1024]{0:T(1024)}, u32[]{:S(2)}) copy-start(f32[1024]{0:T(1024)} %param.17) | copy-start | bytes 12292
  1.7 41.6 %copy-start.7 = (f32[256]{0:T(256)S(1)}, f32[256]{0:T(256)}, u32[]{:S(2)}) copy-start(f32[256]{0:T(256)} %param.14) | copy-start | bytes 3076
  1.7 41.6 %copy-start.8 = (f32[256]{0:T(256)S(1)}, f32[256]{0:T(256)}, u32[]{:S(2)}) copy-start(f32[256]{0:T(256)} %param.15) | copy-start | bytes 3076
  1.7 41.6 %copy-start.9 = (f32[256]{0:T(256)S(1)}, f32[256]{0:T(256)}, u32[]{:S(2)}) copy-start(f32[256]{0:T(256)} %param.19) | copy-start | bytes 3076
  2.6 23.0 %all-to-all-start = ((bf16[32,24,128]{2,1,0:T(8,128)(2,1)}), bf16[32,24,128]{2,1,0:T(8,128)(2,1)S(1)}, u32[]{:S(2)}, u32[]{:S(2)}) async-start(bf16[32,24,128]{2,1,0:T(8,128)(2,1)} %bitcast.1), calls=%async_computation | async-start | bytes 393216 | tf_op jit(solution)/shard_map/all_to_all | solution.py:587
  45.9 3.9 %collective-permute-start = (bf16[2448,128]{1,0:T(8,128)(2,1)S(1)}, bf16[2448,128]{1,0:T(8,128)(2,1)S(1)}, u32[]{:S(2)}, u32[]{:S(2)}) collective-permute-start(bf16[2448,128]{1,0:T(8,128)(2,1)S(1)} %get-tuple-element.47), channel_id=1, source_target_pairs={{0,1},{1,0},{2,3},{3,2},{4,5},{5,4},{6,7},{7,6},{8,9},{9,8},{10,11... | collective-permute-start | bytes 1880072 | tf_op jit(solution)/shard_map/ppermute | solution.py:597
  50.8 25.5 %all-to-all-start.2 = ((bf16[16,176,128]{2,1,0:T(8,128)(2,1)}), bf16[16,176,128]{2,1,0:T(8,128)(2,1)S(1)}, u32[]{:S(2)}, u32[]{:S(2)}) async-start(bf16[16,176,128]{2,1,0:T(8,128)(2,1)} %get-tuple-element.48), calls=%async_computation.2 | async-start | bytes 1441792 | tf_op jit(solution)/shard_map/all_to_all | solution.py:593
  78.5 4.8 %collective-permute-start.1 = (bf16[176,128]{1,0:T(8,128)(2,1)S(1)}, bf16[176,128]{1,0:T(8,128)(2,1)S(1)}, u32[]{:S(2)}, u32[]{:S(2)}) collective-permute-start(bf16[176,128]{1,0:T(8,128)(2,1)S(1)} %get-tuple-element.53.mine_ref), channel_id=1, source_target_pairs={{0,32},{32,0},{64,96},{96,64},{128,160},{160,128},{192,224},{224,1... | collective-permute-start | bytes 135176 | tf_op jit(solution)/shard_map/ppermute | solution.py:701
  133.2 6.7 %collective-permute-start.2 = (bf16[16,224,128]{2,1,0:T(8,128)(2,1)S(1)}, bf16[16,224,128]{2,1,0:T(8,128)(2,1)S(1)}, u32[]{:S(2)}, u32[]{:S(2)}) collective-permute-start(bf16[16,224,128]{2,1,0:T(8,128)(2,1)S(1)} %all_to_all.27.mine_ref), channel_id=1, source_target_pairs={{0,1},{1,0},{2,3},{3,2},{4,5},{5,4},{6,7},{7,6},{8,9},{9,8},{10,11... | collective-permute-start | bytes 2752520 | tf_op jit(solution)/shard_map/ppermute | solution.py:597

commit v8 on v7

--- a/solution.py
+++ b/solution.py
@@ -57,7 +57,8 @@
 
 
 def turned_rows(block):
-    return jnp.concatenate([block[:, :128], block[:, 128:]], axis=0).T
+    block = block.astype(BF16)
+    return jnp.concatenate([block[:, :128], block[:, 128:]], axis=0).T.astype(F32)
 
 
 def put_by_strip(block, k, scr):
@@ -76,7 +77,7 @@
 
 
 def untwisted(parts):
-    rows = jnp.concatenate(parts, axis=0).T
+    rows = jnp.concatenate(parts, axis=0).astype(BF16).T.astype(F32)
     return jnp.concatenate([rows[:COLS], rows[COLS:]], axis=1)
 
 

time: 142 us -> 142 us (level)
  no operation moved by 1% of the time
where the time goes in v8:
time: 142 us; the launch traced here: 141 us
  blocking collectives  65.8 us (46%)
  waiting for transfers between devices  32.3 us (23%)
  starting transfers between devices  23.3 us (16%)
  Pallas kernels  16.9 us (12%)
    all_to_all x1, blocking collectives, between_chips(): lax.all_to_all(x, 'strip', 0, 0, axis_index_groups=groups, tiled=True)  29.4 us
    all_to_all x1, blocking collectives, local(): lax.all_to_all(copies, 'slide', 0, 0, axis_index_groups=groups, tiled=True)  20.5 us
    all_to_all x1, waiting for transfers between devices, between_chips(): lax.all_to_all(x, 'strip', 0, 0, axis_index_groups=groups, tiled=True)  20 us
    all_to_all x1, blocking collectives, messages(): x = lax.all_to_all(x.reshape(STRIPS, MSG, 128), 'strip', 0, 0, tiled=True)  16 us
    all_to_all x1, starting transfers between devices, messages(): x = lax.all_to_all(x.reshape(STRIPS, MSG, 128), 'strip', 0, 0, tiled=True)  11.2 us
    all_to_all x1, waiting for transfers between devices, messages(): x = lax.all_to_all(x.reshape(STRIPS, MSG, 128), 'strip', 0, 0, tiled=True)  8.12 us
    ppermute x2, starting transfers between devices, between_cores(): return lax.ppermute(x, 'strip', [(i, i ^ 1) for i in range(STRIPS)])  6.51 us
    all_to_all x1, starting transfers between devices, between_chips(): lax.all_to_all(x, 'strip', 0, 0, axis_index_groups=groups, tiled=True)  3.62 us
  transfers between devices with their start and end apart: 5, of which 5 were waited for; matrix products, arithmetic and copies ran while one was open for 1% of the time, Pallas kernels for 5%

profile of v8, /device:TPU:1, one launch (start us, length us, event | category | flops | bytes accessed | tf_op | source)
XLA Modules:
  0.0 141.5 jit_solution(3730928028583144102)
XLA Ops:
  0.6 0.0 copy-start
  0.7 0.0 copy-start.1
  0.7 0.0 copy-start.2
  0.7 1.0 copy-done.2
  1.7 0.0 copy-start.7
  1.7 0.9 shard_map.177
  2.5 11.2 %all-to-all-start = ((bf16[32,24,128]{2,1,0:T(8,128)(2,1)}), bf16[32,24,128]{2,1,0:T(8,128)(2,1)S(1)}, u32[]{:S(2)}, u32[]{:S(2)}) async-start(bf16[32,24,128]{2,1,0:T(8,128)(2,1)} %bitcast.1), calls=%async_computation | async-start | bytes 393216 | tf_op jit(solution)/shard_map/all_to_all | solution.py:588
  13.8 0.2 convolution_bitcast_fusion.1
  14.0 1.1 convolution_bitcast_fusion
  15.1 2.3 %shard_map.178 = (bf16[4,320,256]{2,1,0:T(8,128)(2,1)S(1)}, bf16[4,640,128]{2,1,0:T(8,128)(2,1)S(1)}) custom-call(f32[40,128]{1,0:T(8,128)S(1)} %pad.7.tall_ref, f32[40,128]{1,0:T(8,128)S(1)} %pad.8.wide_ref), custom_call_target="tpu_custom_call" | custom-call | tf_op jit(solution)/shard_map/pallas_call | solution.py:643
  17.5 8.1 %all-to-all-done = bf16[32,24,128]{2,1,0:T(8,128)(2,1)S(1)} async-done(((bf16[32,24,128]{2,1,0:T(8,128)(2,1)}), bf16[32,24,128]{2,1,0:T(8,128)(2,1)S(1)}, u32[]{:S(2)}, u32[]{:S(2)}) %all-to-all-start) | async-done | bytes 196640 | tf_op jit(solution)/shard_map/all_to_all | solution.py:588
  25.6 1.6 %shard_map.179 = (bf16[768,128]{1,0:T(8,128)(2,1)S(1)}, bf16[4,192,128]{2,1,0:T(8,128)(2,1)S(1)}) custom-call(bf16[768,128]{1,0:T(8,128)(2,1)S(1)} %bitcast.36, bf16[4,320,256]{2,1,0:T(8,128)(2,1)S(1)} %get-tuple-element.39.tall_ref, bf16[4,640,128]{2,1,0:T(8,128)(2,1)S(1)} %get-tuple-element.40.wide_ref), custom_call_target="tpu_custom_call" | custom-call | tf_op jit(solution)/shard_map/pallas_call | solution.py:648
  27.2 16.0 %all_to_all.25 = bf16[32,24,128]{2,1,0:T(8,128)(2,1)S(1)} all-to-all(bf16[32,24,128]{2,1,0:T(8,128)(2,1)S(1)} %bitcast.40), channel_id=1, replica_groups=mesh['slide'=16,'strip'=32] {'strip'}, dimensions={0} | all-to-all | bytes 393216 | tf_op jit(solution)/shard_map/all_to_all | solution.py:588
  43.2 2.3 %shard_map.180 = (bf16[384,256]{1,0:T(8,128)(2,1)}, bf16[2448,128]{1,0:T(8,128)(2,1)S(1)}, bf16[384,128]{1,0:T(8,128)(2,1)S(1)}, bf16[384,256]{1,0:T(8,128)(2,1)...) custom-call(s32[1]{0:T(128)} %bitcast.core_ref, bf16[768,128]{1,0:T(8,128)(2,1)S(1)} %bitcast.39, ...), custom_call_target="tpu_custom_call" | custom-call | tf_op jit(solution)/shard_map/pallas_call | solution.py:657
  45.5 1.9 %collective-permute-start = (bf16[2448,128]{1,0:T(8,128)(2,1)S(1)}, bf16[2448,128]{1,0:T(8,128)(2,1)S(1)}, u32[]{:S(2)}, u32[]{:S(2)}) collective-permute-start(bf16[2448,128]{1,0:T(8,128)(2,1)S(1)} %get-tuple-element.47), channel_id=1, source_target_pairs={{0,1},{1,0},{2,3},{3,2},{4,5},{5,4},{6,7},{7,6},{8,9},{9,8},{10,11... | collective-permute-start | bytes 1880072 | tf_op jit(solution)/shard_map/ppermute | solution.py:598
  47.5 0.5 shard_map.181.grads_ref
  48.0 1.5 %collective-permute-done.got_ref = bf16[2448,128]{1,0:T(8,128)(2,1)S(1)} collective-permute-done((bf16[2448,128]{1,0:T(8,128)(2,1)S(1)}, bf16[2448,128]{1,0:T(8,128)(2,1)S(1)}, u32[]{:S(2)}, u32[]{:S(2)}) %collective-permute-start) | collective-permute-done | bytes 626720 | tf_op jit(solution)/shard_map/ppermute | solution.py:598
  49.5 0.9 shard_map.182
  50.4 3.6 %all-to-all-start.2 = ((bf16[16,176,128]{2,1,0:T(8,128)(2,1)}), bf16[16,176,128]{2,1,0:T(8,128)(2,1)S(1)}, u32[]{:S(2)}, u32[]{:S(2)}) async-start(bf16[16,176,128]{2,1,0:T(8,128)(2,1)} %get-tuple-element.48), calls=%async_computation.2 | async-start | bytes 1441792 | tf_op jit(solution)/shard_map/all_to_all | solution.py:594
  54.0 1.8 %shard_map.183 = (bf16[4,5,256,128]{3,2,1,0:T(8,128)(2,1)S(1)}, bf16[4,640,128]{2,1,0:T(8,128)(2,1)S(1)}) custom-call(bf16[768,128]{1,0:T(8,128)(2,1)S(1)} %bitcast.37, f32[40,128]{1,0:T(8,128)S(1)} %pad.8.wide_ref), custom_call_target="tpu_custom_call" | custom-call | tf_op jit(solution)/shard_map/pallas_call | solution.py:692
  55.9 20.0 %all-to-all-done.2.parts_ref = bf16[16,176,128]{2,1,0:T(8,128)(2,1)S(1)} async-done(((bf16[16,176,128]{2,1,0:T(8,128)(2,1)}), bf16[16,176,128]{2,1,0:T(8,128)(2,1)S(1)}, u32[]{:S(2)}, u32[]{:S(2)}) %all-to-all-start.2) | async-done | bytes 720928 | tf_op jit(solution)/shard_map/all_to_all | solution.py:594
  75.9 2.3 %shard_map.184 = (bf16[4,192,128]{2,1,0:T(8,128)(2,1)S(1)}, bf16[176,128]{1,0:T(8,128)(2,1)S(1)}) custom-call(bf16[16,176,128]{2,1,0:T(8,128)(2,1)S(1)} %all-to-all-done.2.parts_ref, bf16[4,5,256,128]{3,2,1,0:T(8,128)(2,1)S(1)} %get-tuple-element.49.shifted_ref, bf16[4,192,128]{2,1,0:T(8,128)(2,1)S(1)} %get-tuple-element.50.mixed_ref, ...), custom_call_target="tpu_custom_call" | custom-call | tf_op jit(solution)/shard_map/pallas_call | solution.py:697
  78.1 1.9 %collective-permute-start.1 = (bf16[176,128]{1,0:T(8,128)(2,1)S(1)}, bf16[176,128]{1,0:T(8,128)(2,1)S(1)}, u32[]{:S(2)}, u32[]{:S(2)}) collective-permute-start(bf16[176,128]{1,0:T(8,128)(2,1)S(1)} %get-tuple-element.53.mine_ref), channel_id=1, source_target_pairs={{0,32},{32,0},{64,96},{96,64},{128,160},{160,128},{192,224},{224,1... | collective-permute-start | bytes 135176 | tf_op jit(solution)/shard_map/ppermute | solution.py:702
  80.1 1.0 shard_map.185.d_image_ref
  81.1 1.8 %collective-permute-done.1.got_ref = bf16[176,128]{1,0:T(8,128)(2,1)S(1)} collective-permute-done((bf16[176,128]{1,0:T(8,128)(2,1)S(1)}, bf16[176,128]{1,0:T(8,128)(2,1)S(1)}, u32[]{:S(2)}, u32[]{:S(2)}) %collective-permute-start.1) | collective-permute-done | bytes 45088 | tf_op jit(solution)/shard_map/ppermute | solution.py:702
  83.0 20.5 %all_to_all.26.parts_ref = bf16[8,176,128]{2,1,0:T(8,128)(2,1)S(1)} all-to-all(bf16[8,176,128]{2,1,0:T(8,128)(2,1)S(1)} %shard_map.186), channel_id=1, replica_groups={{0,64,128,192,256,320,384,448},{32,96,160,224,288,352,416,480},{1,65,12..., dimensions={0} | all-to-all | bytes 720896 | tf_op jit(solution)/shard_map/all_to_all | solution.py:708
  103.4 0.1 shard_map.187
  103.5 29.4 %all_to_all.27.mine_ref = bf16[16,224,128]{2,1,0:T(8,128)(2,1)S(1)} all-to-all(bf16[16,224,128]{2,1,0:T(8,128)(2,1)S(1)} %shard_map.187), channel_id=1, replica_groups={{0,2,4,6,8,10,12,14,16,18,20,22,24,26,28,30},{1,3,5,7,9,11,13,15,17,19,..., dimensions={0} | all-to-all | bytes 1835008 | tf_op jit(solution)/shard_map/all_to_all | solution.py:594
  132.9 4.6 %collective-permute-start.2 = (bf16[16,224,128]{2,1,0:T(8,128)(2,1)S(1)}, bf16[16,224,128]{2,1,0:T(8,128)(2,1)S(1)}, u32[]{:S(2)}, u32[]{:S(2)}) collective-permute-start(bf16[16,224,128]{2,1,0:T(8,128)(2,1)S(1)} %all_to_all.27.mine_ref), channel_id=1, source_target_pairs={{0,1},{1,0},{2,3},{3,2},{4,5},{5,4},{6,7},{7,6},{8,9},{9,8},{10,11... | collective-permute-start | bytes 2752520 | tf_op jit(solution)/shard_map/ppermute | solution.py:598
  137.4 1.3 shard_map.188
  138.7 0.8 collective-permute-done.2.got_ref
  139.5 1.9 %shard_map.189 = (bf16[6,64,256]{2,1,0:T(8,128)(2,1)}, f32[5,51,256]{2,1,0:T(8,128)}, f32[5,51,256]{2,1,0:T(8,128)}, f32[1,256]{1,0:T(1,128)}, f32[1,256]{1,0:T(...) custom-call(s32[1]{0:T(128)} %bitcast.core_ref, ...), custom_call_target="tpu_custom_call", output_to_operand_aliasing={{5}: (4, {}), {7}: (5, {})} | custom-call | tf_op jit(solution)/shard_map/pallas_call | solution.py:720
  (19 shorter events, 0.1 us)
Async XLA Ops:
  0.6 13.2 %copy-start = (bf16[51,5,256]{2,0,1:T(8,128)(2,1)S(1)}, bf16[51,5,256]{2,0,1:T(8,128)(2,1)}, u32[]{:S(2)}) copy-start(bf16[51,5,256]{2,0,1:T(8,128)(2,1)} %param.12) | copy-start | bytes 391684
  0.7 42.5 %copy-start.1 = (bf16[1,6,64,256]{3,2,1,0:T(8,128)(2,1)S(1)}, bf16[1,6,64,256]{3,2,1,0:T(8,128)(2,1)}, u32[]{:S(2)}) copy-start(bf16[1,6,64,256]{3,2,1,0:T(8,128)(2,1)} %param.11) | copy-start | bytes 589828
  0.7 1.0 copy-start.2
  1.6 41.5 %copy-start.3 = (bf16[1,6,64,256]{3,2,1,0:T(8,128)(2,1)S(1)}, bf16[1,6,64,256]{3,2,1,0:T(8,128)(2,1)}, u32[]{:S(2)}) copy-start(bf16[1,6,64,256]{3,2,1,0:T(8,128)(2,1)} %image_ref.1) | copy-start | bytes 589828
  1.6 41.5 %copy-start.4 = (bf16[256,1024]{1,0:T(8,128)(2,1)S(1)}, bf16[256,1024]{1,0:T(8,128)(2,1)}, u32[]{:S(2)}) copy-start(bf16[256,1024]{1,0:T(8,128)(2,1)} %w_in_ref.1) | copy-start | bytes 1572868
  1.6 41.5 %copy-start.5 = (bf16[1024,256]{1,0:T(8,128)(2,1)S(1)}, bf16[1024,256]{1,0:T(8,128)(2,1)}, u32[]{:S(2)}) copy-start(bf16[1024,256]{1,0:T(8,128)(2,1)} %w_out_ref.1) | copy-start | bytes 1572868
  1.7 41.5 %copy-start.6 = (f32[1024]{0:T(1024)S(1)}, f32[1024]{0:T(1024)}, u32[]{:S(2)}) copy-start(f32[1024]{0:T(1024)} %param.17) | copy-start | bytes 12292
  1.7 41.5 %copy-start.7 = (f32[256]{0:T(256)S(1)}, f32[256]{0:T(256)}, u32[]{:S(2)}) copy-start(f32[256]{0:T(256)} %param.14) | copy-start | bytes 3076
  1.7 41.5 %copy-start.8 = (f32[256]{0:T(256)S(1)}, f32[256]{0:T(256)}, u32[]{:S(2)}) copy-start(f32[256]{0:T(256)} %param.15) | copy-start | bytes 3076
  1.7 41.5 %copy-start.9 = (f32[256]{0:T(256)S(1)}, f32[256]{0:T(256)}, u32[]{:S(2)}) copy-start(f32[256]{0:T(256)} %param.19) | copy-start | bytes 3076
  2.5 23.0 %all-to-all-start = ((bf16[32,24,128]{2,1,0:T(8,128)(2,1)}), bf16[32,24,128]{2,1,0:T(8,128)(2,1)S(1)}, u32[]{:S(2)}, u32[]{:S(2)}) async-start(bf16[32,24,128]{2,1,0:T(8,128)(2,1)} %bitcast.1), calls=%async_computation | async-start | bytes 393216 | tf_op jit(solution)/shard_map/all_to_all | solution.py:588
  45.5 3.9 %collective-permute-start = (bf16[2448,128]{1,0:T(8,128)(2,1)S(1)}, bf16[2448,128]{1,0:T(8,128)(2,1)S(1)}, u32[]{:S(2)}, u32[]{:S(2)}) collective-permute-start(bf16[2448,128]{1,0:T(8,128)(2,1)S(1)} %get-tuple-element.47), channel_id=1, source_target_pairs={{0,1},{1,0},{2,3},{3,2},{4,5},{5,4},{6,7},{7,6},{8,9},{9,8},{10,11... | collective-permute-start | bytes 1880072 | tf_op jit(solution)/shard_map/ppermute | solution.py:598
  50.4 25.5 %all-to-all-start.2 = ((bf16[16,176,128]{2,1,0:T(8,128)(2,1)}), bf16[16,176,128]{2,1,0:T(8,128)(2,1)S(1)}, u32[]{:S(2)}, u32[]{:S(2)}) async-start(bf16[16,176,128]{2,1,0:T(8,128)(2,1)} %get-tuple-element.48), calls=%async_computation.2 | async-start | bytes 1441792 | tf_op jit(solution)/shard_map/all_to_all | solution.py:594
  78.1 4.8 %collective-permute-start.1 = (bf16[176,128]{1,0:T(8,128)(2,1)S(1)}, bf16[176,128]{1,0:T(8,128)(2,1)S(1)}, u32[]{:S(2)}, u32[]{:S(2)}) collective-permute-start(bf16[176,128]{1,0:T(8,128)(2,1)S(1)} %get-tuple-element.53.mine_ref), channel_id=1, source_target_pairs={{0,32},{32,0},{64,96},{96,64},{128,160},{160,128},{192,224},{224,1... | collective-permute-start | bytes 135176 | tf_op jit(solution)/shard_map/ppermute | solution.py:702
  132.9 6.7 %collective-permute-start.2 = (bf16[16,224,128]{2,1,0:T(8,128)(2,1)S(1)}, bf16[16,224,128]{2,1,0:T(8,128)(2,1)S(1)}, u32[]{:S(2)}, u32[]{:S(2)}) collective-permute-start(bf16[16,224,128]{2,1,0:T(8,128)(2,1)S(1)} %all_to_all.27.mine_ref), channel_id=1, source_target_pairs={{0,1},{1,0},{2,3},{3,2},{4,5},{5,4},{6,7},{7,6},{8,9},{9,8},{10,11... | collective-permute-start | bytes 2752520 | tf_op jit(solution)/shard_map/ppermute | solution.py:598
